TPU v7x, 128 devices: a whole 4x4x4 slice. The times are simulated.
128 devices in a mesh: dp: 32 (over x, y, core), mp: 2 (over z_lo), tower: 2 (over z_hi).
Axes of the slice: x: 4, y: 4, z: 4 (z_hi: 2, z_lo: 2; z = z_hi * 2 + z_lo), core: 2. Of those that a mesh axis runs over, the one named last changes fastest.
Arguments:
- features: bfloat16 [2, 16384, 1536], P('tower', 'dp'), may hold values from -16 to 16
- projection: bfloat16 [2, 1536, 1536], P('tower', None, 'mp'), may hold values from -1 to 1
- similarity_scale: float32 [1], replicated, may hold values from 8 to 16
- logit_bias: float32 [1], replicated, may hold values from -6 to -2
Outputs:
- row_loss: float32 [2, 16384], P('tower', ('dp', 'mp'))
- projection_grad: float32 [2, 1536, 1536], P('tower', None, 'mp')
All inputs are finite; a program needn't handle non-finite values.
Results may differ from a plain program's by a relative error of at most 0.00049.
Values may be sent and summed in bfloat16 or wider, within the bound.
No kernel may reach another device: no remote copies, remote signals or barrier semaphores. Data moves between devices by JAX's collectives and lax.ppermute only.
A program may use at most 192 MiB of HBM per device.

v0:
```python
import functools

import jax
import jax.numpy as jnp
from jax import lax
from jax.experimental import pallas as pl
from jax.experimental.pallas import tpu as pltpu
from jax.sharding import Mesh, PartitionSpec as P

F32 = jnp.float32
BF16 = jnp.bfloat16
STEPS = (2, 1, 3)
EXTRA = 16


def shifted(value, axis, step):
    count = lax.axis_size(axis)
    return lax.ppermute(value, axis, [(i, (i + step) % count) for i in range(count)])


def crossed(value, tower, half):
    flip = 2 * half + tower
    return lax.ppermute(value, ("m", "t"), [(i, i ^ flip) for i in range(4)])


def pick(block, index, size, axis=0):
    return lax.dynamic_slice_in_dim(block, index * size, size, axis)


def tied(*values):
    return lax.optimization_barrier(values)


def in_hbm(values):
    return [pltpu.with_memory_space_constraint(v, pltpu.HBM) for v in values]


def tile_kernel(row_acc, col_acc, row_types, diagonal, *refs):
    refs = list(refs)
    n_rows, n_pairs = len(row_acc), len(col_acc)

    def take(count):
        return [refs.pop(0) for _ in range(count)]

    diag_ref, scale_ref = take(2)
    rows_refs = take(n_rows)
    cols_refs = [take(2) for _ in range(n_pairs)]
    row_sums = [refs.pop(0) if has else None for has in row_acc]
    col_sums = [take(2) if has else None for has in col_acc]
    ga_refs, gb_refs = take(n_rows), take(2 * n_pairs)
    la_ref, lb_ref, acc_ref, loss_ref = take(4)
    part, width = rows_refs[0].shape
    scale = scale_ref[0]
    bias = scale_ref[1]

    for step in range(n_pairs):
        gb = [jnp.zeros((part, width), F32) for _ in range(2)]
        for r in range(n_rows):
            here = pl.ds(r * part, part)
            images = rows_refs[r][...]
            grad = jnp.zeros((part, width), F32)
            for core in range(2):
                texts = cols_refs[step][core][...]
                logits = (
                    lax.dot_general(
                        images, texts, (((1,), (1,)), ((), ())), preferred_element_type=F32
                    )
                    * scale
                    + bias
                )
                meets = diagonal and step == 0 and r == 0 and core == 0
                if meets:
                    image = lax.broadcasted_iota(jnp.int32, (part, part), 0)
                    text = lax.broadcasted_iota(jnp.int32, (part, part), 1)
                    same = image + diag_ref[0] == text
                    logits = jnp.where(same, -logits, logits)
                grown = jnp.exp(logits)
                whole = 1.0 + grown
                inverse = 1.0 / whole
                losses = jnp.log(whole) + (grown - (whole - 1.0)) * inverse
                share = grown * inverse
                if meets:
                    share = jnp.where(same, -share, share)
                coefficient = share.astype(BF16)
                folded = sum(losses[:, k * 128 : (k + 1) * 128] for k in range(part // 128))
                column = jnp.sum(losses, axis=0, keepdims=True)
                if step == 0 and core == 0:
                    loss_ref[here, :] = folded
                else:
                    loss_ref[here, :] += folded
                if r == 0:
                    lb_ref[2 * step + core] = column
                else:
                    lb_ref[2 * step + core] += column
                grad += jnp.dot(coefficient, texts, preferred_element_type=F32)
                gb[core] += lax.dot_general(
                    coefficient, images, (((0,), (0,)), ((), ())), preferred_element_type=F32
                )
            if step == 0 and row_acc[r]:
                grad += row_sums[r][...]
            if step > 0:
                grad += acc_ref[here, :]
            if step < n_pairs - 1:
                acc_ref[here, :] = grad
            else:
                ga_refs[r][...] = grad.astype(row_types[r])
        for core in range(2):
            total = gb[core]
            if col_acc[step]:
                total += col_sums[step][core][...]
            gb_refs[2 * step + core][...] = total.astype(gb_refs[2 * step + core].dtype)
    for r in range(n_rows):
        la_ref[r] = jnp.sum(loss_ref[pl.ds(r * part, part), :].T, axis=0, keepdims=True)


def tile_terms(rows, cols, row_sums, col_sums, row_types, col_types, diagonal, diag, scales):
    part, width = rows[0].shape
    n_rows, n_pairs = len(rows), len(cols)
    smem = pl.BlockSpec(memory_space=pltpu.SMEM)
    vmem = pl.BlockSpec(memory_space=pltpu.VMEM)
    operands = in_hbm(list(rows) + [v for pair in cols for v in pair])
    operands += [v for v in row_sums if v is not None]
    operands += [v for pair in col_sums if pair is not None for v in pair]
    body = functools.partial(
        tile_kernel,
        [v is not None for v in row_sums],
        [v is not None for v in col_sums],
        row_types,
        diagonal,
    )
    kinds = list(row_types) + [kind for kind in col_types for _ in range(2)]
    out_shape = [
        jax.ShapeDtypeStruct((part, width), F32) if kind == F32 else pltpu.HBM((part, width), kind)
        for kind in kinds
    ]
    n_out = len(out_shape)
    out_shape += [jax.ShapeDtypeStruct((n, 1, part), F32) for n in (n_rows, 2 * n_pairs)]
    out = pl.pallas_call(
        body,
        in_specs=[smem, smem] + [vmem] * len(operands),
        out_specs=[vmem] * len(out_shape),
        out_shape=out_shape,
        scratch_shapes=[
            pltpu.VMEM((n_rows * part if n_pairs > 1 else 8, width), F32),
            pltpu.VMEM((n_rows * part, 128), F32),
        ],
        compiler_params=pltpu.CompilerParams(vmem_limit_bytes=32 * 2**20),
        cost_estimate=pl.CostEstimate(
            flops=6 * n_rows * 2 * n_pairs * part * part * width,
            bytes_accessed=2 * 2 * (n_rows + 2 * n_pairs) * part * width,
            transcendentals=3 * 2 * n_rows * n_pairs * part * part,
        ),
    )(diag, scales, *operands)
    grad_rows, grad_cols = out[:n_rows], out[n_rows:n_out]
    return grad_rows, grad_cols, out[-2].reshape(n_rows, part), out[-1].reshape(n_pairs, 2, part)


def staged(body, smalls, operands, out_shape, cost):
    vmem = pl.BlockSpec(memory_space=pltpu.VMEM)
    return pl.pallas_call(
        body,
        in_specs=[pl.BlockSpec(memory_space=pltpu.SMEM)] * len(smalls) + [vmem] * len(operands),
        out_specs=jax.tree.map(lambda _: vmem, out_shape),
        out_shape=out_shape,
        compiler_params=pltpu.CompilerParams(vmem_limit_bytes=10 * 2**20),
        cost_estimate=pl.CostEstimate(flops=cost, bytes_accessed=2 * cost, transcendentals=0),
    )(*smalls, *in_hbm(operands))


def on_device(features, projection, similarity_scale, logit_bias):
    x, y, c = lax.axis_index("x"), lax.axis_index("y"), lax.axis_index("c")
    m, t = lax.axis_index("m"), lax.axis_index("t")
    inputs = features[0]
    rows, width = inputs.shape
    weight = projection[0]
    half = weight.shape[1]
    part = rows // 2
    pairs = rows * 32
    scale_factor = similarity_scale[0]

    projected = jnp.dot(inputs, weight, preferred_element_type=F32)
    squares = lax.psum(jnp.sum(projected * projected, axis=1), "m")[:, None]
    inverse = lax.rsqrt(squares + 1e-06)
    embedded = (projected * inverse).astype(BF16)
    mine = pick(inputs, c, half, 1)
    others = shifted(pick(inputs, 1 - c, half, 1), "c", 1)

    def rows_for(tower, flip):
        return pick(embedded, jnp.where(t == 0, m ^ flip, 1 ^ tower), part)

    kept = rows_for(0, 0)
    far, near, cross = tied(
        crossed(rows_for(1, 0), 1, 0), crossed(rows_for(0, 1), 0, 1), crossed(rows_for(1, 1), 1, 1)
    )
    own = jnp.concatenate([kept, near], axis=1)
    other = jnp.concatenate([far, cross], axis=1)
    own, other = tied(own, other)

    r1, r3, c1, c3, d0 = tied(
        shifted(own, "y", 1),
        shifted(own, "y", 3),
        shifted(other, "x", 1),
        shifted(other, "x", 3),
        shifted(other, "c", 1),
    )
    c2, r2 = shifted(other, "x", 2), shifted(own, "y", 2)
    d1, d3 = shifted(c1, "c", 1), shifted(c3, "c", 1)
    diag = jnp.where(m == t, 0, 2 * part).astype(jnp.int32).reshape(1)
    scales = jnp.stack([scale_factor, logit_bias[0]])
    near = [own, r1, r3]
    cols0, cols1, cols3 = [other, d0], [c1, d1], [c3, d3]
    rows_sum, (a0, b0, a1, b1, a3, b3), la, lb = tile_terms(
        near,
        [cols0, cols1, cols3],
        [None] * 3,
        [None] * 3,
        [F32] * 3,
        [F32] * 3,
        True,
        diag,
        scales,
    )
    c2, r2, a0, b0, a1, b1, a3, b3, *rows_sum = tied(c2, r2, a0, b0, a1, b1, a3, b3, *rows_sum)
    d2 = shifted(c2, "c", 1)
    (sum2,), (s1, t1, s3, t3), la2, lb2 = tile_terms(
        [r2], [cols1, cols3], [None], [[a1, b1], [a3, b3]], [F32], [BF16] * 2, False, diag, scales
    )
    t1, t3 = shifted(t1, "c", 1), shifted(t3, "c", 1)
    (g2,), (s0, t0, a2, b2), la4, lb4 = tile_terms(
        [r2], [cols0, [c2, d2]], [sum2], [[a0, b0], None], [BF16], [BF16, F32], False, diag, scales
    )
    t1, t3, g2, s0, t0, a2, b2 = tied(t1, t3, g2, s0, t0, a2, b2)

    def joined(a, b):
        return (a.astype(F32) + b.astype(F32)).astype(BF16)

    s1, s3, a2, b2 = tied(joined(s1, t1), joined(s3, t3), a2, b2)
    e1, e3 = shifted(s1, "x", 3), shifted(s3, "x", 1)
    f2 = shifted(g2, "y", 2)
    t0 = shifted(t0, "c", 1)
    (g0, g1, g3), (s2, t2), la3, lb3 = tile_terms(
        near, [[c2, d2]], rows_sum, [[a2, b2]], [BF16] * 3, [BF16], False, diag, scales
    )
    loss_rows = jnp.concatenate([la + la3, la2 + la4])
    loss_cols = jnp.stack([lb[0] + lb4[0], lb[1] + lb2[0], lb[2] + lb2[1], lb4[1] + lb3[0]], axis=1)
    e1, e3, f2, t0, g0, g1, g3, s2, t2 = tied(e1, e3, f2, t0, g0, g1, g3, s2, t2)
    s2 = joined(s2, shifted(t2, "c", 1))
    f1, f3 = shifted(g1, "y", 3), shifted(g3, "y", 1)
    e2 = shifted(s2, "x", 2)
    e2, f1, f3 = tied(e2, f1, f3)
    own0, own1 = packed(own, g0, f1, f2, f3)
    other0, other1 = packed(other, s0, t0, e1, e2, e3)
    far, near, cross = tied(crossed(other0, 1, 0), crossed(own1, 0, 1), crossed(other1, 1, 1))
    flags = jnp.stack([t, m]).astype(jnp.int32)
    scale = (scale_factor / pairs).reshape(1)
    grad_proj = unpacked(flags, scale, [own0, far, near, cross], projected, inverse)

    given = shifted(
        jnp.where(c == 0, jnp.stack([loss_rows, loss_rows]), loss_cols), "c", 1
    )
    losses = jnp.where(c == 0, loss_cols + given[::-1], jnp.stack([given[0], loss_rows]))
    losses, grad_proj = tied(losses, grad_proj)
    lines = losses.transpose(1, 0, 2).reshape(4, 1, rows)
    lines = jnp.pad(lines, ((0, 0), (0, 7), (0, half - rows)))

    grad_swap = shifted(grad_proj, "c", 1)
    weight_part = lax.dot_general(
        mine, grad_proj, (((0,), (0,)), ((), ())), preferred_element_type=F32
    ) + lax.dot_general(others, grad_swap, (((0,), (0,)), ((), ())), preferred_element_type=F32)

    small = half // 4
    lead = jnp.where(c == 0, x, y)
    back = jnp.where(c == 0, y, x)

    def message(k):
        block = pick(weight_part, (lead + k) % 4, small)
        return jnp.concatenate([block, lines[{0: 0, 1: 2, 2: 3, 3: 1}[k]]], axis=0)

    a2, a1, a3 = tied(*(turned(message(k), 0, k) for k in STEPS))
    piece = pick(weight_part, lead, small) + a1[:small] + a2[:small] + a3[:small]
    line = (lines[0] + a1[small:] + a2[small:] + a3[small:])[0, :rows].reshape(2, part)
    a2, a1, a3 = tied(*(turned(piece, 1, k) for k in STEPS))
    piece = (piece + a2) + (a1 + a3)
    given = shifted(jnp.where(c == 0, line[1], line[0]), "c", 1)
    loss_rows, loss_cols, piece = tied(
        jnp.where(c == 0, given, line[1]), jnp.where(c == 0, line[0], given), piece
    )
    pieces = [piece] + [turned(piece, 0, k) for k in (1, 3, 2)]
    loss_far = crossed(loss_cols, 1, 0)
    loss_near = crossed(jnp.where(m == 0, loss_rows, loss_far), 0, 1)
    upper = jnp.logical_and(t == 1, m == 1)
    lower = jnp.logical_and(t == 1, m == 0)
    row_loss = (
        jnp.where(lower, 0.0, loss_rows)
        + jnp.where(upper, 0.0, loss_far)
        + jnp.where(t == 1, loss_near, 0.0)
    ) / pairs
    *pieces, row_loss = tied(*pieces, row_loss)
    swapped = [shifted(v, "c", 1) for v in pieces]
    places = [c * half + (lead - k) % 4 * small for k in (0, 1, 3, 2)]
    places += [(1 - c) * half + (back - k) % 4 * small for k in (0, 1, 3, 2)]
    weight_grad = placed_rows(jnp.stack(places).astype(jnp.int32), pieces + swapped)
    return (row_loss[None], weight_grad[None])


def pack_kernel(embed_ref, *refs):
    refs, out_refs = refs[:-2], refs[-2:]
    part, width = embed_ref.shape
    half = width // 2
    total = jnp.zeros((part, 128), F32)
    for k in range(2):
        here = pl.ds(k * half, half)
        grad = sum(ref[:, here].astype(F32) for ref in refs)
        product = grad * embed_ref[:, here].astype(F32)
        total += sum(product[:, i * 128 : (i + 1) * 128] for i in range(half // 128))
        out_refs[k][:part, :] = grad.astype(BF16)
    line = jnp.sum(total.T, axis=0, keepdims=True)
    parts = []
    for _ in range(3):
        parts.append(line.astype(BF16).astype(F32))
        line = line - parts[-1]
    extra = jnp.broadcast_to(jnp.concatenate(parts, axis=1), (EXTRA, 3 * part)).astype(BF16)
    for k in range(2):
        out_refs[k][part:, :] = extra


def packed(embed, *grads):
    part, width = embed.shape
    out = [pltpu.HBM((part + EXTRA, width // 2), BF16)] * 2
    return staged(pack_kernel, (), (embed,) + grads, out, 6 * part * width)


def unpack_kernel(flags_ref, scale_ref, p00, p10, p01, p11, projected_ref, inverse_ref, out_ref):
    part = p00.shape[0] - EXTRA
    t, m = flags_ref[0], flags_ref[1]
    scale = scale_ref[0]

    def finish(first, second, here):
        grad = first[:part, :].astype(F32) + second[:part, :].astype(F32)
        line = first[part : part + 1, :].astype(F32) + second[part : part + 1, :].astype(F32)
        line = line[:, :part] + line[:, part : 2 * part] + line[:, 2 * part :]
        along = jnp.broadcast_to(line, (128, part)).T[:, :1]
        inverse = inverse_ref[here, :]
        result = inverse * scale * (grad - inverse * along * projected_ref[here, :])
        out_ref[here, :] = result.astype(BF16)

    low, high = pl.ds(0, part), pl.ds(part, part)

    @pl.when(jnp.logical_and(t == 0, m == 0))
    def _():
        finish(p00, p10, low)
        finish(p01, p11, high)

    @pl.when(jnp.logical_and(t == 0, m == 1))
    def _():
        finish(p01, p11, low)
        finish(p00, p10, high)

    @pl.when(t == 1)
    def _():
        finish(p10, p11, low)
        finish(p00, p01, high)


def unpacked(flags, scale, pieces, projected, inverse):
    out = jax.ShapeDtypeStruct(projected.shape, BF16)
    operands = (*pieces, projected, inverse)
    return staged(unpack_kernel, (flags, scale), operands, out, 6 * projected.size)


def turned(value, late, step):
    route = []
    for i in range(32):
        x, y, c = i // 8, i // 2 % 4, i % 2
        if c ^ late:
            y = (y + step) % 4
        else:
            x = (x + step) % 4
        route.append((i, x * 8 + y * 2 + c))
    return lax.ppermute(value, ("x", "y", "c"), route)


def place_kernel(places_ref, *refs):
    *pieces, out_ref, sems = refs
    copies = []
    for i, piece in enumerate(pieces):
        size = piece.shape[0]
        here = pl.ds(pl.multiple_of(places_ref[i], size), size)
        copies.append(pltpu.make_async_copy(piece, out_ref.at[here, :], sems.at[i]))
        copies[-1].start()
    for copy in copies:
        copy.wait()


def placed_rows(places, pieces):
    size, width = pieces[0].shape
    count = len(pieces)
    return pl.pallas_call(
        place_kernel,
        in_specs=[pl.BlockSpec(memory_space=pltpu.SMEM)]
        + [pl.BlockSpec(memory_space=pltpu.VMEM)] * count,
        out_specs=pl.BlockSpec(memory_space=pltpu.HBM),
        out_shape=pltpu.HBM((size * count, width), F32),
        scratch_shapes=[pltpu.SemaphoreType.DMA((count,))],
        compiler_params=pltpu.CompilerParams(vmem_limit_bytes=10 * 2**20),
    )(places, *in_hbm(pieces))


def solution(mesh):
    fine = Mesh(mesh.devices.reshape(4, 4, 2, 2, 2), ("x", "y", "c", "m", "t"))
    dp = ("x", "y", "c")
    placed = (P("t", dp, None), P("t", None, "m"), P(), P())
    return jax.shard_map(
        on_device,
        mesh=fine,
        in_specs=placed,
        out_specs=(P("t", dp + ("m",)), P("t", None, "m")),
        check_vma=False,
    )
```

profile of v0, /device:TPU:1, one launch (start us, length us, event | category | flops | bytes accessed | tf_op | source)
XLA Modules:
  0.0 252.7 jit_solution(2668701412966947983)
XLA Ops:
  2.3 3.9 %multiply_reduce_fusion = (f32[512]{0:T(512)S(1)}, f32[512,768]{1,0:T(8,128)}) fusion(bf16[1,1536,768]{2,1,0:T(8,128)(2,1)S(1)} %copy-done, bf16[1,512,1536]{2,1,0:T(8,128)(2,1)} %param.4), kind=kOutput, calls=%fused_computation.8 | convolution fusion | flops 1208745472 | bytes 5507072 | tf_op jit(solution)/shard_map/dot_general | solution.py:181
  6.2 4.8 %psum.7 = f32[512]{0:T(512)S(1)} all-reduce(f32[512]{0:T(512)S(1)} %get-tuple-element.217), channel_id=1, replica_groups=mesh['x'=4,'y'=4,'c'=2,'m'=2,'t'=2] {'m'}, use_global_device_ids=true, to_apply=%region_1.0 | all-reduce | flops 512 | bytes 4096 | tf_op jit(solution)/shard_map/psum | solution.py:182
  12.7 3.5 %collective-permute-start = (bf16[256,768]{1,0:T(8,128)(2,1)S(1)}, bf16[256,768]{1,0:T(8,128)(2,1)S(1)}, u32[]{:S(2)}, u32[]{:S(2)}) collective-permute-start(bf16[256,768]{1,0:T(8,128)(2,1)S(1)} %get-tuple-element.206), channel_id=1, source_target_pairs={{0,1},{1,0},{2,3},{3,2},{4,5},{5,4},{6,7},{7,6},{8,9},{9,8},{10,11... | collective-permute-start | bytes 1179656 | tf_op jit(solution)/shard_map/ppermute | solution.py:23
  17.0 6.9 %collective-permute-done = bf16[256,768]{1,0:T(8,128)(2,1)S(1)} collective-permute-done((bf16[256,768]{1,0:T(8,128)(2,1)S(1)}, bf16[256,768]{1,0:T(8,128)(2,1)S(1)}, u32[]{:S(2)}, u32[]{:S(2)}) %collective-permute-start) | collective-permute-done | bytes 393248 | tf_op jit(solution)/shard_map/ppermute | solution.py:23
  23.9 8.9 %collective-permute-done.1 = bf16[256,768]{1,0:T(8,128)(2,1)S(1)} collective-permute-done((bf16[256,768]{1,0:T(8,128)(2,1)S(1)}, bf16[256,768]{1,0:T(8,128)(2,1)S(1)}, u32[]{:S(2)}, u32[]{:S(2)}) %collective-permute-start.1) | collective-permute-done | bytes 393248 | tf_op jit(solution)/shard_map/ppermute | solution.py:23
  43.0 11.5 %collective-permute-done.3.refs_3_ = bf16[256,1536]{1,0:T(8,128)(2,1)S(1)} collective-permute-done((bf16[256,1536]{1,0:T(8,128)(2,1)}, bf16[256,1536]{1,0:T(8,128)(2,1)S(1)}, u32[]{:S(2)}, u32[]{:S(2)}) %collective-permute-start.3) | collective-permute-done | bytes 786464 | tf_op jit(solution)/shard_map/ppermute | solution.py:18
  56.5 2.8 %collective-permute-start.8 = (bf16[256,1536]{1,0:T(8,128)(2,1)S(1)}, bf16[256,1536]{1,0:T(8,128)(2,1)}, u32[]{:S(2)}, u32[]{:S(2)}) collective-permute-start(bf16[256,1536]{1,0:T(8,128)(2,1)S(1)} %collective-permute-done.5.refs_7_.refs_3_), channel_id=1, source_target_pairs={{0,4},{4,0},{1,5},{5,1},{2,6},{6,2},{3,7},{7,3},{8,12},{12,8},{9,1... | collective-permute-start | bytes 2359304 | tf_op jit(solution)/shard_map/ppermute | solution.py:18
  65.8 17.3 %shard_map.59 = (f32[256,1536]{1,0:T(8,128)S(1)}, f32[256,1536]{1,0:T(8,128)S(1)}, f32[256,1536]{1,0:T(8,128)S(1)}, f32[256,1536]{1,0:T(8,128)S(1)}, f32[256,153...) custom-call(s32[1]{0:T(128)} %bitcast.refs_0_, ...), custom_call_target="tpu_custom_call" | custom-call | flops 10871635968 | bytes 14155776 | tf_op jit(solution)/shard_map/pallas_call | solution.py:138
  85.8 6.4 %shard_map.60 = (f32[256,1536]{1,0:T(8,128)S(1)}, bf16[256,1536]{1,0:T(8,128)(2,1)}, bf16[256,1536]{1,0:T(8,128)(2,1)}, bf16[256,1536]{1,0:T(8,128)(2,1)}, bf16[...) custom-call(s32[1]{0:T(128)} %bitcast.refs_0_, f32[2]{0:T(128)S(1)} %pad_maximum_fusion.8.refs_1_, ...), custom_call_target="tpu_custom_call" | custom-call | flops 2415919104 | bytes 7864320 | tf_op jit(solution)/shard_map/pallas_call | solution.py:138
  94.1 6.1 %shard_map.61 = (bf16[256,1536]{1,0:T(8,128)(2,1)}, bf16[256,1536]{1,0:T(8,128)(2,1)}, bf16[256,1536]{1,0:T(8,128)(2,1)}, f32[256,1536]{1,0:T(8,128)S(1)}, f32[2...) custom-call(s32[1]{0:T(128)} %bitcast.refs_0_, f32[2]{0:T(128)S(1)} %pad_maximum_fusion.8.refs_1_, ...), custom_call_target="tpu_custom_call" | custom-call | flops 2415919104 | bytes 7864320 | tf_op jit(solution)/shard_map/pallas_call | solution.py:138
  106.4 8.5 %shard_map.62 = (bf16[256,1536]{1,0:T(8,128)(2,1)}, bf16[256,1536]{1,0:T(8,128)(2,1)}, bf16[256,1536]{1,0:T(8,128)(2,1)}, bf16[256,1536]{1,0:T(8,128)(2,1)}, bf1...) custom-call(s32[1]{0:T(128)} %bitcast.refs_0_, f32[2]{0:T(128)S(1)} %pad_maximum_fusion.8.refs_1_, ...), custom_call_target="tpu_custom_call" | custom-call | flops 3623878656 | bytes 7864320 | tf_op jit(solution)/shard_map/pallas_call | solution.py:138
  114.9 5.6 %collective-permute-done.16.refs_2_ = bf16[256,1536]{1,0:T(8,128)(2,1)} collective-permute-done((bf16[256,1536]{1,0:T(8,128)(2,1)S(1)}, bf16[256,1536]{1,0:T(8,128)(2,1)}, u32[]{:S(2)}, u32[]{:S(2)}) %collective-permute-start.16) | collective-permute-done | bytes 786464 | tf_op jit(solution)/shard_map/ppermute | solution.py:18
  130.1 14.9 %collective-permute-done.22.refs_1_ = bf16[256,1536]{1,0:T(8,128)(2,1)S(1)} collective-permute-done((bf16[256,1536]{1,0:T(8,128)(2,1)}, bf16[256,1536]{1,0:T(8,128)(2,1)S(1)}, u32[]{:S(2)}, u32[]{:S(2)}) %collective-permute-start.22) | collective-permute-done | bytes 786464 | tf_op jit(solution)/shard_map/ppermute | solution.py:18
  149.4 4.0 %shard_map.64 = (bf16[272,768]{1,0:T(8,128)(2,1)}, bf16[272,768]{1,0:T(8,128)(2,1)}) custom-call(bf16[256,1536]{1,0:T(8,128)(2,1)} %copy-done.2, bf16[256,1536]{1,0:T(8,128)(2,1)} %get-tuple-element.173.refs_0_, bf16[256,1536]{1,0:T(8,128)(2,1)} %collective-permute-done.19.refs_1_, bf16[256,1536]{1,0:T(8,128)(2,1)} %collective-permute-done.16.refs_2_, ...), custom_call_target="tpu_custom_call" | custom-call | flops 2359296 | bytes 4718592 | tf_op jit(solution)/shard_map/pallas_call | solution.py:160
  153.3 3.0 %collective-permute-start.24 = (bf16[272,768]{1,0:T(8,128)(2,1)}, bf16[272,768]{1,0:T(8,128)(2,1)S(1)}, u32[]{:S(2)}, u32[]{:S(2)}) collective-permute-start(bf16[272,768]{1,0:T(8,128)(2,1)} %get-tuple-element.178), channel_id=1, source_target_pairs={{0,1},{1,0},{2,3},{3,2},{4,5},{5,4},{6,7},{7,6},{8,9},{9,8},{10,11... | collective-permute-start | bytes 1253384 | tf_op jit(solution)/shard_map/ppermute | solution.py:23
  156.7 3.7 %shard_map.63 = (bf16[272,768]{1,0:T(8,128)(2,1)}, bf16[272,768]{1,0:T(8,128)(2,1)}) custom-call(bf16[256,1536]{1,0:T(8,128)(2,1)} %get-tuple-element.104.refs_2_.embed_ref, bf16[256,1536]{1,0:T(8,128)(2,1)} %get-tuple-element.164.refs_0_, bf16[256,1536]{1,0:T(8,128)(2,1)} %copy-done.8, bf16[256,1536]{1,0:T(8,128)(2,1)} %collective-permute-done.18.refs_2_, ...), custom_call_target="tpu_custom_call" | custom-call | flops 2359296 | bytes 4718592 | tf_op jit(solution)/shard_map/pallas_call | solution.py:160
  164.3 11.2 %collective-permute-done.26.p11 = bf16[272,768]{1,0:T(8,128)(2,1)S(1)} collective-permute-done((bf16[272,768]{1,0:T(8,128)(2,1)}, bf16[272,768]{1,0:T(8,128)(2,1)S(1)}, u32[]{:S(2)}, u32[]{:S(2)}) %collective-permute-start.26) | collective-permute-done | bytes 417824 | tf_op jit(solution)/shard_map/ppermute | solution.py:23
  189.5 10.7 %collective-permute-done.31 = f32[200,768]{1,0:T(8,128)} collective-permute-done((f32[200,768]{1,0:T(8,128)S(1)}, f32[200,768]{1,0:T(8,128)}, u32[]{:S(2)}, u32[]{:S(2)}) %collective-permute-start.31) | collective-permute-done | bytes 614432 | tf_op jit(solution)/shard_map/ppermute | solution.py:380
  200.3 4.6 %collective-permute-done.30 = f32[200,768]{1,0:T(8,128)} collective-permute-done((f32[200,768]{1,0:T(8,128)}, f32[200,768]{1,0:T(8,128)}, u32[]{:S(2)}, u32[]{:S(2)}) %collective-permute-start.30) | collective-permute-done | bytes 614432 | tf_op jit(solution)/shard_map/ppermute | solution.py:380
  210.8 2.9 %collective-permute-start.32 = (f32[256]{0:T(256)S(1)}, f32[256]{0:T(256)S(1)}, u32[]{:S(2)}, u32[]{:S(2)}) collective-permute-start(f32[256]{0:T(256)S(1)} %broadcast_select_fusion.3), channel_id=1, source_target_pairs={{0,4},{4,0},{1,5},{5,1},{2,6},{6,2},{3,7},{7,3},{8,12},{12,8},{9,1... | collective-permute-start | bytes 3080 | tf_op jit(solution)/shard_map/ppermute | solution.py:18
  217.1 6.3 %collective-permute-done.34 = f32[192,768]{1,0:T(8,128)S(1)} collective-permute-done((f32[192,768]{1,0:T(8,128)S(1)}, f32[192,768]{1,0:T(8,128)S(1)}, u32[]{:S(2)}, u32[]{:S(2)}) %collective-permute-start.34) | collective-permute-done | bytes 589856 | tf_op jit(solution)/shard_map/ppermute | solution.py:380
  233.5 6.7 %collective-permute-done.36.refs_1_ = f32[192,768]{1,0:T(8,128)S(1)} collective-permute-done((f32[192,768]{1,0:T(8,128)S(1)}, f32[192,768]{1,0:T(8,128)S(1)}, u32[]{:S(2)}, u32[]{:S(2)}) %collective-permute-start.36) | collective-permute-done | bytes 589856 | tf_op jit(solution)/shard_map/ppermute | solution.py:380
  240.2 3.3 %collective-permute-start.41 = (f32[192,768]{1,0:T(8,128)S(1)}, f32[192,768]{1,0:T(8,128)S(1)}, u32[]{:S(2)}, u32[]{:S(2)}) collective-permute-start(f32[192,768]{1,0:T(8,128)S(1)} %add_add_fusion.refs_0_), channel_id=1, source_target_pairs={{0,4},{4,0},{1,5},{5,1},{2,6},{6,2},{3,7},{7,3},{8,12},{12,8},{9,1... | collective-permute-start | bytes 1769480 | tf_op jit(solution)/shard_map/ppermute | solution.py:18
  247.8 4.7 %shard_map.66 = f32[1536,768]{1,0:T(8,128)} custom-call(s32[8]{0:T(128)S(1)} %stack.73.places_ref, f32[192,768]{1,0:T(8,128)} %copy-done.3, f32[192,768]{1,0:T(8,128)} %copy-done.13, f32[192,768]{1,0:T(8,128)} %copy-done.14, f32[192,768]{1,0:T(8,128)} %copy-done.15, f32[192,768]{1,0:T(8,128)} %copy-done.16, f32[192,768]{1,0:T(8,128)} %copy-done.17, ...), custom_call_target="tpu_custom_call" | custom-call | tf_op jit(solution)/shard_map/pallas_call | solution.py:398
  (167 shorter events, 88.0 us)
Async XLA Ops:
  16.2 16.6 %collective-permute-start.1 = (bf16[256,768]{1,0:T(8,128)(2,1)S(1)}, bf16[256,768]{1,0:T(8,128)(2,1)S(1)}, u32[]{:S(2)}, u32[]{:S(2)}) collective-permute-start(bf16[256,768]{1,0:T(8,128)(2,1)S(1)} %get-tuple-element.205), channel_id=1, source_target_pairs={{0,2},{1,3},{2,0},{3,1},{4,6},{5,7},{6,4},{7,5},{8,10},{9,11},{10,... | collective-permute-start | bytes 1179656 | tf_op jit(solution)/shard_map/ppermute | solution.py:23
  17.0 17.3 %collective-permute-start.2 = (bf16[256,768]{1,0:T(8,128)(2,1)S(1)}, bf16[256,768]{1,0:T(8,128)(2,1)S(1)}, u32[]{:S(2)}, u32[]{:S(2)}) collective-permute-start(bf16[256,768]{1,0:T(8,128)(2,1)S(1)} %get-tuple-element.204), channel_id=1, source_target_pairs={{0,3},{1,2},{2,1},{3,0},{4,7},{5,6},{6,5},{7,4},{8,11},{9,10},{10,... | collective-permute-start | bytes 1179656 | tf_op jit(solution)/shard_map/ppermute | solution.py:23
  35.3 19.3 %collective-permute-start.3 = (bf16[256,1536]{1,0:T(8,128)(2,1)}, bf16[256,1536]{1,0:T(8,128)(2,1)S(1)}, u32[]{:S(2)}, u32[]{:S(2)}) collective-permute-start(bf16[256,1536]{1,0:T(8,128)(2,1)} %get-tuple-element.104.refs_2_.embed_ref), channel_id=1, source_target_pairs={{0,8},{8,16},{16,24},{24,0},{1,9},{9,17},{17,25},{25,1},{2,10},{10... | collective-permute-start | bytes 2359304 | tf_op jit(solution)/shard_map/ppermute | solution.py:18
  36.6 18.0 %collective-permute-start.4 = (bf16[256,1536]{1,0:T(8,128)(2,1)}, bf16[256,1536]{1,0:T(8,128)(2,1)S(1)}, u32[]{:S(2)}, u32[]{:S(2)}) collective-permute-start(bf16[256,1536]{1,0:T(8,128)(2,1)} %get-tuple-element.104.refs_2_.embed_ref), channel_id=1, source_target_pairs={{0,24},{8,0},{16,8},{24,16},{1,25},{9,1},{17,9},{25,17},{2,26},{10... | collective-permute-start | bytes 2359304 | tf_op jit(solution)/shard_map/ppermute | solution.py:18
  38.0 18.5 %collective-permute-start.5 = (bf16[256,1536]{1,0:T(8,128)(2,1)S(1)}, bf16[256,1536]{1,0:T(8,128)(2,1)S(1)}, u32[]{:S(2)}, u32[]{:S(2)}) collective-permute-start(bf16[256,1536]{1,0:T(8,128)(2,1)S(1)} %get-tuple-element.105.refs_5_.refs_3_.embed_ref), channel_id=1, source_target_pairs={{0,32},{32,64},{64,96},{96,0},{1,33},{33,65},{65,97},{97,1},{2,34}... | collective-permute-start | bytes 2359304 | tf_op jit(solution)/shard_map/ppermute | solution.py:18
  39.2 17.3 %collective-permute-start.6 = (bf16[256,1536]{1,0:T(8,128)(2,1)S(1)}, bf16[256,1536]{1,0:T(8,128)(2,1)S(1)}, u32[]{:S(2)}, u32[]{:S(2)}) collective-permute-start(bf16[256,1536]{1,0:T(8,128)(2,1)S(1)} %get-tuple-element.105.refs_5_.refs_3_.embed_ref), channel_id=1, source_target_pairs={{0,96},{32,0},{64,32},{96,64},{1,97},{33,1},{65,33},{97,65},{2,98}... | collective-permute-start | bytes 2359304 | tf_op jit(solution)/shard_map/ppermute | solution.py:18
  40.7 15.8 %collective-permute-start.7 = (bf16[256,1536]{1,0:T(8,128)(2,1)S(1)}, bf16[256,1536]{1,0:T(8,128)(2,1)S(1)}, u32[]{:S(2)}, u32[]{:S(2)}) collective-permute-start(bf16[256,1536]{1,0:T(8,128)(2,1)S(1)} %get-tuple-element.105.refs_5_.refs_3_.embed_ref), channel_id=1, source_target_pairs={{0,4},{4,0},{1,5},{5,1},{2,6},{6,2},{3,7},{7,3},{8,12},{12,8},{9,1... | collective-permute-start | bytes 2359304 | tf_op jit(solution)/shard_map/ppermute | solution.py:18
  61.5 21.6 %collective-permute-start.10 = (bf16[256,1536]{1,0:T(8,128)(2,1)S(1)}, bf16[256,1536]{1,0:T(8,128)(2,1)S(1)}, u32[]{:S(2)}, u32[]{:S(2)}) collective-permute-start(bf16[256,1536]{1,0:T(8,128)(2,1)S(1)} %get-tuple-element.105.refs_5_.refs_3_.embed_ref), channel_id=1, source_target_pairs={{0,64},{32,96},{64,0},{96,32},{1,65},{33,97},{65,1},{97,33},{2,66}... | collective-permute-start | bytes 2359304 | tf_op jit(solution)/shard_map/ppermute | solution.py:18
  64.0 20.7 %collective-permute-start.11 = (bf16[256,1536]{1,0:T(8,128)(2,1)}, bf16[256,1536]{1,0:T(8,128)(2,1)S(1)}, u32[]{:S(2)}, u32[]{:S(2)}) collective-permute-start(bf16[256,1536]{1,0:T(8,128)(2,1)} %get-tuple-element.104.refs_2_.embed_ref), channel_id=1, source_target_pairs={{0,16},{8,24},{16,0},{24,8},{1,17},{9,25},{17,1},{25,9},{2,18},{10... | collective-permute-start | bytes 2359304 | tf_op jit(solution)/shard_map/ppermute | solution.py:18
  101.6 18.9 %collective-permute-start.16 = (bf16[256,1536]{1,0:T(8,128)(2,1)S(1)}, bf16[256,1536]{1,0:T(8,128)(2,1)}, u32[]{:S(2)}, u32[]{:S(2)}) collective-permute-start(bf16[256,1536]{1,0:T(8,128)(2,1)S(1)} %add_convert_fusion.2), channel_id=1, source_target_pairs={{0,96},{32,0},{64,32},{96,64},{1,97},{33,1},{65,33},{97,65},{2,98}... | collective-permute-start | bytes 2359304 | tf_op jit(solution)/shard_map/ppermute | solution.py:18
  102.8 19.7 %collective-permute-start.17 = (bf16[256,1536]{1,0:T(8,128)(2,1)S(1)}, bf16[256,1536]{1,0:T(8,128)(2,1)}, u32[]{:S(2)}, u32[]{:S(2)}) collective-permute-start(bf16[256,1536]{1,0:T(8,128)(2,1)S(1)} %add_convert_fusion.1), channel_id=1, source_target_pairs={{0,32},{32,64},{64,96},{96,0},{1,33},{33,65},{65,97},{97,1},{2,34}... | collective-permute-start | bytes 2359304 | tf_op jit(solution)/shard_map/ppermute | solution.py:18
  103.1 19.7 %collective-permute-start.18 = (bf16[256,1536]{1,0:T(8,128)(2,1)S(1)}, bf16[256,1536]{1,0:T(8,128)(2,1)}, u32[]{:S(2)}, u32[]{:S(2)}) collective-permute-start(bf16[256,1536]{1,0:T(8,128)(2,1)S(1)} %copy-done.26), channel_id=1, source_target_pairs={{0,16},{8,24},{16,0},{24,8},{1,17},{9,25},{17,1},{25,9},{2,18},{10... | collective-permute-start | bytes 2359304 | tf_op jit(solution)/shard_map/ppermute | solution.py:18
  104.7 18.0 %collective-permute-start.19 = (bf16[256,1536]{1,0:T(8,128)(2,1)S(1)}, bf16[256,1536]{1,0:T(8,128)(2,1)}, u32[]{:S(2)}, u32[]{:S(2)}) collective-permute-start(bf16[256,1536]{1,0:T(8,128)(2,1)S(1)} %copy-done.25), channel_id=1, source_target_pairs={{0,4},{4,0},{1,5},{5,1},{2,6},{6,2},{3,7},{7,3},{8,12},{12,8},{9,1... | collective-permute-start | bytes 2359304 | tf_op jit(solution)/shard_map/ppermute | solution.py:18
  125.9 55.8 %collective-permute-start.27 = (bf16[512,768]{1,0:T(8,128)(2,1)S(1)}, bf16[512,768]{1,0:T(8,128)(2,1)S(1)}, u32[]{:S(2)}, u32[]{:S(2)}) collective-permute-start(bf16[512,768]{1,0:T(8,128)(2,1)S(1)} %dynamic-slice_bitcast_fusion), channel_id=1, source_target_pairs={{0,4},{4,0},{1,5},{5,1},{2,6},{6,2},{3,7},{7,3},{8,12},{12,8},{9,1... | collective-permute-start | bytes 2359304 | tf_op jit(solution)/shard_map/ppermute | solution.py:18
  126.0 19.0 %collective-permute-start.22 = (bf16[256,1536]{1,0:T(8,128)(2,1)}, bf16[256,1536]{1,0:T(8,128)(2,1)S(1)}, u32[]{:S(2)}, u32[]{:S(2)}) collective-permute-start(bf16[256,1536]{1,0:T(8,128)(2,1)} %get-tuple-element.167), channel_id=1, source_target_pairs={{0,24},{8,0},{16,8},{24,16},{1,25},{9,1},{17,9},{25,17},{2,26},{10... | collective-permute-start | bytes 2359304 | tf_op jit(solution)/shard_map/ppermute | solution.py:18
  127.5 19.8 %collective-permute-start.23 = (bf16[256,1536]{1,0:T(8,128)(2,1)}, bf16[256,1536]{1,0:T(8,128)(2,1)S(1)}, u32[]{:S(2)}, u32[]{:S(2)}) collective-permute-start(bf16[256,1536]{1,0:T(8,128)(2,1)} %get-tuple-element.168), channel_id=1, source_target_pairs={{0,8},{8,16},{16,24},{24,0},{1,9},{9,17},{17,25},{25,1},{2,10},{10... | collective-permute-start | bytes 2359304 | tf_op jit(solution)/shard_map/ppermute | solution.py:18
  128.8 19.6 %collective-permute-start.21 = (bf16[256,1536]{1,0:T(8,128)(2,1)S(1)}, bf16[256,1536]{1,0:T(8,128)(2,1)S(1)}, u32[]{:S(2)}, u32[]{:S(2)}) collective-permute-start(bf16[256,1536]{1,0:T(8,128)(2,1)S(1)} %add_convert_fusion), channel_id=1, source_target_pairs={{0,64},{32,96},{64,0},{96,32},{1,65},{33,97},{65,1},{97,33},{2,66}... | collective-permute-start | bytes 2359304 | tf_op jit(solution)/shard_map/ppermute | solution.py:18
  156.3 19.3 %collective-permute-start.26 = (bf16[272,768]{1,0:T(8,128)(2,1)}, bf16[272,768]{1,0:T(8,128)(2,1)S(1)}, u32[]{:S(2)}, u32[]{:S(2)}) collective-permute-start(bf16[272,768]{1,0:T(8,128)(2,1)} %get-tuple-element.180), channel_id=1, source_target_pairs={{0,3},{1,2},{2,1},{3,0},{4,7},{5,6},{6,5},{7,4},{8,11},{9,10},{10,... | collective-permute-start | bytes 1253384 | tf_op jit(solution)/shard_map/ppermute | solution.py:23
  183.9 16.4 %collective-permute-start.31 = (f32[200,768]{1,0:T(8,128)S(1)}, f32[200,768]{1,0:T(8,128)}, u32[]{:S(2)}, u32[]{:S(2)}) collective-permute-start(f32[200,768]{1,0:T(8,128)S(1)} %pad_maximum_fusion.4), channel_id=1, source_target_pairs={{0,96},{4,28},{8,104},{12,4},{16,112},{20,12},{24,120},{28,20},{32... | collective-permute-start | bytes 1843208 | tf_op jit(solution)/shard_map/ppermute | solution.py:380
  187.5 17.4 %collective-permute-start.30 = (f32[200,768]{1,0:T(8,128)}, f32[200,768]{1,0:T(8,128)}, u32[]{:S(2)}, u32[]{:S(2)}) collective-permute-start(f32[200,768]{1,0:T(8,128)} %pad_maximum_fusion.3), channel_id=1, source_target_pairs={{0,32},{4,12},{8,40},{12,20},{16,48},{20,28},{24,56},{28,4},{32,64... | collective-permute-start | bytes 1843208 | tf_op jit(solution)/shard_map/ppermute | solution.py:380
  188.3 16.5 %collective-permute-start.29 = (f32[200,768]{1,0:T(8,128)}, f32[200,768]{1,0:T(8,128)}, u32[]{:S(2)}, u32[]{:S(2)}) collective-permute-start(f32[200,768]{1,0:T(8,128)} %pad_maximum_fusion.2), channel_id=1, source_target_pairs={{0,64},{4,20},{8,72},{12,28},{16,80},{20,4},{24,88},{28,12},{32,96... | collective-permute-start | bytes 1843208 | tf_op jit(solution)/shard_map/ppermute | solution.py:380
  207.3 16.0 %collective-permute-start.34 = (f32[192,768]{1,0:T(8,128)S(1)}, f32[192,768]{1,0:T(8,128)S(1)}, u32[]{:S(2)}, u32[]{:S(2)}) collective-permute-start(f32[192,768]{1,0:T(8,128)S(1)} %slice_add_fusion), channel_id=1, source_target_pairs={{0,8},{4,36},{8,16},{12,44},{16,24},{20,52},{24,0},{28,60},{32,40}... | collective-permute-start | bytes 1769480 | tf_op jit(solution)/shard_map/ppermute | solution.py:380
  223.5 16.6 %collective-permute-start.36 = (f32[192,768]{1,0:T(8,128)S(1)}, f32[192,768]{1,0:T(8,128)S(1)}, u32[]{:S(2)}, u32[]{:S(2)}) collective-permute-start(f32[192,768]{1,0:T(8,128)S(1)} %add_add_fusion.refs_0_), channel_id=1, source_target_pairs={{0,32},{4,12},{8,40},{12,20},{16,48},{20,28},{24,56},{28,4},{32,64... | collective-permute-start | bytes 1769480 | tf_op jit(solution)/shard_map/ppermute | solution.py:380
  223.6 16.6 %collective-permute-start.37 = (f32[192,768]{1,0:T(8,128)S(1)}, f32[192,768]{1,0:T(8,128)S(1)}, u32[]{:S(2)}, u32[]{:S(2)}) collective-permute-start(f32[192,768]{1,0:T(8,128)S(1)} %add_add_fusion.refs_0_), channel_id=1, source_target_pairs={{0,96},{4,28},{8,104},{12,4},{16,112},{20,12},{24,120},{28,20},{32... | collective-permute-start | bytes 1769480 | tf_op jit(solution)/shard_map/ppermute | solution.py:380
  (48 other events, 338.2 us)
where the time goes:
time: 258 us; the launch traced here: 253 us
  waiting for transfers between devices  107 us (41%)
  starting transfers between devices  59.3 us (23%)
  Pallas kernels  53.1 us (21%)
  other arithmetic  9.36 us (4%)
  local copies, waits for them, and re-layouts  8.3 us (3%)
  matrix products  7.84 us (3%)
  blocking collectives  4.76 us (2%)
    ppermute x28, waiting for transfers between devices, shifted(): lax.ppermute(value, axis, [(i, (i + step) % count) for i in range(count)])  45.1 us
    pallas_call x4, Pallas kernels, tile_terms(): pl.pallas_call(body, in_specs=[smem, smem] + [vmem] * len(operands), out_...  38.3 us
    ppermute x28, starting transfers between devices, shifted(): lax.ppermute(value, axis, [(i, (i + step) % count) for i in range(count)])  37.5 us
    ppermute x8, waiting for transfers between devices, crossed(): return lax.ppermute(value, ('m', 't'), [(i, i ^ flip) for i in range(4)])  31.6 us
    ppermute x9, waiting for transfers between devices, turned(): return lax.ppermute(value, ('x', 'y', 'c'), route)  30.8 us
    ppermute x8, starting transfers between devices, crossed(): return lax.ppermute(value, ('m', 't'), [(i, i ^ flip) for i in range(4)])  11.6 us
    ppermute x9, starting transfers between devices, turned(): return lax.ppermute(value, ('x', 'y', 'c'), route)  10.3 us
    pallas_call x3, Pallas kernels, staged(): pl.pallas_call(body, in_specs=[pl.BlockSpec(memory_space=pltpu.SMEM)] * l...  10.1 us
  transfers between devices with their start and end apart: 45, of which 26 were waited for; matrix products, arithmetic and copies ran while one was open for 3% of the time, Pallas kernels for 19%

commit v1 on v0

--- a/solution.py
+++ b/solution.py
@@ -1,4 +1,5 @@
 import functools
+import math
 
 import jax
 import jax.numpy as jnp
@@ -53,49 +54,55 @@
     scale = scale_ref[0]
     bias = scale_ref[1]
 
-    for step in range(n_pairs):
-        gb = [jnp.zeros((part, width), F32) for _ in range(2)]
-        for r in range(n_rows):
-            here = pl.ds(r * part, part)
-            images = rows_refs[r][...]
+    def products(step, r, core):
+        return lax.dot_general(
+            rows_refs[r][...],
+            cols_refs[step][core][...],
+            (((1,), (1,)), ((), ())),
+            preferred_element_type=F32,
+        )
+
+    order = [(k, r, core) for k in range(n_pairs) for r in range(n_rows) for core in range(2)]
+    coming = products(*order[0])
+    for i, (step, r, core) in enumerate(order):
+        logits = coming * scale + bias
+        if i + 1 < len(order):
+            coming = products(*order[i + 1])
+        here = pl.ds(r * part, part)
+        if r == 0 and core == 0:
+            gb = [jnp.zeros((part, width), F32) for _ in range(2)]
+        if core == 0:
             grad = jnp.zeros((part, width), F32)
-            for core in range(2):
-                texts = cols_refs[step][core][...]
-                logits = (
-                    lax.dot_general(
-                        images, texts, (((1,), (1,)), ((), ())), preferred_element_type=F32
-                    )
-                    * scale
-                    + bias
-                )
-                meets = diagonal and step == 0 and r == 0 and core == 0
-                if meets:
-                    image = lax.broadcasted_iota(jnp.int32, (part, part), 0)
-                    text = lax.broadcasted_iota(jnp.int32, (part, part), 1)
-                    same = image + diag_ref[0] == text
-                    logits = jnp.where(same, -logits, logits)
-                grown = jnp.exp(logits)
-                whole = 1.0 + grown
-                inverse = 1.0 / whole
-                losses = jnp.log(whole) + (grown - (whole - 1.0)) * inverse
-                share = grown * inverse
-                if meets:
-                    share = jnp.where(same, -share, share)
-                coefficient = share.astype(BF16)
-                folded = sum(losses[:, k * 128 : (k + 1) * 128] for k in range(part // 128))
-                column = jnp.sum(losses, axis=0, keepdims=True)
-                if step == 0 and core == 0:
-                    loss_ref[here, :] = folded
-                else:
-                    loss_ref[here, :] += folded
-                if r == 0:
-                    lb_ref[2 * step + core] = column
-                else:
-                    lb_ref[2 * step + core] += column
-                grad += jnp.dot(coefficient, texts, preferred_element_type=F32)
-                gb[core] += lax.dot_general(
-                    coefficient, images, (((0,), (0,)), ((), ())), preferred_element_type=F32
-                )
+        meets = diagonal and i == 0
+        if meets:
+            image = lax.broadcasted_iota(jnp.int32, (part, part), 0)
+            text = lax.broadcasted_iota(jnp.int32, (part, part), 1)
+            same = image + diag_ref[0] == text
+            logits = jnp.where(same, -logits, logits)
+        grown = jnp.exp2(logits)
+        whole = 1.0 + grown
+        inverse = pl.reciprocal(whole, approx=True)
+        inverse = inverse * (2.0 - whole * inverse)
+        losses = jnp.log(whole) + (grown - (whole - 1.0)) * inverse
+        share = grown * inverse
+        if meets:
+            share = jnp.where(same, -share, share)
+        coefficient = share.astype(BF16)
+        folded = sum(losses[:, k * 128 : (k + 1) * 128] for k in range(part // 128))
+        column = jnp.sum(losses, axis=0, keepdims=True)
+        if step == 0 and core == 0:
+            loss_ref[here, :] = folded
+        else:
+            loss_ref[here, :] += folded
+        if r == 0:
+            lb_ref[2 * step + core] = column
+        else:
+            lb_ref[2 * step + core] += column
+        grad += jnp.dot(coefficient, cols_refs[step][core][...], preferred_element_type=F32)
+        gb[core] += lax.dot_general(
+            coefficient, rows_refs[r][...], (((0,), (0,)), ((), ())), preferred_element_type=F32
+        )
+        if core == 1:
             if step == 0 and row_acc[r]:
                 grad += row_sums[r][...]
             if step > 0:
@@ -104,7 +111,7 @@
                 acc_ref[here, :] = grad
             else:
                 ga_refs[r][...] = grad.astype(row_types[r])
-        for core in range(2):
+        if r == n_rows - 1:
             total = gb[core]
             if col_acc[step]:
                 total += col_sums[step][core][...]
@@ -206,7 +213,7 @@
     c2, r2 = shifted(other, "x", 2), shifted(own, "y", 2)
     d1, d3 = shifted(c1, "c", 1), shifted(c3, "c", 1)
     diag = jnp.where(m == t, 0, 2 * part).astype(jnp.int32).reshape(1)
-    scales = jnp.stack([scale_factor, logit_bias[0]])
+    scales = jnp.stack([scale_factor, logit_bias[0]]) * math.log2(math.e)
     near = [own, r1, r3]
     cols0, cols1, cols3 = [other, d0], [c1, d1], [c3, d3]
     rows_sum, (a0, b0, a1, b1, a3, b3), la, lb = tile_terms(

time: 258 us -> 257 us (level)
  waiting for transfers between devices: 107 us -> 111 us
  Pallas kernels: 53.1 us -> 49.8 us
    pallas_call x4, Pallas kernels: 38.3 us -> 35 us  [tile_terms(): pl.pallas_call(body, in_specs=[smem, smem] + [vmem] * len(operands), out_...]
    ppermute x28, waiting for transfers between devices: 45.1 us -> 48.1 us  [shifted(): lax.ppermute(value, axis, [(i, (i + step) % count) for i in range(count)])]
  transfers between devices with their start and end apart: 45 -> 45, of which waited for: 26 -> 27; matrix products, arithmetic and copies ran while one was open for 3% -> 3% of each run, Pallas kernels for 19% -> 18%
where the time goes in v1:
time: 257 us; the launch traced here: 252 us
  waiting for transfers between devices  111 us (43%)
  starting transfers between devices  59.3 us (23%)
  Pallas kernels  49.8 us (19%)
  other arithmetic  9.36 us (4%)
  local copies, waits for them, and re-layouts  8.3 us (3%)
  matrix products  7.84 us (3%)
  blocking collectives  4.76 us (2%)
    ppermute x28, waiting for transfers between devices, shifted(): lax.ppermute(value, axis, [(i, (i + step) % count) for i in range(count)])  48.1 us
    ppermute x28, starting transfers between devices, shifted(): lax.ppermute(value, axis, [(i, (i + step) % count) for i in range(count)])  37.5 us
    pallas_call x4, Pallas kernels, tile_terms(): pl.pallas_call(body, in_specs=[smem, smem] + [vmem] * len(operands), out_...  35 us
    ppermute x8, waiting for transfers between devices, crossed(): return lax.ppermute(value, ('m', 't'), [(i, i ^ flip) for i in range(4)])  31.6 us
    ppermute x9, waiting for transfers between devices, turned(): return lax.ppermute(value, ('x', 'y', 'c'), route)  30.8 us
    ppermute x8, starting transfers between devices, crossed(): return lax.ppermute(value, ('m', 't'), [(i, i ^ flip) for i in range(4)])  11.6 us
    ppermute x9, starting transfers between devices, turned(): return lax.ppermute(value, ('x', 'y', 'c'), route)  10.3 us
    pallas_call x3, Pallas kernels, staged(): pl.pallas_call(body, in_specs=[pl.BlockSpec(memory_space=pltpu.SMEM)] * l...  10.1 us
  transfers between devices with their start and end apart: 45, of which 27 were waited for; matrix products, arithmetic and copies ran while one was open for 3% of the time, Pallas kernels for 18%

profile of v1, /device:TPU:1, one launch (start us, length us, event | category | flops | bytes accessed | tf_op | source)
XLA Modules:
  0.0 252.4 jit_solution(17537914840415707883)
XLA Ops:
  2.3 3.9 %multiply_reduce_fusion = (f32[512]{0:T(512)S(1)}, f32[512,768]{1,0:T(8,128)}) fusion(bf16[1,1536,768]{2,1,0:T(8,128)(2,1)S(1)} %copy-done, bf16[1,512,1536]{2,1,0:T(8,128)(2,1)} %param.4), kind=kOutput, calls=%fused_computation.8 | convolution fusion | flops 1208745472 | bytes 5507072 | tf_op jit(solution)/shard_map/dot_general | solution.py:188
  6.2 4.8 %psum.7 = f32[512]{0:T(512)S(1)} all-reduce(f32[512]{0:T(512)S(1)} %get-tuple-element.217), channel_id=1, replica_groups=mesh['x'=4,'y'=4,'c'=2,'m'=2,'t'=2] {'m'}, use_global_device_ids=true, to_apply=%region_1.0 | all-reduce | flops 512 | bytes 4096 | tf_op jit(solution)/shard_map/psum | solution.py:189
  12.7 3.5 %collective-permute-start = (bf16[256,768]{1,0:T(8,128)(2,1)S(1)}, bf16[256,768]{1,0:T(8,128)(2,1)S(1)}, u32[]{:S(2)}, u32[]{:S(2)}) collective-permute-start(bf16[256,768]{1,0:T(8,128)(2,1)S(1)} %get-tuple-element.206), channel_id=1, source_target_pairs={{0,1},{1,0},{2,3},{3,2},{4,5},{5,4},{6,7},{7,6},{8,9},{9,8},{10,11... | collective-permute-start | bytes 1179656 | tf_op jit(solution)/shard_map/ppermute | solution.py:24
  17.0 6.9 %collective-permute-done = bf16[256,768]{1,0:T(8,128)(2,1)S(1)} collective-permute-done((bf16[256,768]{1,0:T(8,128)(2,1)S(1)}, bf16[256,768]{1,0:T(8,128)(2,1)S(1)}, u32[]{:S(2)}, u32[]{:S(2)}) %collective-permute-start) | collective-permute-done | bytes 393248 | tf_op jit(solution)/shard_map/ppermute | solution.py:24
  23.9 8.9 %collective-permute-done.1 = bf16[256,768]{1,0:T(8,128)(2,1)S(1)} collective-permute-done((bf16[256,768]{1,0:T(8,128)(2,1)S(1)}, bf16[256,768]{1,0:T(8,128)(2,1)S(1)}, u32[]{:S(2)}, u32[]{:S(2)}) %collective-permute-start.1) | collective-permute-done | bytes 393248 | tf_op jit(solution)/shard_map/ppermute | solution.py:24
  43.0 11.5 %collective-permute-done.3.refs_3_ = bf16[256,1536]{1,0:T(8,128)(2,1)S(1)} collective-permute-done((bf16[256,1536]{1,0:T(8,128)(2,1)}, bf16[256,1536]{1,0:T(8,128)(2,1)S(1)}, u32[]{:S(2)}, u32[]{:S(2)}) %collective-permute-start.3) | collective-permute-done | bytes 786464 | tf_op jit(solution)/shard_map/ppermute | solution.py:19
  56.5 2.8 %collective-permute-start.8 = (bf16[256,1536]{1,0:T(8,128)(2,1)S(1)}, bf16[256,1536]{1,0:T(8,128)(2,1)}, u32[]{:S(2)}, u32[]{:S(2)}) collective-permute-start(bf16[256,1536]{1,0:T(8,128)(2,1)S(1)} %collective-permute-done.5.refs_7_.refs_3_), channel_id=1, source_target_pairs={{0,4},{4,0},{1,5},{5,1},{2,6},{6,2},{3,7},{7,3},{8,12},{12,8},{9,1... | collective-permute-start | bytes 2359304 | tf_op jit(solution)/shard_map/ppermute | solution.py:19
  65.8 15.2 %shard_map.59 = (f32[256,1536]{1,0:T(8,128)S(1)}, f32[256,1536]{1,0:T(8,128)S(1)}, f32[256,1536]{1,0:T(8,128)S(1)}, f32[256,1536]{1,0:T(8,128)S(1)}, f32[256,153...) custom-call(s32[1]{0:T(128)} %bitcast.refs_0_, ...), custom_call_target="tpu_custom_call" | custom-call | flops 10871635968 | bytes 14155776 | tf_op jit(solution)/shard_map/pallas_call | solution.py:145
  86.0 5.9 %shard_map.60 = (f32[256,1536]{1,0:T(8,128)S(1)}, bf16[256,1536]{1,0:T(8,128)(2,1)}, bf16[256,1536]{1,0:T(8,128)(2,1)}, bf16[256,1536]{1,0:T(8,128)(2,1)}, bf16[...) custom-call(s32[1]{0:T(128)} %bitcast.refs_0_, f32[2]{0:T(128)S(1)} %maximum_multiply_fusion.refs_1_, ...), custom_call_target="tpu_custom_call" | custom-call | flops 2415919104 | bytes 7864320 | tf_op jit(solution)/shard_map/pallas_call | solution.py:145
  93.6 6.3 %shard_map.61 = (bf16[256,1536]{1,0:T(8,128)(2,1)}, bf16[256,1536]{1,0:T(8,128)(2,1)}, bf16[256,1536]{1,0:T(8,128)(2,1)}, f32[256,1536]{1,0:T(8,128)S(1)}, f32[2...) custom-call(s32[1]{0:T(128)} %bitcast.refs_0_, f32[2]{0:T(128)S(1)} %maximum_multiply_fusion.refs_1_, ...), custom_call_target="tpu_custom_call" | custom-call | flops 2415919104 | bytes 7864320 | tf_op jit(solution)/shard_map/pallas_call | solution.py:145
  106.0 7.6 %shard_map.62 = (bf16[256,1536]{1,0:T(8,128)(2,1)}, bf16[256,1536]{1,0:T(8,128)(2,1)}, bf16[256,1536]{1,0:T(8,128)(2,1)}, bf16[256,1536]{1,0:T(8,128)(2,1)}, bf1...) custom-call(s32[1]{0:T(128)} %bitcast.refs_0_, f32[2]{0:T(128)S(1)} %maximum_multiply_fusion.refs_1_, ...), custom_call_target="tpu_custom_call" | custom-call | flops 3623878656 | bytes 7864320 | tf_op jit(solution)/shard_map/pallas_call | solution.py:145
  113.6 6.5 %collective-permute-done.16.refs_2_ = bf16[256,1536]{1,0:T(8,128)(2,1)} collective-permute-done((bf16[256,1536]{1,0:T(8,128)(2,1)S(1)}, bf16[256,1536]{1,0:T(8,128)(2,1)}, u32[]{:S(2)}, u32[]{:S(2)}) %collective-permute-start.16) | collective-permute-done | bytes 786464 | tf_op jit(solution)/shard_map/ppermute | solution.py:19
  129.7 14.9 %collective-permute-done.22.refs_1_ = bf16[256,1536]{1,0:T(8,128)(2,1)S(1)} collective-permute-done((bf16[256,1536]{1,0:T(8,128)(2,1)}, bf16[256,1536]{1,0:T(8,128)(2,1)S(1)}, u32[]{:S(2)}, u32[]{:S(2)}) %collective-permute-start.22) | collective-permute-done | bytes 786464 | tf_op jit(solution)/shard_map/ppermute | solution.py:19
  149.0 4.0 %shard_map.64 = (bf16[272,768]{1,0:T(8,128)(2,1)}, bf16[272,768]{1,0:T(8,128)(2,1)}) custom-call(bf16[256,1536]{1,0:T(8,128)(2,1)} %copy-done.2, bf16[256,1536]{1,0:T(8,128)(2,1)} %get-tuple-element.173.refs_0_, bf16[256,1536]{1,0:T(8,128)(2,1)} %collective-permute-done.19.refs_1_, bf16[256,1536]{1,0:T(8,128)(2,1)} %collective-permute-done.16.refs_2_, ...), custom_call_target="tpu_custom_call" | custom-call | flops 2359296 | bytes 4718592 | tf_op jit(solution)/shard_map/pallas_call | solution.py:167
  153.0 3.0 %collective-permute-start.24 = (bf16[272,768]{1,0:T(8,128)(2,1)}, bf16[272,768]{1,0:T(8,128)(2,1)S(1)}, u32[]{:S(2)}, u32[]{:S(2)}) collective-permute-start(bf16[272,768]{1,0:T(8,128)(2,1)} %get-tuple-element.178), channel_id=1, source_target_pairs={{0,1},{1,0},{2,3},{3,2},{4,5},{5,4},{6,7},{7,6},{8,9},{9,8},{10,11... | collective-permute-start | bytes 1253384 | tf_op jit(solution)/shard_map/ppermute | solution.py:24
  156.4 3.7 %shard_map.63 = (bf16[272,768]{1,0:T(8,128)(2,1)}, bf16[272,768]{1,0:T(8,128)(2,1)}) custom-call(bf16[256,1536]{1,0:T(8,128)(2,1)} %get-tuple-element.104.refs_2_.embed_ref, bf16[256,1536]{1,0:T(8,128)(2,1)} %get-tuple-element.164.refs_0_, bf16[256,1536]{1,0:T(8,128)(2,1)} %copy-done.8, bf16[256,1536]{1,0:T(8,128)(2,1)} %collective-permute-done.18.refs_2_, ...), custom_call_target="tpu_custom_call" | custom-call | flops 2359296 | bytes 4718592 | tf_op jit(solution)/shard_map/pallas_call | solution.py:167
  164.0 11.2 %collective-permute-done.26.p11 = bf16[272,768]{1,0:T(8,128)(2,1)S(1)} collective-permute-done((bf16[272,768]{1,0:T(8,128)(2,1)}, bf16[272,768]{1,0:T(8,128)(2,1)S(1)}, u32[]{:S(2)}, u32[]{:S(2)}) %collective-permute-start.26) | collective-permute-done | bytes 417824 | tf_op jit(solution)/shard_map/ppermute | solution.py:24
  189.2 10.7 %collective-permute-done.31 = f32[200,768]{1,0:T(8,128)} collective-permute-done((f32[200,768]{1,0:T(8,128)S(1)}, f32[200,768]{1,0:T(8,128)}, u32[]{:S(2)}, u32[]{:S(2)}) %collective-permute-start.31) | collective-permute-done | bytes 614432 | tf_op jit(solution)/shard_map/ppermute | solution.py:387
  199.9 4.6 %collective-permute-done.30 = f32[200,768]{1,0:T(8,128)} collective-permute-done((f32[200,768]{1,0:T(8,128)}, f32[200,768]{1,0:T(8,128)}, u32[]{:S(2)}, u32[]{:S(2)}) %collective-permute-start.30) | collective-permute-done | bytes 614432 | tf_op jit(solution)/shard_map/ppermute | solution.py:387
  210.5 2.9 %collective-permute-start.32 = (f32[256]{0:T(256)S(1)}, f32[256]{0:T(256)S(1)}, u32[]{:S(2)}, u32[]{:S(2)}) collective-permute-start(f32[256]{0:T(256)S(1)} %broadcast_select_fusion.3), channel_id=1, source_target_pairs={{0,4},{4,0},{1,5},{5,1},{2,6},{6,2},{3,7},{7,3},{8,12},{12,8},{9,1... | collective-permute-start | bytes 3080 | tf_op jit(solution)/shard_map/ppermute | solution.py:19
  216.7 6.3 %collective-permute-done.34 = f32[192,768]{1,0:T(8,128)S(1)} collective-permute-done((f32[192,768]{1,0:T(8,128)S(1)}, f32[192,768]{1,0:T(8,128)S(1)}, u32[]{:S(2)}, u32[]{:S(2)}) %collective-permute-start.34) | collective-permute-done | bytes 589856 | tf_op jit(solution)/shard_map/ppermute | solution.py:387
  233.1 6.7 %collective-permute-done.36.refs_1_ = f32[192,768]{1,0:T(8,128)S(1)} collective-permute-done((f32[192,768]{1,0:T(8,128)S(1)}, f32[192,768]{1,0:T(8,128)S(1)}, u32[]{:S(2)}, u32[]{:S(2)}) %collective-permute-start.36) | collective-permute-done | bytes 589856 | tf_op jit(solution)/shard_map/ppermute | solution.py:387
  239.8 3.3 %collective-permute-start.41 = (f32[192,768]{1,0:T(8,128)S(1)}, f32[192,768]{1,0:T(8,128)S(1)}, u32[]{:S(2)}, u32[]{:S(2)}) collective-permute-start(f32[192,768]{1,0:T(8,128)S(1)} %add_add_fusion.refs_0_), channel_id=1, source_target_pairs={{0,4},{4,0},{1,5},{5,1},{2,6},{6,2},{3,7},{7,3},{8,12},{12,8},{9,1... | collective-permute-start | bytes 1769480 | tf_op jit(solution)/shard_map/ppermute | solution.py:19
  247.4 4.7 %shard_map.66 = f32[1536,768]{1,0:T(8,128)} custom-call(s32[8]{0:T(128)S(1)} %stack.73.places_ref, f32[192,768]{1,0:T(8,128)} %copy-done.3, f32[192,768]{1,0:T(8,128)} %copy-done.13, f32[192,768]{1,0:T(8,128)} %copy-done.14, f32[192,768]{1,0:T(8,128)} %copy-done.15, f32[192,768]{1,0:T(8,128)} %copy-done.16, f32[192,768]{1,0:T(8,128)} %copy-done.17, ...), custom_call_target="tpu_custom_call" | custom-call | tf_op jit(solution)/shard_map/pallas_call | solution.py:405
  (167 shorter events, 90.2 us)
Async XLA Ops:
  16.2 16.6 %collective-permute-start.1 = (bf16[256,768]{1,0:T(8,128)(2,1)S(1)}, bf16[256,768]{1,0:T(8,128)(2,1)S(1)}, u32[]{:S(2)}, u32[]{:S(2)}) collective-permute-start(bf16[256,768]{1,0:T(8,128)(2,1)S(1)} %get-tuple-element.205), channel_id=1, source_target_pairs={{0,2},{1,3},{2,0},{3,1},{4,6},{5,7},{6,4},{7,5},{8,10},{9,11},{10,... | collective-permute-start | bytes 1179656 | tf_op jit(solution)/shard_map/ppermute | solution.py:24
  17.0 17.3 %collective-permute-start.2 = (bf16[256,768]{1,0:T(8,128)(2,1)S(1)}, bf16[256,768]{1,0:T(8,128)(2,1)S(1)}, u32[]{:S(2)}, u32[]{:S(2)}) collective-permute-start(bf16[256,768]{1,0:T(8,128)(2,1)S(1)} %get-tuple-element.204), channel_id=1, source_target_pairs={{0,3},{1,2},{2,1},{3,0},{4,7},{5,6},{6,5},{7,4},{8,11},{9,10},{10,... | collective-permute-start | bytes 1179656 | tf_op jit(solution)/shard_map/ppermute | solution.py:24
  35.3 19.3 %collective-permute-start.3 = (bf16[256,1536]{1,0:T(8,128)(2,1)}, bf16[256,1536]{1,0:T(8,128)(2,1)S(1)}, u32[]{:S(2)}, u32[]{:S(2)}) collective-permute-start(bf16[256,1536]{1,0:T(8,128)(2,1)} %get-tuple-element.104.refs_2_.embed_ref), channel_id=1, source_target_pairs={{0,8},{8,16},{16,24},{24,0},{1,9},{9,17},{17,25},{25,1},{2,10},{10... | collective-permute-start | bytes 2359304 | tf_op jit(solution)/shard_map/ppermute | solution.py:19
  36.6 18.0 %collective-permute-start.4 = (bf16[256,1536]{1,0:T(8,128)(2,1)}, bf16[256,1536]{1,0:T(8,128)(2,1)S(1)}, u32[]{:S(2)}, u32[]{:S(2)}) collective-permute-start(bf16[256,1536]{1,0:T(8,128)(2,1)} %get-tuple-element.104.refs_2_.embed_ref), channel_id=1, source_target_pairs={{0,24},{8,0},{16,8},{24,16},{1,25},{9,1},{17,9},{25,17},{2,26},{10... | collective-permute-start | bytes 2359304 | tf_op jit(solution)/shard_map/ppermute | solution.py:19
  38.0 18.5 %collective-permute-start.5 = (bf16[256,1536]{1,0:T(8,128)(2,1)S(1)}, bf16[256,1536]{1,0:T(8,128)(2,1)S(1)}, u32[]{:S(2)}, u32[]{:S(2)}) collective-permute-start(bf16[256,1536]{1,0:T(8,128)(2,1)S(1)} %get-tuple-element.105.refs_5_.refs_3_.embed_ref), channel_id=1, source_target_pairs={{0,32},{32,64},{64,96},{96,0},{1,33},{33,65},{65,97},{97,1},{2,34}... | collective-permute-start | bytes 2359304 | tf_op jit(solution)/shard_map/ppermute | solution.py:19
  39.2 17.3 %collective-permute-start.6 = (bf16[256,1536]{1,0:T(8,128)(2,1)S(1)}, bf16[256,1536]{1,0:T(8,128)(2,1)S(1)}, u32[]{:S(2)}, u32[]{:S(2)}) collective-permute-start(bf16[256,1536]{1,0:T(8,128)(2,1)S(1)} %get-tuple-element.105.refs_5_.refs_3_.embed_ref), channel_id=1, source_target_pairs={{0,96},{32,0},{64,32},{96,64},{1,97},{33,1},{65,33},{97,65},{2,98}... | collective-permute-start | bytes 2359304 | tf_op jit(solution)/shard_map/ppermute | solution.py:19
  40.7 15.8 %collective-permute-start.7 = (bf16[256,1536]{1,0:T(8,128)(2,1)S(1)}, bf16[256,1536]{1,0:T(8,128)(2,1)S(1)}, u32[]{:S(2)}, u32[]{:S(2)}) collective-permute-start(bf16[256,1536]{1,0:T(8,128)(2,1)S(1)} %get-tuple-element.105.refs_5_.refs_3_.embed_ref), channel_id=1, source_target_pairs={{0,4},{4,0},{1,5},{5,1},{2,6},{6,2},{3,7},{7,3},{8,12},{12,8},{9,1... | collective-permute-start | bytes 2359304 | tf_op jit(solution)/shard_map/ppermute | solution.py:19
  61.5 20.7 %collective-permute-start.10 = (bf16[256,1536]{1,0:T(8,128)(2,1)S(1)}, bf16[256,1536]{1,0:T(8,128)(2,1)S(1)}, u32[]{:S(2)}, u32[]{:S(2)}) collective-permute-start(bf16[256,1536]{1,0:T(8,128)(2,1)S(1)} %get-tuple-element.105.refs_5_.refs_3_.embed_ref), channel_id=1, source_target_pairs={{0,64},{32,96},{64,0},{96,32},{1,65},{33,97},{65,1},{97,33},{2,66}... | collective-permute-start | bytes 2359304 | tf_op jit(solution)/shard_map/ppermute | solution.py:19
  64.0 20.7 %collective-permute-start.11 = (bf16[256,1536]{1,0:T(8,128)(2,1)}, bf16[256,1536]{1,0:T(8,128)(2,1)S(1)}, u32[]{:S(2)}, u32[]{:S(2)}) collective-permute-start(bf16[256,1536]{1,0:T(8,128)(2,1)} %get-tuple-element.104.refs_2_.embed_ref), channel_id=1, source_target_pairs={{0,16},{8,24},{16,0},{24,8},{1,17},{9,25},{17,1},{25,9},{2,18},{10... | collective-permute-start | bytes 2359304 | tf_op jit(solution)/shard_map/ppermute | solution.py:19
  101.2 18.9 %collective-permute-start.16 = (bf16[256,1536]{1,0:T(8,128)(2,1)S(1)}, bf16[256,1536]{1,0:T(8,128)(2,1)}, u32[]{:S(2)}, u32[]{:S(2)}) collective-permute-start(bf16[256,1536]{1,0:T(8,128)(2,1)S(1)} %add_convert_fusion.2), channel_id=1, source_target_pairs={{0,96},{32,0},{64,32},{96,64},{1,97},{33,1},{65,33},{97,65},{2,98}... | collective-permute-start | bytes 2359304 | tf_op jit(solution)/shard_map/ppermute | solution.py:19
  102.4 19.7 %collective-permute-start.17 = (bf16[256,1536]{1,0:T(8,128)(2,1)S(1)}, bf16[256,1536]{1,0:T(8,128)(2,1)}, u32[]{:S(2)}, u32[]{:S(2)}) collective-permute-start(bf16[256,1536]{1,0:T(8,128)(2,1)S(1)} %add_convert_fusion.1), channel_id=1, source_target_pairs={{0,32},{32,64},{64,96},{96,0},{1,33},{33,65},{65,97},{97,1},{2,34}... | collective-permute-start | bytes 2359304 | tf_op jit(solution)/shard_map/ppermute | solution.py:19
  102.7 19.7 %collective-permute-start.18 = (bf16[256,1536]{1,0:T(8,128)(2,1)S(1)}, bf16[256,1536]{1,0:T(8,128)(2,1)}, u32[]{:S(2)}, u32[]{:S(2)}) collective-permute-start(bf16[256,1536]{1,0:T(8,128)(2,1)S(1)} %copy-done.26), channel_id=1, source_target_pairs={{0,16},{8,24},{16,0},{24,8},{1,17},{9,25},{17,1},{25,9},{2,18},{10... | collective-permute-start | bytes 2359304 | tf_op jit(solution)/shard_map/ppermute | solution.py:19
  104.4 18.0 %collective-permute-start.19 = (bf16[256,1536]{1,0:T(8,128)(2,1)S(1)}, bf16[256,1536]{1,0:T(8,128)(2,1)}, u32[]{:S(2)}, u32[]{:S(2)}) collective-permute-start(bf16[256,1536]{1,0:T(8,128)(2,1)S(1)} %copy-done.25), channel_id=1, source_target_pairs={{0,4},{4,0},{1,5},{5,1},{2,6},{6,2},{3,7},{7,3},{8,12},{12,8},{9,1... | collective-permute-start | bytes 2359304 | tf_op jit(solution)/shard_map/ppermute | solution.py:19
  125.5 55.8 %collective-permute-start.27 = (bf16[512,768]{1,0:T(8,128)(2,1)S(1)}, bf16[512,768]{1,0:T(8,128)(2,1)S(1)}, u32[]{:S(2)}, u32[]{:S(2)}) collective-permute-start(bf16[512,768]{1,0:T(8,128)(2,1)S(1)} %dynamic-slice_bitcast_fusion), channel_id=1, source_target_pairs={{0,4},{4,0},{1,5},{5,1},{2,6},{6,2},{3,7},{7,3},{8,12},{12,8},{9,1... | collective-permute-start | bytes 2359304 | tf_op jit(solution)/shard_map/ppermute | solution.py:19
  125.6 19.0 %collective-permute-start.22 = (bf16[256,1536]{1,0:T(8,128)(2,1)}, bf16[256,1536]{1,0:T(8,128)(2,1)S(1)}, u32[]{:S(2)}, u32[]{:S(2)}) collective-permute-start(bf16[256,1536]{1,0:T(8,128)(2,1)} %get-tuple-element.167), channel_id=1, source_target_pairs={{0,24},{8,0},{16,8},{24,16},{1,25},{9,1},{17,9},{25,17},{2,26},{10... | collective-permute-start | bytes 2359304 | tf_op jit(solution)/shard_map/ppermute | solution.py:19
  127.1 19.8 %collective-permute-start.23 = (bf16[256,1536]{1,0:T(8,128)(2,1)}, bf16[256,1536]{1,0:T(8,128)(2,1)S(1)}, u32[]{:S(2)}, u32[]{:S(2)}) collective-permute-start(bf16[256,1536]{1,0:T(8,128)(2,1)} %get-tuple-element.168), channel_id=1, source_target_pairs={{0,8},{8,16},{16,24},{24,0},{1,9},{9,17},{17,25},{25,1},{2,10},{10... | collective-permute-start | bytes 2359304 | tf_op jit(solution)/shard_map/ppermute | solution.py:19
  128.5 19.6 %collective-permute-start.21 = (bf16[256,1536]{1,0:T(8,128)(2,1)S(1)}, bf16[256,1536]{1,0:T(8,128)(2,1)S(1)}, u32[]{:S(2)}, u32[]{:S(2)}) collective-permute-start(bf16[256,1536]{1,0:T(8,128)(2,1)S(1)} %add_convert_fusion), channel_id=1, source_target_pairs={{0,64},{32,96},{64,0},{96,32},{1,65},{33,97},{65,1},{97,33},{2,66}... | collective-permute-start | bytes 2359304 | tf_op jit(solution)/shard_map/ppermute | solution.py:19
  156.0 19.3 %collective-permute-start.26 = (bf16[272,768]{1,0:T(8,128)(2,1)}, bf16[272,768]{1,0:T(8,128)(2,1)S(1)}, u32[]{:S(2)}, u32[]{:S(2)}) collective-permute-start(bf16[272,768]{1,0:T(8,128)(2,1)} %get-tuple-element.180), channel_id=1, source_target_pairs={{0,3},{1,2},{2,1},{3,0},{4,7},{5,6},{6,5},{7,4},{8,11},{9,10},{10,... | collective-permute-start | bytes 1253384 | tf_op jit(solution)/shard_map/ppermute | solution.py:24
  183.5 16.4 %collective-permute-start.31 = (f32[200,768]{1,0:T(8,128)S(1)}, f32[200,768]{1,0:T(8,128)}, u32[]{:S(2)}, u32[]{:S(2)}) collective-permute-start(f32[200,768]{1,0:T(8,128)S(1)} %pad_maximum_fusion.4), channel_id=1, source_target_pairs={{0,96},{4,28},{8,104},{12,4},{16,112},{20,12},{24,120},{28,20},{32... | collective-permute-start | bytes 1843208 | tf_op jit(solution)/shard_map/ppermute | solution.py:387
  187.1 17.4 %collective-permute-start.30 = (f32[200,768]{1,0:T(8,128)}, f32[200,768]{1,0:T(8,128)}, u32[]{:S(2)}, u32[]{:S(2)}) collective-permute-start(f32[200,768]{1,0:T(8,128)} %pad_maximum_fusion.3), channel_id=1, source_target_pairs={{0,32},{4,12},{8,40},{12,20},{16,48},{20,28},{24,56},{28,4},{32,64... | collective-permute-start | bytes 1843208 | tf_op jit(solution)/shard_map/ppermute | solution.py:387
  188.0 16.5 %collective-permute-start.29 = (f32[200,768]{1,0:T(8,128)}, f32[200,768]{1,0:T(8,128)}, u32[]{:S(2)}, u32[]{:S(2)}) collective-permute-start(f32[200,768]{1,0:T(8,128)} %pad_maximum_fusion.2), channel_id=1, source_target_pairs={{0,64},{4,20},{8,72},{12,28},{16,80},{20,4},{24,88},{28,12},{32,96... | collective-permute-start | bytes 1843208 | tf_op jit(solution)/shard_map/ppermute | solution.py:387
  207.0 16.0 %collective-permute-start.34 = (f32[192,768]{1,0:T(8,128)S(1)}, f32[192,768]{1,0:T(8,128)S(1)}, u32[]{:S(2)}, u32[]{:S(2)}) collective-permute-start(f32[192,768]{1,0:T(8,128)S(1)} %slice_add_fusion), channel_id=1, source_target_pairs={{0,8},{4,36},{8,16},{12,44},{16,24},{20,52},{24,0},{28,60},{32,40}... | collective-permute-start | bytes 1769480 | tf_op jit(solution)/shard_map/ppermute | solution.py:387
  223.2 16.6 %collective-permute-start.36 = (f32[192,768]{1,0:T(8,128)S(1)}, f32[192,768]{1,0:T(8,128)S(1)}, u32[]{:S(2)}, u32[]{:S(2)}) collective-permute-start(f32[192,768]{1,0:T(8,128)S(1)} %add_add_fusion.refs_0_), channel_id=1, source_target_pairs={{0,32},{4,12},{8,40},{12,20},{16,48},{20,28},{24,56},{28,4},{32,64... | collective-permute-start | bytes 1769480 | tf_op jit(solution)/shard_map/ppermute | solution.py:387
  223.2 16.6 %collective-permute-start.37 = (f32[192,768]{1,0:T(8,128)S(1)}, f32[192,768]{1,0:T(8,128)S(1)}, u32[]{:S(2)}, u32[]{:S(2)}) collective-permute-start(f32[192,768]{1,0:T(8,128)S(1)} %add_add_fusion.refs_0_), channel_id=1, source_target_pairs={{0,96},{4,28},{8,104},{12,4},{16,112},{20,12},{24,120},{28,20},{32... | collective-permute-start | bytes 1769480 | tf_op jit(solution)/shard_map/ppermute | solution.py:387
  (48 other events, 339.7 us)

commit v2 on v1

--- a/solution.py
+++ b/solution.py
@@ -12,6 +12,7 @@
 BF16 = jnp.bfloat16
 STEPS = (2, 1, 3)
 EXTRA = 16
+LINES = (0, 2, 3, 1)
 
 
 def shifted(value, axis, step):
@@ -271,28 +272,20 @@
     lines = jnp.pad(lines, ((0, 0), (0, 7), (0, half - rows)))
 
     grad_swap = shifted(grad_proj, "c", 1)
-    weight_part = lax.dot_general(
-        mine, grad_proj, (((0,), (0,)), ((), ())), preferred_element_type=F32
-    ) + lax.dot_general(others, grad_swap, (((0,), (0,)), ((), ())), preferred_element_type=F32)
-
     small = half // 4
     lead = jnp.where(c == 0, x, y)
     back = jnp.where(c == 0, y, x)
-
-    def message(k):
-        block = pick(weight_part, (lead + k) % 4, small)
-        return jnp.concatenate([block, lines[{0: 0, 1: 2, 2: 3, 3: 1}[k]]], axis=0)
-
-    a2, a1, a3 = tied(*(turned(message(k), 0, k) for k in STEPS))
-    piece = pick(weight_part, lead, small) + a1[:small] + a2[:small] + a3[:small]
-    line = (lines[0] + a1[small:] + a2[small:] + a3[small:])[0, :rows].reshape(2, part)
+    keep, m1, m2, m3 = weight_messages(
+        lead.reshape(1).astype(jnp.int32), mine, others, grad_proj, grad_swap, lines
+    )
+    a2, a1, a3 = tied(turned(m2, 0, 2), turned(m1, 0, 1), turned(m3, 0, 3))
+    total = keep + a1 + a2 + a3
+    piece = total[:small]
+    line = total[small, :rows].reshape(2, part)
     a2, a1, a3 = tied(*(turned(piece, 1, k) for k in STEPS))
     piece = (piece + a2) + (a1 + a3)
     given = shifted(jnp.where(c == 0, line[1], line[0]), "c", 1)
-    loss_rows, loss_cols, piece = tied(
-        jnp.where(c == 0, given, line[1]), jnp.where(c == 0, line[0], given), piece
-    )
-    pieces = [piece] + [turned(piece, 0, k) for k in (1, 3, 2)]
+    loss_rows, loss_cols = jnp.where(c == 0, given, line[1]), jnp.where(c == 0, line[0], given)
     loss_far = crossed(loss_cols, 1, 0)
     loss_near = crossed(jnp.where(m == 0, loss_rows, loss_far), 0, 1)
     upper = jnp.logical_and(t == 1, m == 1)
@@ -302,11 +295,15 @@
         + jnp.where(upper, 0.0, loss_far)
         + jnp.where(t == 1, loss_near, 0.0)
     ) / pairs
-    *pieces, row_loss = tied(*pieces, row_loss)
-    swapped = [shifted(v, "c", 1) for v in pieces]
+    row_loss, piece = tied(row_loss, piece)
+    p2, p1, p3, first = tied(*(turned(piece, 0, k) for k in STEPS), shifted(piece, "c", 1))
+    pieces = [piece, p1, p3, p2]
+    swapped = [shifted(v, "c", 1) for v in pieces[1:]]
     places = [c * half + (lead - k) % 4 * small for k in (0, 1, 3, 2)]
-    places += [(1 - c) * half + (back - k) % 4 * small for k in (0, 1, 3, 2)]
-    weight_grad = placed_rows(jnp.stack(places).astype(jnp.int32), pieces + swapped)
+    others = [(1 - c) * half + (back - k) % 4 * small for k in (0, 1, 3, 2)]
+    weight_grad = placed_rows(places + others[:1], pieces + [first], None)
+    *swapped, weight_grad = tied(*swapped, weight_grad)
+    weight_grad = placed_rows(others[1:], swapped, weight_grad)
     return (row_loss[None], weight_grad[None])
 
 
@@ -387,8 +384,40 @@
     return lax.ppermute(value, ("x", "y", "c"), route)
 
 
-def place_kernel(places_ref, *refs):
-    *pieces, out_ref, sems = refs
+def weight_kernel(lead_ref, mine, others, own_grad, other_grad, lines, *refs):
+    *outs, total_ref = refs
+    small = outs[0].shape[0] - lines.shape[1]
+    total_ref[...] = lax.dot_general(
+        mine[...], own_grad[...], (((0,), (0,)), ((), ())), preferred_element_type=F32
+    ) + lax.dot_general(
+        others[...], other_grad[...], (((0,), (0,)), ((), ())), preferred_element_type=F32
+    )
+    for k, out in enumerate(outs):
+        here = pl.multiple_of((lead_ref[0] + k) % 4 * small, small)
+        out[:small, :] = total_ref[pl.ds(here, small), :]
+        out[small:, :] = lines[LINES[k]]
+
+
+def weight_messages(lead, mine, others, own_grad, other_grad, lines):
+    half = mine.shape[1]
+    small = half // 4
+    vmem = pl.BlockSpec(memory_space=pltpu.VMEM)
+    message = jax.ShapeDtypeStruct((small + lines.shape[1], half), F32)
+    return pl.pallas_call(
+        weight_kernel,
+        in_specs=[pl.BlockSpec(memory_space=pltpu.SMEM)] + [vmem] * 5,
+        out_specs=[vmem] * 4,
+        out_shape=[message] * 4,
+        scratch_shapes=[pltpu.VMEM((half, half), F32)],
+        compiler_params=pltpu.CompilerParams(vmem_limit_bytes=14 * 2**20),
+        cost_estimate=pl.CostEstimate(
+            flops=4 * mine.size * half, bytes_accessed=8 * mine.size, transcendentals=0
+        ),
+    )(lead, mine, others, own_grad, other_grad, lines)
+
+
+def place_kernel(count, places_ref, *refs):
+    pieces, out_ref, sems = refs[:count], refs[-2], refs[-1]
     copies = []
     for i, piece in enumerate(pieces):
         size = piece.shape[0]
@@ -399,18 +428,23 @@
         copy.wait()
 
 
-def placed_rows(places, pieces):
+def placed_rows(places, pieces, target):
     size, width = pieces[0].shape
     count = len(pieces)
+    operands = in_hbm(pieces)
+    specs = [pl.BlockSpec(memory_space=pltpu.VMEM)] * count
+    if target is not None:
+        operands += in_hbm([target])
+        specs += [pl.BlockSpec(memory_space=pltpu.HBM)]
     return pl.pallas_call(
-        place_kernel,
-        in_specs=[pl.BlockSpec(memory_space=pltpu.SMEM)]
-        + [pl.BlockSpec(memory_space=pltpu.VMEM)] * count,
+        functools.partial(place_kernel, count),
+        in_specs=[pl.BlockSpec(memory_space=pltpu.SMEM)] + specs,
         out_specs=pl.BlockSpec(memory_space=pltpu.HBM),
-        out_shape=pltpu.HBM((size * count, width), F32),
+        out_shape=pltpu.HBM((8 * size, width), F32),
         scratch_shapes=[pltpu.SemaphoreType.DMA((count,))],
+        input_output_aliases={} if target is None else {count + 1: 0},
         compiler_params=pltpu.CompilerParams(vmem_limit_bytes=10 * 2**20),
-    )(places, *in_hbm(pieces))
+    )(jnp.stack(places).astype(jnp.int32), *operands)
 
 
 def solution(mesh):

time: 257 us -> 251 us (0.977)
  other arithmetic: 9.36 us -> 4.89 us
  matrix products: 7.84 us -> 3.93 us
  Pallas kernels: 49.8 us -> 53.1 us
    dot_general x2 -> x0, matrix products: 3.9 us -> none  [the longest x1 1.96 us: on_device(): lax.dot_general(others, grad_swap, (((0,), (0,)), ((), ())), preferred_el...]
    pallas_call x1 -> x3, Pallas kernels: 4.71 us -> 7.81 us  [the longest x2 6.23 us: placed_rows(): pl.pallas_call(functools.partial(place_kernel, count), in_specs=[pl.Block...]
    ppermute x9, starting transfers between devices: 10.3 us -> 13 us  [turned(): return lax.ppermute(value, ('x', 'y', 'c'), route)]
    unnamed x54 -> x58, local copies, waits for them, and re-layouts: 5.89 us -> 6.3 us
  transfers between devices with their start and end apart: 45 -> 45, of which waited for: 27 -> 24; matrix products, arithmetic and copies ran while one was open for 3% -> 2% of each run, Pallas kernels for 18% -> 20%
where the time goes in v2:
time: 251 us; the launch traced here: 246 us
  waiting for transfers between devices  109 us (43%)
  starting transfers between devices  60 us (24%)
  Pallas kernels  53.1 us (21%)
  local copies, waits for them, and re-layouts  8.42 us (3%)
  other arithmetic  4.89 us (2%)
  blocking collectives  4.76 us (2%)
  matrix products  3.93 us (2%)
  between operations  2.54 us (1%)
    ppermute x28, waiting for transfers between devices, shifted(): lax.ppermute(value, axis, [(i, (i + step) % count) for i in range(count)])  46.1 us
    ppermute x28, starting transfers between devices, shifted(): lax.ppermute(value, axis, [(i, (i + step) % count) for i in range(count)])  36.5 us
    pallas_call x4, Pallas kernels, tile_terms(): pl.pallas_call(body, in_specs=[smem, smem] + [vmem] * len(operands), out_...  35.3 us
    ppermute x8, waiting for transfers between devices, crossed(): return lax.ppermute(value, ('m', 't'), [(i, i ^ flip) for i in range(4)])  32.9 us
    ppermute x9, waiting for transfers between devices, turned(): return lax.ppermute(value, ('x', 'y', 'c'), route)  29.7 us
    ppermute x9, starting transfers between devices, turned(): return lax.ppermute(value, ('x', 'y', 'c'), route)  13 us
    ppermute x8, starting transfers between devices, crossed(): return lax.ppermute(value, ('m', 't'), [(i, i ^ flip) for i in range(4)])  10.6 us
    pallas_call x3, Pallas kernels, staged(): pl.pallas_call(body, in_specs=[pl.BlockSpec(memory_space=pltpu.SMEM)] * l...  10 us
  transfers between devices with their start and end apart: 45, of which 24 were waited for; matrix products, arithmetic and copies ran while one was open for 2% of the time, Pallas kernels for 20%

profile of v2, /device:TPU:1, one launch (start us, length us, event | category | flops | bytes accessed | tf_op | source)
XLA Modules:
  0.0 246.4 jit_solution(14538322473215649183)
XLA Ops:
  2.3 3.9 %multiply_reduce_fusion = (f32[512]{0:T(512)S(1)}, f32[512,768]{1,0:T(8,128)}) fusion(bf16[1,1536,768]{2,1,0:T(8,128)(2,1)S(1)} %copy-done, bf16[1,512,1536]{2,1,0:T(8,128)(2,1)} %param.4), kind=kOutput, calls=%fused_computation.7 | convolution fusion | flops 1208745472 | bytes 5507072 | tf_op jit(solution)/shard_map/dot_general | solution.py:189
  6.2 4.8 %psum.7 = f32[512]{0:T(512)S(1)} all-reduce(f32[512]{0:T(512)S(1)} %get-tuple-element.223), channel_id=1, replica_groups=mesh['x'=4,'y'=4,'c'=2,'m'=2,'t'=2] {'m'}, use_global_device_ids=true, to_apply=%region_1.0 | all-reduce | flops 512 | bytes 4096 | tf_op jit(solution)/shard_map/psum | solution.py:190
  12.7 3.5 %collective-permute-start.1 = (bf16[256,768]{1,0:T(8,128)(2,1)S(1)}, bf16[256,768]{1,0:T(8,128)(2,1)S(1)}, u32[]{:S(2)}, u32[]{:S(2)}) collective-permute-start(bf16[256,768]{1,0:T(8,128)(2,1)S(1)} %get-tuple-element.217), channel_id=1, source_target_pairs={{0,1},{1,0},{2,3},{3,2},{4,5},{5,4},{6,7},{7,6},{8,9},{9,8},{10,11... | collective-permute-start | bytes 1179656 | tf_op jit(solution)/shard_map/ppermute | solution.py:25
  17.0 6.9 %collective-permute-done.1 = bf16[256,768]{1,0:T(8,128)(2,1)S(1)} collective-permute-done((bf16[256,768]{1,0:T(8,128)(2,1)S(1)}, bf16[256,768]{1,0:T(8,128)(2,1)S(1)}, u32[]{:S(2)}, u32[]{:S(2)}) %collective-permute-start.1) | collective-permute-done | bytes 393248 | tf_op jit(solution)/shard_map/ppermute | solution.py:25
  23.9 8.9 %collective-permute-done.2 = bf16[256,768]{1,0:T(8,128)(2,1)S(1)} collective-permute-done((bf16[256,768]{1,0:T(8,128)(2,1)S(1)}, bf16[256,768]{1,0:T(8,128)(2,1)S(1)}, u32[]{:S(2)}, u32[]{:S(2)}) %collective-permute-start.2) | collective-permute-done | bytes 393248 | tf_op jit(solution)/shard_map/ppermute | solution.py:25
  42.2 11.3 %collective-permute-done.4.refs_3_ = bf16[256,1536]{1,0:T(8,128)(2,1)S(1)} collective-permute-done((bf16[256,1536]{1,0:T(8,128)(2,1)S(1)}, bf16[256,1536]{1,0:T(8,128)(2,1)S(1)}, u32[]{:S(2)}, u32[]{:S(2)}) %collective-permute-start.4) | collective-permute-done | bytes 786464 | tf_op jit(solution)/shard_map/ppermute | solution.py:20
  55.8 2.8 %collective-permute-start.10 = (bf16[256,1536]{1,0:T(8,128)(2,1)}, bf16[256,1536]{1,0:T(8,128)(2,1)}, u32[]{:S(2)}, u32[]{:S(2)}) collective-permute-start(bf16[256,1536]{1,0:T(8,128)(2,1)} %collective-permute-done.7.refs_9_.refs_5_), channel_id=1, source_target_pairs={{0,4},{4,0},{1,5},{5,1},{2,6},{6,2},{3,7},{7,3},{8,12},{12,8},{9,1... | collective-permute-start | bytes 2359304 | tf_op jit(solution)/shard_map/ppermute | solution.py:20
  65.0 15.2 %shard_map.59 = (f32[256,1536]{1,0:T(8,128)S(1)}, f32[256,1536]{1,0:T(8,128)S(1)}, f32[256,1536]{1,0:T(8,128)S(1)}, f32[256,1536]{1,0:T(8,128)S(1)}, f32[256,153...) custom-call(s32[1]{0:T(128)} %bitcast.3.refs_0_, ...), custom_call_target="tpu_custom_call" | custom-call | flops 10871635968 | bytes 14155776 | tf_op jit(solution)/shard_map/pallas_call | solution.py:146
  85.1 6.0 %shard_map.60 = (f32[256,1536]{1,0:T(8,128)S(1)}, bf16[256,1536]{1,0:T(8,128)(2,1)}, bf16[256,1536]{1,0:T(8,128)(2,1)}, bf16[256,1536]{1,0:T(8,128)(2,1)}, bf16[...) custom-call(s32[1]{0:T(128)} %bitcast.3.refs_0_, f32[2]{0:T(128)S(1)} %maximum_multiply_fusion.refs_1_, ...), custom_call_target="tpu_custom_call" | custom-call | flops 2415919104 | bytes 7864320 | tf_op jit(solution)/shard_map/pallas_call | solution.py:146
  92.7 6.4 %shard_map.61 = (bf16[256,1536]{1,0:T(8,128)(2,1)}, bf16[256,1536]{1,0:T(8,128)(2,1)}, bf16[256,1536]{1,0:T(8,128)(2,1)}, f32[256,1536]{1,0:T(8,128)S(1)}, f32[2...) custom-call(s32[1]{0:T(128)} %bitcast.3.refs_0_, f32[2]{0:T(128)S(1)} %maximum_multiply_fusion.refs_1_, ...), custom_call_target="tpu_custom_call" | custom-call | flops 2415919104 | bytes 7864320 | tf_op jit(solution)/shard_map/pallas_call | solution.py:146
  105.2 7.7 %shard_map.62 = (bf16[256,1536]{1,0:T(8,128)(2,1)}, bf16[256,1536]{1,0:T(8,128)(2,1)}, bf16[256,1536]{1,0:T(8,128)(2,1)}, bf16[256,1536]{1,0:T(8,128)(2,1)}, bf1...) custom-call(s32[1]{0:T(128)} %bitcast.3.refs_0_, f32[2]{0:T(128)S(1)} %maximum_multiply_fusion.refs_1_, ...), custom_call_target="tpu_custom_call" | custom-call | flops 3623878656 | bytes 7864320 | tf_op jit(solution)/shard_map/pallas_call | solution.py:146
  112.9 6.4 %collective-permute-done.17.refs_2_ = bf16[256,1536]{1,0:T(8,128)(2,1)S(1)} collective-permute-done((bf16[256,1536]{1,0:T(8,128)(2,1)S(1)}, bf16[256,1536]{1,0:T(8,128)(2,1)S(1)}, u32[]{:S(2)}, u32[]{:S(2)}) %collective-permute-start.17) | collective-permute-done | bytes 786464 | tf_op jit(solution)/shard_map/ppermute | solution.py:20
  128.9 14.6 %collective-permute-done.23.refs_1_ = bf16[256,1536]{1,0:T(8,128)(2,1)S(1)} collective-permute-done((bf16[256,1536]{1,0:T(8,128)(2,1)}, bf16[256,1536]{1,0:T(8,128)(2,1)S(1)}, u32[]{:S(2)}, u32[]{:S(2)}) %collective-permute-start.23) | collective-permute-done | bytes 786464 | tf_op jit(solution)/shard_map/ppermute | solution.py:20
  148.1 3.9 %shard_map.64 = (bf16[272,768]{1,0:T(8,128)(2,1)}, bf16[272,768]{1,0:T(8,128)(2,1)}) custom-call(bf16[256,1536]{1,0:T(8,128)(2,1)} %copy-done.2, bf16[256,1536]{1,0:T(8,128)(2,1)} %get-tuple-element.179.refs_0_, bf16[256,1536]{1,0:T(8,128)(2,1)} %collective-permute-done.20.refs_1_, bf16[256,1536]{1,0:T(8,128)(2,1)} %copy-done.6, ...), custom_call_target="tpu_custom_call" | custom-call | flops 2359296 | bytes 4718592 | tf_op jit(solution)/shard_map/pallas_call | solution.py:168
  152.0 3.0 %collective-permute-start.25 = (bf16[272,768]{1,0:T(8,128)(2,1)}, bf16[272,768]{1,0:T(8,128)(2,1)S(1)}, u32[]{:S(2)}, u32[]{:S(2)}) collective-permute-start(bf16[272,768]{1,0:T(8,128)(2,1)} %get-tuple-element.184), channel_id=1, source_target_pairs={{0,1},{1,0},{2,3},{3,2},{4,5},{5,4},{6,7},{7,6},{8,9},{9,8},{10,11... | collective-permute-start | bytes 1253384 | tf_op jit(solution)/shard_map/ppermute | solution.py:25
  155.4 3.6 %shard_map.63 = (bf16[272,768]{1,0:T(8,128)(2,1)}, bf16[272,768]{1,0:T(8,128)(2,1)}) custom-call(bf16[256,1536]{1,0:T(8,128)(2,1)} %copy-done.3, bf16[256,1536]{1,0:T(8,128)(2,1)} %get-tuple-element.170.refs_0_, bf16[256,1536]{1,0:T(8,128)(2,1)} %copy-done.10, bf16[256,1536]{1,0:T(8,128)(2,1)} %collective-permute-done.19.refs_2_, bf16[256,1536]{1,0:T(8,128)(2,1)} %copy-done.11), custom_call_target="tpu_custom_call" | custom-call | flops 2359296 | bytes 4718592 | tf_op jit(solution)/shard_map/pallas_call | solution.py:168
  163.0 11.3 %collective-permute-done.27.p11 = bf16[272,768]{1,0:T(8,128)(2,1)S(1)} collective-permute-done((bf16[272,768]{1,0:T(8,128)(2,1)}, bf16[272,768]{1,0:T(8,128)(2,1)S(1)}, u32[]{:S(2)}, u32[]{:S(2)}) %collective-permute-start.27) | collective-permute-done | bytes 417824 | tf_op jit(solution)/shard_map/ppermute | solution.py:25
  186.8 6.6 %collective-permute-done.29 = f32[200,768]{1,0:T(8,128)S(1)} collective-permute-done((f32[200,768]{1,0:T(8,128)S(1)}, f32[200,768]{1,0:T(8,128)S(1)}, u32[]{:S(2)}, u32[]{:S(2)}) %collective-permute-start.29) | collective-permute-done | bytes 614432 | tf_op jit(solution)/shard_map/ppermute | solution.py:384
  193.4 6.5 %collective-permute-done.30 = f32[200,768]{1,0:T(8,128)S(1)} collective-permute-done((f32[200,768]{1,0:T(8,128)S(1)}, f32[200,768]{1,0:T(8,128)S(1)}, u32[]{:S(2)}, u32[]{:S(2)}) %collective-permute-start.30) | collective-permute-done | bytes 614432 | tf_op jit(solution)/shard_map/ppermute | solution.py:384
  213.3 5.2 %collective-permute-done.36 = f32[192,768]{1,0:T(8,128)S(1)} collective-permute-done((f32[192,768]{1,0:T(8,128)S(1)}, f32[192,768]{1,0:T(8,128)S(1)}, u32[]{:S(2)}, u32[]{:S(2)}) %collective-permute-start.36) | collective-permute-done | bytes 589856 | tf_op jit(solution)/shard_map/ppermute | solution.py:384
  224.9 4.5 %collective-permute-done.38.refs_3_ = f32[192,768]{1,0:T(8,128)S(1)} collective-permute-done((f32[192,768]{1,0:T(8,128)S(1)}, f32[192,768]{1,0:T(8,128)S(1)}, u32[]{:S(2)}, u32[]{:S(2)}) %collective-permute-start.38) | collective-permute-done | bytes 589856 | tf_op jit(solution)/shard_map/ppermute | solution.py:384
  229.4 6.3 %collective-permute-done.39.refs_1_ = f32[192,768]{1,0:T(8,128)S(1)} collective-permute-done((f32[192,768]{1,0:T(8,128)S(1)}, f32[192,768]{1,0:T(8,128)S(1)}, u32[]{:S(2)}, u32[]{:S(2)}) %collective-permute-start.39) | collective-permute-done | bytes 589856 | tf_op jit(solution)/shard_map/ppermute | solution.py:384
  238.8 3.4 %shard_map.67.refs_3_ = f32[1536,768]{1,0:T(8,128)} custom-call(s32[5]{0:T(128)S(1)} %stack.77.places_ref, f32[192,768]{1,0:T(8,128)} %copy-done.4, f32[192,768]{1,0:T(8,128)} %copy-done.17, f32[192,768]{1,0:T(8,128)} %collective-permute-done.40.refs_2_, f32[192,768]{1,0:T(8,128)} %copy-done.16, f32[192,768]{1,0:T(8,128)} %copy-done.18), custom_call_target="tpu_custom_call" | custom-call | tf_op jit(solution)/shard_map/pallas_call | solution.py:439
  243.3 2.8 %shard_map.68 = f32[1536,768]{1,0:T(8,128)} custom-call(s32[3]{0:T(128)S(1)} %pad_add_fusion.1.places_ref, f32[192,768]{1,0:T(8,128)} %copy-done.14, f32[192,768]{1,0:T(8,128)} %copy-done.15, f32[192,768]{1,0:T(8,128)} %collective-permute-done.44.refs_2_, f32[1536,768]{1,0:T(8,128)} %shard_map.67.refs_3_), custom_call_target="tpu_custom_call", output_to_operand_aliasing={{}: (4, {})} | custom-call | tf_op jit(solution)/shard_map/pallas_call | solution.py:439
  (168 shorter events, 88.3 us)
Async XLA Ops:
  16.2 16.6 %collective-permute-start.2 = (bf16[256,768]{1,0:T(8,128)(2,1)S(1)}, bf16[256,768]{1,0:T(8,128)(2,1)S(1)}, u32[]{:S(2)}, u32[]{:S(2)}) collective-permute-start(bf16[256,768]{1,0:T(8,128)(2,1)S(1)} %get-tuple-element.216), channel_id=1, source_target_pairs={{0,2},{1,3},{2,0},{3,1},{4,6},{5,7},{6,4},{7,5},{8,10},{9,11},{10,... | collective-permute-start | bytes 1179656 | tf_op jit(solution)/shard_map/ppermute | solution.py:25
  17.0 17.3 %collective-permute-start.3 = (bf16[256,768]{1,0:T(8,128)(2,1)S(1)}, bf16[256,768]{1,0:T(8,128)(2,1)S(1)}, u32[]{:S(2)}, u32[]{:S(2)}) collective-permute-start(bf16[256,768]{1,0:T(8,128)(2,1)S(1)} %get-tuple-element.215), channel_id=1, source_target_pairs={{0,3},{1,2},{2,1},{3,0},{4,7},{5,6},{6,5},{7,4},{8,11},{9,10},{10,... | collective-permute-start | bytes 1179656 | tf_op jit(solution)/shard_map/ppermute | solution.py:25
  34.4 19.2 %collective-permute-start.4 = (bf16[256,1536]{1,0:T(8,128)(2,1)S(1)}, bf16[256,1536]{1,0:T(8,128)(2,1)S(1)}, u32[]{:S(2)}, u32[]{:S(2)}) collective-permute-start(bf16[256,1536]{1,0:T(8,128)(2,1)S(1)} %get-tuple-element.110.refs_2_.embed_ref), channel_id=1, source_target_pairs={{0,8},{8,16},{16,24},{24,0},{1,9},{9,17},{17,25},{25,1},{2,10},{10... | collective-permute-start | bytes 2359304 | tf_op jit(solution)/shard_map/ppermute | solution.py:20
  35.7 17.8 %collective-permute-start.5 = (bf16[256,1536]{1,0:T(8,128)(2,1)S(1)}, bf16[256,1536]{1,0:T(8,128)(2,1)S(1)}, u32[]{:S(2)}, u32[]{:S(2)}) collective-permute-start(bf16[256,1536]{1,0:T(8,128)(2,1)S(1)} %get-tuple-element.110.refs_2_.embed_ref), channel_id=1, source_target_pairs={{0,24},{8,0},{16,8},{24,16},{1,25},{9,1},{17,9},{25,17},{2,26},{10... | collective-permute-start | bytes 2359304 | tf_op jit(solution)/shard_map/ppermute | solution.py:20
  37.2 18.5 %collective-permute-start.6 = (bf16[256,1536]{1,0:T(8,128)(2,1)S(1)}, bf16[256,1536]{1,0:T(8,128)(2,1)S(1)}, u32[]{:S(2)}, u32[]{:S(2)}) collective-permute-start(bf16[256,1536]{1,0:T(8,128)(2,1)S(1)} %get-tuple-element.111.refs_5_.refs_3_.embed_ref), channel_id=1, source_target_pairs={{0,32},{32,64},{64,96},{96,0},{1,33},{33,65},{65,97},{97,1},{2,34}... | collective-permute-start | bytes 2359304 | tf_op jit(solution)/shard_map/ppermute | solution.py:20
  38.5 17.3 %collective-permute-start.7 = (bf16[256,1536]{1,0:T(8,128)(2,1)S(1)}, bf16[256,1536]{1,0:T(8,128)(2,1)}, u32[]{:S(2)}, u32[]{:S(2)}) collective-permute-start(bf16[256,1536]{1,0:T(8,128)(2,1)S(1)} %get-tuple-element.111.refs_5_.refs_3_.embed_ref), channel_id=1, source_target_pairs={{0,96},{32,0},{64,32},{96,64},{1,97},{33,1},{65,33},{97,65},{2,98}... | collective-permute-start | bytes 2359304 | tf_op jit(solution)/shard_map/ppermute | solution.py:20
  39.9 15.9 %collective-permute-start.8 = (bf16[256,1536]{1,0:T(8,128)(2,1)S(1)}, bf16[256,1536]{1,0:T(8,128)(2,1)S(1)}, u32[]{:S(2)}, u32[]{:S(2)}) collective-permute-start(bf16[256,1536]{1,0:T(8,128)(2,1)S(1)} %get-tuple-element.111.refs_5_.refs_3_.embed_ref), channel_id=1, source_target_pairs={{0,4},{4,0},{1,5},{5,1},{2,6},{6,2},{3,7},{7,3},{8,12},{12,8},{9,1... | collective-permute-start | bytes 2359304 | tf_op jit(solution)/shard_map/ppermute | solution.py:20
  60.9 20.7 %collective-permute-start.11 = (bf16[256,1536]{1,0:T(8,128)(2,1)S(1)}, bf16[256,1536]{1,0:T(8,128)(2,1)S(1)}, u32[]{:S(2)}, u32[]{:S(2)}) collective-permute-start(bf16[256,1536]{1,0:T(8,128)(2,1)S(1)} %get-tuple-element.111.refs_5_.refs_3_.embed_ref), channel_id=1, source_target_pairs={{0,64},{32,96},{64,0},{96,32},{1,65},{33,97},{65,1},{97,33},{2,66}... | collective-permute-start | bytes 2359304 | tf_op jit(solution)/shard_map/ppermute | solution.py:20
  63.3 20.5 %collective-permute-start.12 = (bf16[256,1536]{1,0:T(8,128)(2,1)S(1)}, bf16[256,1536]{1,0:T(8,128)(2,1)S(1)}, u32[]{:S(2)}, u32[]{:S(2)}) collective-permute-start(bf16[256,1536]{1,0:T(8,128)(2,1)S(1)} %get-tuple-element.110.refs_2_.embed_ref), channel_id=1, source_target_pairs={{0,16},{8,24},{16,0},{24,8},{1,17},{9,25},{17,1},{25,9},{2,18},{10... | collective-permute-start | bytes 2359304 | tf_op jit(solution)/shard_map/ppermute | solution.py:20
  100.5 18.9 %collective-permute-start.17 = (bf16[256,1536]{1,0:T(8,128)(2,1)S(1)}, bf16[256,1536]{1,0:T(8,128)(2,1)S(1)}, u32[]{:S(2)}, u32[]{:S(2)}) collective-permute-start(bf16[256,1536]{1,0:T(8,128)(2,1)S(1)} %add_convert_fusion.2), channel_id=1, source_target_pairs={{0,96},{32,0},{64,32},{96,64},{1,97},{33,1},{65,33},{97,65},{2,98}... | collective-permute-start | bytes 2359304 | tf_op jit(solution)/shard_map/ppermute | solution.py:20
  101.7 19.7 %collective-permute-start.18 = (bf16[256,1536]{1,0:T(8,128)(2,1)S(1)}, bf16[256,1536]{1,0:T(8,128)(2,1)}, u32[]{:S(2)}, u32[]{:S(2)}) collective-permute-start(bf16[256,1536]{1,0:T(8,128)(2,1)S(1)} %add_convert_fusion.1), channel_id=1, source_target_pairs={{0,32},{32,64},{64,96},{96,0},{1,33},{33,65},{65,97},{97,1},{2,34}... | collective-permute-start | bytes 2359304 | tf_op jit(solution)/shard_map/ppermute | solution.py:20
  102.0 19.7 %collective-permute-start.19 = (bf16[256,1536]{1,0:T(8,128)(2,1)S(1)}, bf16[256,1536]{1,0:T(8,128)(2,1)}, u32[]{:S(2)}, u32[]{:S(2)}) collective-permute-start(bf16[256,1536]{1,0:T(8,128)(2,1)S(1)} %copy-done.28), channel_id=1, source_target_pairs={{0,16},{8,24},{16,0},{24,8},{1,17},{9,25},{17,1},{25,9},{2,18},{10... | collective-permute-start | bytes 2359304 | tf_op jit(solution)/shard_map/ppermute | solution.py:20
  103.6 18.1 %collective-permute-start.20 = (bf16[256,1536]{1,0:T(8,128)(2,1)S(1)}, bf16[256,1536]{1,0:T(8,128)(2,1)}, u32[]{:S(2)}, u32[]{:S(2)}) collective-permute-start(bf16[256,1536]{1,0:T(8,128)(2,1)S(1)} %copy-done.27), channel_id=1, source_target_pairs={{0,4},{4,0},{1,5},{5,1},{2,6},{6,2},{3,7},{7,3},{8,12},{12,8},{9,1... | collective-permute-start | bytes 2359304 | tf_op jit(solution)/shard_map/ppermute | solution.py:20
  124.6 54.3 %collective-permute-start = (bf16[512,768]{1,0:T(8,128)(2,1)}, bf16[512,768]{1,0:T(8,128)(2,1)S(1)}, u32[]{:S(2)}, u32[]{:S(2)}) collective-permute-start(bf16[512,768]{1,0:T(8,128)(2,1)} %get-tuple-element.212), channel_id=1, source_target_pairs={{0,4},{4,0},{1,5},{5,1},{2,6},{6,2},{3,7},{7,3},{8,12},{12,8},{9,1... | collective-permute-start | bytes 2359304 | tf_op jit(solution)/shard_map/ppermute | solution.py:20
  124.6 18.8 %collective-permute-start.23 = (bf16[256,1536]{1,0:T(8,128)(2,1)}, bf16[256,1536]{1,0:T(8,128)(2,1)S(1)}, u32[]{:S(2)}, u32[]{:S(2)}) collective-permute-start(bf16[256,1536]{1,0:T(8,128)(2,1)} %get-tuple-element.173), channel_id=1, source_target_pairs={{0,24},{8,0},{16,8},{24,16},{1,25},{9,1},{17,9},{25,17},{2,26},{10... | collective-permute-start | bytes 2359304 | tf_op jit(solution)/shard_map/ppermute | solution.py:20
  126.0 19.7 %collective-permute-start.24 = (bf16[256,1536]{1,0:T(8,128)(2,1)}, bf16[256,1536]{1,0:T(8,128)(2,1)S(1)}, u32[]{:S(2)}, u32[]{:S(2)}) collective-permute-start(bf16[256,1536]{1,0:T(8,128)(2,1)} %get-tuple-element.174), channel_id=1, source_target_pairs={{0,8},{8,16},{16,24},{24,0},{1,9},{9,17},{17,25},{25,1},{2,10},{10... | collective-permute-start | bytes 2359304 | tf_op jit(solution)/shard_map/ppermute | solution.py:20
  127.6 19.6 %collective-permute-start.22 = (bf16[256,1536]{1,0:T(8,128)(2,1)S(1)}, bf16[256,1536]{1,0:T(8,128)(2,1)S(1)}, u32[]{:S(2)}, u32[]{:S(2)}) collective-permute-start(bf16[256,1536]{1,0:T(8,128)(2,1)S(1)} %add_convert_fusion), channel_id=1, source_target_pairs={{0,64},{32,96},{64,0},{96,32},{1,65},{33,97},{65,1},{97,33},{2,66}... | collective-permute-start | bytes 2359304 | tf_op jit(solution)/shard_map/ppermute | solution.py:20
  155.0 19.3 %collective-permute-start.27 = (bf16[272,768]{1,0:T(8,128)(2,1)}, bf16[272,768]{1,0:T(8,128)(2,1)S(1)}, u32[]{:S(2)}, u32[]{:S(2)}) collective-permute-start(bf16[272,768]{1,0:T(8,128)(2,1)} %get-tuple-element.186), channel_id=1, source_target_pairs={{0,3},{1,2},{2,1},{3,0},{4,7},{5,6},{6,5},{7,4},{8,11},{9,10},{10,... | collective-permute-start | bytes 1253384 | tf_op jit(solution)/shard_map/ppermute | solution.py:25
  159.1 15.2 %collective-permute-start.26 = (bf16[272,768]{1,0:T(8,128)(2,1)}, bf16[272,768]{1,0:T(8,128)(2,1)S(1)}, u32[]{:S(2)}, u32[]{:S(2)}) collective-permute-start(bf16[272,768]{1,0:T(8,128)(2,1)} %get-tuple-element.185), channel_id=1, source_target_pairs={{0,2},{1,3},{2,0},{3,1},{4,6},{5,7},{6,4},{7,5},{8,10},{9,11},{10,... | collective-permute-start | bytes 1253384 | tf_op jit(solution)/shard_map/ppermute | solution.py:25
  184.2 15.8 %collective-permute-start.30 = (f32[200,768]{1,0:T(8,128)S(1)}, f32[200,768]{1,0:T(8,128)S(1)}, u32[]{:S(2)}, u32[]{:S(2)}) collective-permute-start(f32[200,768]{1,0:T(8,128)S(1)} %get-tuple-element.194), channel_id=1, source_target_pairs={{0,32},{4,12},{8,40},{12,20},{16,48},{20,28},{24,56},{28,4},{32,64... | collective-permute-start | bytes 1843208 | tf_op jit(solution)/shard_map/ppermute | solution.py:384
  185.8 14.5 %collective-permute-start.31 = (f32[200,768]{1,0:T(8,128)S(1)}, f32[200,768]{1,0:T(8,128)S(1)}, u32[]{:S(2)}, u32[]{:S(2)}) collective-permute-start(f32[200,768]{1,0:T(8,128)S(1)} %get-tuple-element.195), channel_id=1, source_target_pairs={{0,96},{4,28},{8,104},{12,4},{16,112},{20,12},{24,120},{28,20},{32... | collective-permute-start | bytes 1843208 | tf_op jit(solution)/shard_map/ppermute | solution.py:384
  203.1 15.4 %collective-permute-start.36 = (f32[192,768]{1,0:T(8,128)S(1)}, f32[192,768]{1,0:T(8,128)S(1)}, u32[]{:S(2)}, u32[]{:S(2)}) collective-permute-start(f32[192,768]{1,0:T(8,128)S(1)} %slice.61), channel_id=1, source_target_pairs={{0,8},{4,36},{8,16},{12,44},{16,24},{20,52},{24,0},{28,60},{32,40}... | collective-permute-start | bytes 1769480 | tf_op jit(solution)/shard_map/ppermute | solution.py:384
  220.3 15.3 %collective-permute-start.39 = (f32[192,768]{1,0:T(8,128)S(1)}, f32[192,768]{1,0:T(8,128)S(1)}, u32[]{:S(2)}, u32[]{:S(2)}) collective-permute-start(f32[192,768]{1,0:T(8,128)S(1)} %add_add_fusion.1.refs_0_), channel_id=1, source_target_pairs={{0,32},{4,12},{8,40},{12,20},{16,48},{20,28},{24,56},{28,4},{32,64... | collective-permute-start | bytes 1769480 | tf_op jit(solution)/shard_map/ppermute | solution.py:384
  222.0 14.0 %collective-permute-start.40 = (f32[192,768]{1,0:T(8,128)S(1)}, f32[192,768]{1,0:T(8,128)}, u32[]{:S(2)}, u32[]{:S(2)}) collective-permute-start(f32[192,768]{1,0:T(8,128)S(1)} %add_add_fusion.1.refs_0_), channel_id=1, source_target_pairs={{0,96},{4,28},{8,104},{12,4},{16,112},{20,12},{24,120},{28,20},{32... | collective-permute-start | bytes 1769480 | tf_op jit(solution)/shard_map/ppermute | solution.py:384
  (50 other events, 370.8 us)

commit v3 on v2

--- a/solution.py
+++ b/solution.py
@@ -121,12 +121,14 @@
         la_ref[r] = jnp.sum(loss_ref[pl.ds(r * part, part), :].T, axis=0, keepdims=True)
 
 
-def tile_terms(rows, cols, row_sums, col_sums, row_types, col_types, diagonal, diag, scales):
+def tile_terms(rows, cols, row_sums, col_sums, row_types, col_types, diagonal, diag, scales, far=()):
     part, width = rows[0].shape
     n_rows, n_pairs = len(rows), len(cols)
     smem = pl.BlockSpec(memory_space=pltpu.SMEM)
     vmem = pl.BlockSpec(memory_space=pltpu.VMEM)
-    operands = in_hbm(list(rows) + [v for pair in cols for v in pair])
+    operands = list(rows) + [v for pair in cols for v in pair]
+    held = set(map(id, far))
+    operands = [v if id(v) in held else in_hbm([v])[0] for v in operands]
     operands += [v for v in row_sums if v is not None]
     operands += [v for pair in col_sums if pair is not None for v in pair]
     body = functools.partial(
@@ -163,7 +165,7 @@
     return grad_rows, grad_cols, out[-2].reshape(n_rows, part), out[-1].reshape(n_pairs, 2, part)
 
 
-def staged(body, smalls, operands, out_shape, cost):
+def staged(body, smalls, operands, out_shape, cost, held=False):
     vmem = pl.BlockSpec(memory_space=pltpu.VMEM)
     return pl.pallas_call(
         body,
@@ -172,7 +174,7 @@
         out_shape=out_shape,
         compiler_params=pltpu.CompilerParams(vmem_limit_bytes=10 * 2**20),
         cost_estimate=pl.CostEstimate(flops=cost, bytes_accessed=2 * cost, transcendentals=0),
-    )(*smalls, *in_hbm(operands))
+    )(*smalls, *(in_hbm(operands) if held else operands))
 
 
 def on_device(features, projection, similarity_scale, logit_bias):
@@ -231,11 +233,29 @@
     c2, r2, a0, b0, a1, b1, a3, b3, *rows_sum = tied(c2, r2, a0, b0, a1, b1, a3, b3, *rows_sum)
     d2 = shifted(c2, "c", 1)
     (sum2,), (s1, t1, s3, t3), la2, lb2 = tile_terms(
-        [r2], [cols1, cols3], [None], [[a1, b1], [a3, b3]], [F32], [BF16] * 2, False, diag, scales
+        [r2],
+        [cols1, cols3],
+        [None],
+        [[a1, b1], [a3, b3]],
+        [F32],
+        [BF16] * 2,
+        False,
+        diag,
+        scales,
+        [r2],
     )
     t1, t3 = shifted(t1, "c", 1), shifted(t3, "c", 1)
     (g2,), (s0, t0, a2, b2), la4, lb4 = tile_terms(
-        [r2], [cols0, [c2, d2]], [sum2], [[a0, b0], None], [BF16], [BF16, F32], False, diag, scales
+        [r2],
+        [cols0, [c2, d2]],
+        [sum2],
+        [[a0, b0], None],
+        [BF16],
+        [BF16, F32],
+        False,
+        diag,
+        scales,
+        [r2, c2, d2],
     )
     t1, t3, g2, s0, t0, a2, b2 = tied(t1, t3, g2, s0, t0, a2, b2)
 
@@ -247,7 +267,16 @@
     f2 = shifted(g2, "y", 2)
     t0 = shifted(t0, "c", 1)
     (g0, g1, g3), (s2, t2), la3, lb3 = tile_terms(
-        near, [[c2, d2]], rows_sum, [[a2, b2]], [BF16] * 3, [BF16], False, diag, scales
+        near,
+        [[c2, d2]],
+        rows_sum,
+        [[a2, b2]],
+        [BF16] * 3,
+        [BF16],
+        False,
+        diag,
+        scales,
+        [c2, d2],
     )
     loss_rows = jnp.concatenate([la + la3, la2 + la4])
     loss_cols = jnp.stack([lb[0] + lb4[0], lb[1] + lb2[0], lb[2] + lb2[1], lb4[1] + lb3[0]], axis=1)
@@ -369,7 +398,7 @@
 def unpacked(flags, scale, pieces, projected, inverse):
     out = jax.ShapeDtypeStruct(projected.shape, BF16)
     operands = (*pieces, projected, inverse)
-    return staged(unpack_kernel, (flags, scale), operands, out, 6 * projected.size)
+    return staged(unpack_kernel, (flags, scale), operands, out, 6 * projected.size, held=True)
 
 
 def turned(value, late, step):

time: 251 us -> 250 us (level)
  Pallas kernels: 53.1 us -> 49.2 us
  waiting for transfers between devices: 109 us -> 112 us
    pallas_call x3, Pallas kernels: 10 us -> 5.65 us  [staged(): pl.pallas_call(body, in_specs=[pl.BlockSpec(memory_space=pltpu.SMEM)] * l...]
    unnamed x58 -> x64, local copies, waits for them, and re-layouts: 6.3 us -> 6.28 us
  transfers between devices with their start and end apart: 45 -> 45, of which waited for: 24 -> 25; matrix products, arithmetic and copies ran while one was open for 2% -> 2% of each run, Pallas kernels for 20% -> 18%
where the time goes in v3:
time: 250 us; the launch traced here: 245 us
  waiting for transfers between devices  112 us (45%)
  starting transfers between devices  58.9 us (24%)
  Pallas kernels  49.2 us (20%)
  local copies, waits for them, and re-layouts  8.69 us (3%)
  other arithmetic  4.92 us (2%)
  blocking collectives  4.76 us (2%)
  matrix products  3.93 us (2%)
  between operations  2.56 us (1%)
    ppermute x28, waiting for transfers between devices, shifted(): lax.ppermute(value, axis, [(i, (i + step) % count) for i in range(count)])  47.1 us
    ppermute x28, starting transfers between devices, shifted(): lax.ppermute(value, axis, [(i, (i + step) % count) for i in range(count)])  35.2 us
    ppermute x8, waiting for transfers between devices, crossed(): return lax.ppermute(value, ('m', 't'), [(i, i ^ flip) for i in range(4)])  35 us
    pallas_call x4, Pallas kernels, tile_terms(): pl.pallas_call(body, in_specs=[smem, smem] + [vmem] * len(operands), out_...  34.6 us
    ppermute x9, waiting for transfers between devices, turned(): return lax.ppermute(value, ('x', 'y', 'c'), route)  29.7 us
    ppermute x9, starting transfers between devices, turned(): return lax.ppermute(value, ('x', 'y', 'c'), route)  13 us
    ppermute x8, starting transfers between devices, crossed(): return lax.ppermute(value, ('m', 't'), [(i, i ^ flip) for i in range(4)])  10.7 us
    unnamed x64, local copies, waits for them, and re-layouts  6.28 us
  transfers between devices with their start and end apart: 45, of which 25 were waited for; matrix products, arithmetic and copies ran while one was open for 2% of the time, Pallas kernels for 18%

profile of v3, /device:TPU:1, one launch (start us, length us, event | category | flops | bytes accessed | tf_op | source)
XLA Modules:
  0.0 244.8 jit_solution(9094350356480115346)
XLA Ops:
  2.3 3.9 %multiply_reduce_fusion = (f32[512]{0:T(512)S(1)}, f32[512,768]{1,0:T(8,128)}) fusion(bf16[1,1536,768]{2,1,0:T(8,128)(2,1)S(1)} %copy-done, bf16[1,512,1536]{2,1,0:T(8,128)(2,1)} %param.4), kind=kOutput, calls=%fused_computation.7 | convolution fusion | flops 1208745472 | bytes 5507072 | tf_op jit(solution)/shard_map/dot_general | solution.py:191
  6.2 4.8 %psum.7 = f32[512]{0:T(512)S(1)} all-reduce(f32[512]{0:T(512)S(1)} %get-tuple-element.223), channel_id=1, replica_groups=mesh['x'=4,'y'=4,'c'=2,'m'=2,'t'=2] {'m'}, use_global_device_ids=true, to_apply=%region_1.0 | all-reduce | flops 512 | bytes 4096 | tf_op jit(solution)/shard_map/psum | solution.py:192
  12.7 3.5 %collective-permute-start.1 = (bf16[256,768]{1,0:T(8,128)(2,1)S(1)}, bf16[256,768]{1,0:T(8,128)(2,1)S(1)}, u32[]{:S(2)}, u32[]{:S(2)}) collective-permute-start(bf16[256,768]{1,0:T(8,128)(2,1)S(1)} %get-tuple-element.217), channel_id=1, source_target_pairs={{0,1},{1,0},{2,3},{3,2},{4,5},{5,4},{6,7},{7,6},{8,9},{9,8},{10,11... | collective-permute-start | bytes 1179656 | tf_op jit(solution)/shard_map/ppermute | solution.py:25
  17.0 6.9 %collective-permute-done.1 = bf16[256,768]{1,0:T(8,128)(2,1)S(1)} collective-permute-done((bf16[256,768]{1,0:T(8,128)(2,1)S(1)}, bf16[256,768]{1,0:T(8,128)(2,1)S(1)}, u32[]{:S(2)}, u32[]{:S(2)}) %collective-permute-start.1) | collective-permute-done | bytes 393248 | tf_op jit(solution)/shard_map/ppermute | solution.py:25
  23.9 8.9 %collective-permute-done.2 = bf16[256,768]{1,0:T(8,128)(2,1)S(1)} collective-permute-done((bf16[256,768]{1,0:T(8,128)(2,1)S(1)}, bf16[256,768]{1,0:T(8,128)(2,1)S(1)}, u32[]{:S(2)}, u32[]{:S(2)}) %collective-permute-start.2) | collective-permute-done | bytes 393248 | tf_op jit(solution)/shard_map/ppermute | solution.py:25
  42.2 11.3 %collective-permute-done.4.refs_3_ = bf16[256,1536]{1,0:T(8,128)(2,1)S(1)} collective-permute-done((bf16[256,1536]{1,0:T(8,128)(2,1)S(1)}, bf16[256,1536]{1,0:T(8,128)(2,1)S(1)}, u32[]{:S(2)}, u32[]{:S(2)}) %collective-permute-start.4) | collective-permute-done | bytes 786464 | tf_op jit(solution)/shard_map/ppermute | solution.py:20
  55.8 2.7 %collective-permute-start.10 = (bf16[256,1536]{1,0:T(8,128)(2,1)S(1)}, bf16[256,1536]{1,0:T(8,128)(2,1)}, u32[]{:S(2)}, u32[]{:S(2)}) collective-permute-start(bf16[256,1536]{1,0:T(8,128)(2,1)S(1)} %collective-permute-done.7.refs_9_.refs_5_), channel_id=1, source_target_pairs={{0,4},{4,0},{1,5},{5,1},{2,6},{6,2},{3,7},{7,3},{8,12},{12,8},{9,1... | collective-permute-start | bytes 2359304 | tf_op jit(solution)/shard_map/ppermute | solution.py:20
  65.0 15.2 %shard_map.59 = (f32[256,1536]{1,0:T(8,128)S(1)}, f32[256,1536]{1,0:T(8,128)S(1)}, f32[256,1536]{1,0:T(8,128)S(1)}, f32[256,1536]{1,0:T(8,128)S(1)}, f32[256,153...) custom-call(s32[1]{0:T(128)} %bitcast.3.refs_0_, ...), custom_call_target="tpu_custom_call" | custom-call | flops 10871635968 | bytes 14155776 | tf_op jit(solution)/shard_map/pallas_call | solution.py:148
  85.0 6.2 %shard_map.60 = (f32[256,1536]{1,0:T(8,128)S(1)}, bf16[256,1536]{1,0:T(8,128)(2,1)}, bf16[256,1536]{1,0:T(8,128)(2,1)}, bf16[256,1536]{1,0:T(8,128)(2,1)}, bf16[...) custom-call(s32[1]{0:T(128)} %bitcast.3.refs_0_, f32[2]{0:T(128)S(1)} %maximum_multiply_fusion.refs_1_, ...), custom_call_target="tpu_custom_call" | custom-call | flops 2415919104 | bytes 7864320 | tf_op jit(solution)/shard_map/pallas_call | solution.py:148
  91.7 5.8 %shard_map.61 = (bf16[256,1536]{1,0:T(8,128)(2,1)}, bf16[256,1536]{1,0:T(8,128)(2,1)}, bf16[256,1536]{1,0:T(8,128)(2,1)}, f32[256,1536]{1,0:T(8,128)S(1)}, f32[2...) custom-call(s32[1]{0:T(128)} %bitcast.3.refs_0_, f32[2]{0:T(128)S(1)} %maximum_multiply_fusion.refs_1_, ...), custom_call_target="tpu_custom_call" | custom-call | flops 2415919104 | bytes 7864320 | tf_op jit(solution)/shard_map/pallas_call | solution.py:148
  103.2 7.5 %shard_map.62 = (bf16[256,1536]{1,0:T(8,128)(2,1)}, bf16[256,1536]{1,0:T(8,128)(2,1)}, bf16[256,1536]{1,0:T(8,128)(2,1)}, bf16[256,1536]{1,0:T(8,128)(2,1)}, bf1...) custom-call(s32[1]{0:T(128)} %bitcast.3.refs_0_, f32[2]{0:T(128)S(1)} %maximum_multiply_fusion.refs_1_, ...), custom_call_target="tpu_custom_call" | custom-call | flops 3623878656 | bytes 7864320 | tf_op jit(solution)/shard_map/pallas_call | solution.py:148
  110.7 7.4 %collective-permute-done.17.refs_2_ = bf16[256,1536]{1,0:T(8,128)(2,1)S(1)} collective-permute-done((bf16[256,1536]{1,0:T(8,128)(2,1)S(1)}, bf16[256,1536]{1,0:T(8,128)(2,1)S(1)}, u32[]{:S(2)}, u32[]{:S(2)}) %collective-permute-start.17) | collective-permute-done | bytes 786464 | tf_op jit(solution)/shard_map/ppermute | solution.py:20
  129.3 14.6 %collective-permute-done.23.refs_1_ = bf16[256,1536]{1,0:T(8,128)(2,1)S(1)} collective-permute-done((bf16[256,1536]{1,0:T(8,128)(2,1)}, bf16[256,1536]{1,0:T(8,128)(2,1)S(1)}, u32[]{:S(2)}, u32[]{:S(2)}) %collective-permute-start.23) | collective-permute-done | bytes 786464 | tf_op jit(solution)/shard_map/ppermute | solution.py:20
  149.3 3.0 %collective-permute-start.25 = (bf16[272,768]{1,0:T(8,128)(2,1)}, bf16[272,768]{1,0:T(8,128)(2,1)S(1)}, u32[]{:S(2)}, u32[]{:S(2)}) collective-permute-start(bf16[272,768]{1,0:T(8,128)(2,1)} %get-tuple-element.184), channel_id=1, source_target_pairs={{0,1},{1,0},{2,3},{3,2},{4,5},{5,4},{6,7},{7,6},{8,9},{9,8},{10,11... | collective-permute-start | bytes 1253384 | tf_op jit(solution)/shard_map/ppermute | solution.py:25
  154.6 2.6 %collective-permute-start.16 = (f32[2,4,256]{2,1,0:T(4,128)S(1)}, f32[2,4,256]{2,1,0:T(4,128)S(1)}, u32[]{:S(2)}, u32[]{:S(2)}) collective-permute-start(f32[2,4,256]{2,1,0:T(4,128)S(1)} %fusion.3), channel_id=1, source_target_pairs={{0,4},{4,0},{1,5},{5,1},{2,6},{6,2},{3,7},{7,3},{8,12},{12,8},{9,1... | collective-permute-start | bytes 24584 | tf_op jit(solution)/shard_map/ppermute | solution.py:20
  160.4 11.2 %collective-permute-done.27.p11 = bf16[272,768]{1,0:T(8,128)(2,1)S(1)} collective-permute-done((bf16[272,768]{1,0:T(8,128)(2,1)}, bf16[272,768]{1,0:T(8,128)(2,1)S(1)}, u32[]{:S(2)}, u32[]{:S(2)}) %collective-permute-start.27) | collective-permute-done | bytes 417824 | tf_op jit(solution)/shard_map/ppermute | solution.py:25
  178.1 2.7 %shard_map.66 = (f32[200,768]{1,0:T(8,128)S(1)}, f32[200,768]{1,0:T(8,128)S(1)}, f32[200,768]{1,0:T(8,128)S(1)}, f32[200,768]{1,0:T(8,128)S(1)}) custom-call(s32[1]{0:T(128)} %bitcast.lead_ref, bf16[512,768]{1,0:T(8,128)(2,1)S(1)} %copy-done.9, bf16[512,768]{1,0:T(8,128)(2,1)} %collective-permute-done.others, bf16[512,768]{1,0:T(8,128)(2,1)S(1)} %shard_map.65.own_grad, ...), custom_call_target="tpu_custom_call" | custom-call | flops 1207959552 | bytes 3145728 | tf_op jit(solution)/shard_map/pallas_call | solution.py:435
  185.3 6.6 %collective-permute-done.29 = f32[200,768]{1,0:T(8,128)S(1)} collective-permute-done((f32[200,768]{1,0:T(8,128)S(1)}, f32[200,768]{1,0:T(8,128)S(1)}, u32[]{:S(2)}, u32[]{:S(2)}) %collective-permute-start.29) | collective-permute-done | bytes 614432 | tf_op jit(solution)/shard_map/ppermute | solution.py:413
  191.9 6.5 %collective-permute-done.30 = f32[200,768]{1,0:T(8,128)S(1)} collective-permute-done((f32[200,768]{1,0:T(8,128)S(1)}, f32[200,768]{1,0:T(8,128)S(1)}, u32[]{:S(2)}, u32[]{:S(2)}) %collective-permute-start.30) | collective-permute-done | bytes 614432 | tf_op jit(solution)/shard_map/ppermute | solution.py:413
  211.8 5.2 %collective-permute-done.36 = f32[192,768]{1,0:T(8,128)S(1)} collective-permute-done((f32[192,768]{1,0:T(8,128)S(1)}, f32[192,768]{1,0:T(8,128)S(1)}, u32[]{:S(2)}, u32[]{:S(2)}) %collective-permute-start.36) | collective-permute-done | bytes 589856 | tf_op jit(solution)/shard_map/ppermute | solution.py:413
  223.3 4.5 %collective-permute-done.38.refs_3_ = f32[192,768]{1,0:T(8,128)S(1)} collective-permute-done((f32[192,768]{1,0:T(8,128)S(1)}, f32[192,768]{1,0:T(8,128)S(1)}, u32[]{:S(2)}, u32[]{:S(2)}) %collective-permute-start.38) | collective-permute-done | bytes 589856 | tf_op jit(solution)/shard_map/ppermute | solution.py:413
  227.9 6.3 %collective-permute-done.39.refs_1_ = f32[192,768]{1,0:T(8,128)S(1)} collective-permute-done((f32[192,768]{1,0:T(8,128)S(1)}, f32[192,768]{1,0:T(8,128)S(1)}, u32[]{:S(2)}, u32[]{:S(2)}) %collective-permute-start.39) | collective-permute-done | bytes 589856 | tf_op jit(solution)/shard_map/ppermute | solution.py:413
  237.3 3.4 %shard_map.67.refs_3_ = f32[1536,768]{1,0:T(8,128)} custom-call(s32[5]{0:T(128)S(1)} %stack.77.places_ref, f32[192,768]{1,0:T(8,128)} %copy-done.13, f32[192,768]{1,0:T(8,128)} %copy-done.22, f32[192,768]{1,0:T(8,128)} %collective-permute-done.40.refs_2_, f32[192,768]{1,0:T(8,128)} %copy-done.21, f32[192,768]{1,0:T(8,128)} %copy-done.23), custom_call_target="tpu_custom_call" | custom-call | tf_op jit(solution)/shard_map/pallas_call | solution.py:468
  241.8 2.8 %shard_map.68 = f32[1536,768]{1,0:T(8,128)} custom-call(s32[3]{0:T(128)S(1)} %pad_add_fusion.1.places_ref, f32[192,768]{1,0:T(8,128)} %copy-done.19, f32[192,768]{1,0:T(8,128)} %copy-done.20, f32[192,768]{1,0:T(8,128)} %collective-permute-done.44.refs_2_, f32[1536,768]{1,0:T(8,128)} %shard_map.67.refs_3_), custom_call_target="tpu_custom_call", output_to_operand_aliasing={{}: (4, {})} | custom-call | tf_op jit(solution)/shard_map/pallas_call | solution.py:468
  (174 shorter events, 88.7 us)
Async XLA Ops:
  16.2 16.6 %collective-permute-start.2 = (bf16[256,768]{1,0:T(8,128)(2,1)S(1)}, bf16[256,768]{1,0:T(8,128)(2,1)S(1)}, u32[]{:S(2)}, u32[]{:S(2)}) collective-permute-start(bf16[256,768]{1,0:T(8,128)(2,1)S(1)} %get-tuple-element.216), channel_id=1, source_target_pairs={{0,2},{1,3},{2,0},{3,1},{4,6},{5,7},{6,4},{7,5},{8,10},{9,11},{10,... | collective-permute-start | bytes 1179656 | tf_op jit(solution)/shard_map/ppermute | solution.py:25
  17.0 17.3 %collective-permute-start.3 = (bf16[256,768]{1,0:T(8,128)(2,1)S(1)}, bf16[256,768]{1,0:T(8,128)(2,1)S(1)}, u32[]{:S(2)}, u32[]{:S(2)}) collective-permute-start(bf16[256,768]{1,0:T(8,128)(2,1)S(1)} %get-tuple-element.215), channel_id=1, source_target_pairs={{0,3},{1,2},{2,1},{3,0},{4,7},{5,6},{6,5},{7,4},{8,11},{9,10},{10,... | collective-permute-start | bytes 1179656 | tf_op jit(solution)/shard_map/ppermute | solution.py:25
  34.4 19.2 %collective-permute-start.4 = (bf16[256,1536]{1,0:T(8,128)(2,1)S(1)}, bf16[256,1536]{1,0:T(8,128)(2,1)S(1)}, u32[]{:S(2)}, u32[]{:S(2)}) collective-permute-start(bf16[256,1536]{1,0:T(8,128)(2,1)S(1)} %get-tuple-element.110.refs_2_.embed_ref), channel_id=1, source_target_pairs={{0,8},{8,16},{16,24},{24,0},{1,9},{9,17},{17,25},{25,1},{2,10},{10... | collective-permute-start | bytes 2359304 | tf_op jit(solution)/shard_map/ppermute | solution.py:20
  35.7 17.8 %collective-permute-start.5 = (bf16[256,1536]{1,0:T(8,128)(2,1)S(1)}, bf16[256,1536]{1,0:T(8,128)(2,1)S(1)}, u32[]{:S(2)}, u32[]{:S(2)}) collective-permute-start(bf16[256,1536]{1,0:T(8,128)(2,1)S(1)} %get-tuple-element.110.refs_2_.embed_ref), channel_id=1, source_target_pairs={{0,24},{8,0},{16,8},{24,16},{1,25},{9,1},{17,9},{25,17},{2,26},{10... | collective-permute-start | bytes 2359304 | tf_op jit(solution)/shard_map/ppermute | solution.py:20
  37.2 18.5 %collective-permute-start.6 = (bf16[256,1536]{1,0:T(8,128)(2,1)S(1)}, bf16[256,1536]{1,0:T(8,128)(2,1)S(1)}, u32[]{:S(2)}, u32[]{:S(2)}) collective-permute-start(bf16[256,1536]{1,0:T(8,128)(2,1)S(1)} %get-tuple-element.111.refs_5_.refs_3_.embed_ref), channel_id=1, source_target_pairs={{0,32},{32,64},{64,96},{96,0},{1,33},{33,65},{65,97},{97,1},{2,34}... | collective-permute-start | bytes 2359304 | tf_op jit(solution)/shard_map/ppermute | solution.py:20
  38.4 17.3 %collective-permute-start.7 = (bf16[256,1536]{1,0:T(8,128)(2,1)S(1)}, bf16[256,1536]{1,0:T(8,128)(2,1)S(1)}, u32[]{:S(2)}, u32[]{:S(2)}) collective-permute-start(bf16[256,1536]{1,0:T(8,128)(2,1)S(1)} %get-tuple-element.111.refs_5_.refs_3_.embed_ref), channel_id=1, source_target_pairs={{0,96},{32,0},{64,32},{96,64},{1,97},{33,1},{65,33},{97,65},{2,98}... | collective-permute-start | bytes 2359304 | tf_op jit(solution)/shard_map/ppermute | solution.py:20
  39.9 15.9 %collective-permute-start.8 = (bf16[256,1536]{1,0:T(8,128)(2,1)S(1)}, bf16[256,1536]{1,0:T(8,128)(2,1)S(1)}, u32[]{:S(2)}, u32[]{:S(2)}) collective-permute-start(bf16[256,1536]{1,0:T(8,128)(2,1)S(1)} %get-tuple-element.111.refs_5_.refs_3_.embed_ref), channel_id=1, source_target_pairs={{0,4},{4,0},{1,5},{5,1},{2,6},{6,2},{3,7},{7,3},{8,12},{12,8},{9,1... | collective-permute-start | bytes 2359304 | tf_op jit(solution)/shard_map/ppermute | solution.py:20
  60.7 20.7 %collective-permute-start.11 = (bf16[256,1536]{1,0:T(8,128)(2,1)S(1)}, bf16[256,1536]{1,0:T(8,128)(2,1)S(1)}, u32[]{:S(2)}, u32[]{:S(2)}) collective-permute-start(bf16[256,1536]{1,0:T(8,128)(2,1)S(1)} %get-tuple-element.111.refs_5_.refs_3_.embed_ref), channel_id=1, source_target_pairs={{0,64},{32,96},{64,0},{96,32},{1,65},{33,97},{65,1},{97,33},{2,66}... | collective-permute-start | bytes 2359304 | tf_op jit(solution)/shard_map/ppermute | solution.py:20
  63.2 20.5 %collective-permute-start.12 = (bf16[256,1536]{1,0:T(8,128)(2,1)S(1)}, bf16[256,1536]{1,0:T(8,128)(2,1)S(1)}, u32[]{:S(2)}, u32[]{:S(2)}) collective-permute-start(bf16[256,1536]{1,0:T(8,128)(2,1)S(1)} %get-tuple-element.110.refs_2_.embed_ref), channel_id=1, source_target_pairs={{0,16},{8,24},{16,0},{24,8},{1,17},{9,25},{17,1},{25,9},{2,18},{10... | collective-permute-start | bytes 2359304 | tf_op jit(solution)/shard_map/ppermute | solution.py:20
  98.9 19.2 %collective-permute-start.17 = (bf16[256,1536]{1,0:T(8,128)(2,1)S(1)}, bf16[256,1536]{1,0:T(8,128)(2,1)S(1)}, u32[]{:S(2)}, u32[]{:S(2)}) collective-permute-start(bf16[256,1536]{1,0:T(8,128)(2,1)S(1)} %add_convert_fusion.2), channel_id=1, source_target_pairs={{0,96},{32,0},{64,32},{96,64},{1,97},{33,1},{65,33},{97,65},{2,98}... | collective-permute-start | bytes 2359304 | tf_op jit(solution)/shard_map/ppermute | solution.py:20
  100.1 20.0 %collective-permute-start.18 = (bf16[256,1536]{1,0:T(8,128)(2,1)S(1)}, bf16[256,1536]{1,0:T(8,128)(2,1)S(1)}, u32[]{:S(2)}, u32[]{:S(2)}) collective-permute-start(bf16[256,1536]{1,0:T(8,128)(2,1)S(1)} %add_convert_fusion.1), channel_id=1, source_target_pairs={{0,32},{32,64},{64,96},{96,0},{1,33},{33,65},{65,97},{97,1},{2,34}... | collective-permute-start | bytes 2359304 | tf_op jit(solution)/shard_map/ppermute | solution.py:20
  100.4 20.0 %collective-permute-start.19 = (bf16[256,1536]{1,0:T(8,128)(2,1)S(1)}, bf16[256,1536]{1,0:T(8,128)(2,1)S(1)}, u32[]{:S(2)}, u32[]{:S(2)}) collective-permute-start(bf16[256,1536]{1,0:T(8,128)(2,1)S(1)} %copy-done.31), channel_id=1, source_target_pairs={{0,16},{8,24},{16,0},{24,8},{1,17},{9,25},{17,1},{25,9},{2,18},{10... | collective-permute-start | bytes 2359304 | tf_op jit(solution)/shard_map/ppermute | solution.py:20
  102.0 19.3 %collective-permute-start.20 = (bf16[256,1536]{1,0:T(8,128)(2,1)S(1)}, bf16[256,1536]{1,0:T(8,128)(2,1)S(1)}, u32[]{:S(2)}, u32[]{:S(2)}) collective-permute-start(bf16[256,1536]{1,0:T(8,128)(2,1)S(1)} %copy-done.30), channel_id=1, source_target_pairs={{0,4},{4,0},{1,5},{5,1},{2,6},{6,2},{3,7},{7,3},{8,12},{12,8},{9,1... | collective-permute-start | bytes 2359304 | tf_op jit(solution)/shard_map/ppermute | solution.py:20
  124.9 51.4 %collective-permute-start = (bf16[512,768]{1,0:T(8,128)(2,1)}, bf16[512,768]{1,0:T(8,128)(2,1)}, u32[]{:S(2)}, u32[]{:S(2)}) collective-permute-start(bf16[512,768]{1,0:T(8,128)(2,1)} %get-tuple-element.212), channel_id=1, source_target_pairs={{0,4},{4,0},{1,5},{5,1},{2,6},{6,2},{3,7},{7,3},{8,12},{12,8},{9,1... | collective-permute-start | bytes 2359304 | tf_op jit(solution)/shard_map/ppermute | solution.py:20
  124.9 19.0 %collective-permute-start.23 = (bf16[256,1536]{1,0:T(8,128)(2,1)}, bf16[256,1536]{1,0:T(8,128)(2,1)S(1)}, u32[]{:S(2)}, u32[]{:S(2)}) collective-permute-start(bf16[256,1536]{1,0:T(8,128)(2,1)} %get-tuple-element.173), channel_id=1, source_target_pairs={{0,24},{8,0},{16,8},{24,16},{1,25},{9,1},{17,9},{25,17},{2,26},{10... | collective-permute-start | bytes 2359304 | tf_op jit(solution)/shard_map/ppermute | solution.py:20
  126.4 19.8 %collective-permute-start.24 = (bf16[256,1536]{1,0:T(8,128)(2,1)}, bf16[256,1536]{1,0:T(8,128)(2,1)S(1)}, u32[]{:S(2)}, u32[]{:S(2)}) collective-permute-start(bf16[256,1536]{1,0:T(8,128)(2,1)} %get-tuple-element.174), channel_id=1, source_target_pairs={{0,8},{8,16},{16,24},{24,0},{1,9},{9,17},{17,25},{25,1},{2,10},{10... | collective-permute-start | bytes 2359304 | tf_op jit(solution)/shard_map/ppermute | solution.py:20
  128.0 19.6 %collective-permute-start.22 = (bf16[256,1536]{1,0:T(8,128)(2,1)S(1)}, bf16[256,1536]{1,0:T(8,128)(2,1)S(1)}, u32[]{:S(2)}, u32[]{:S(2)}) collective-permute-start(bf16[256,1536]{1,0:T(8,128)(2,1)S(1)} %add_convert_fusion), channel_id=1, source_target_pairs={{0,64},{32,96},{64,0},{96,32},{1,65},{33,97},{65,1},{97,33},{2,66}... | collective-permute-start | bytes 2359304 | tf_op jit(solution)/shard_map/ppermute | solution.py:20
  152.3 19.3 %collective-permute-start.27 = (bf16[272,768]{1,0:T(8,128)(2,1)}, bf16[272,768]{1,0:T(8,128)(2,1)S(1)}, u32[]{:S(2)}, u32[]{:S(2)}) collective-permute-start(bf16[272,768]{1,0:T(8,128)(2,1)} %get-tuple-element.186), channel_id=1, source_target_pairs={{0,3},{1,2},{2,1},{3,0},{4,7},{5,6},{6,5},{7,4},{8,11},{9,10},{10,... | collective-permute-start | bytes 1253384 | tf_op jit(solution)/shard_map/ppermute | solution.py:25
  154.2 17.4 %collective-permute-start.26 = (bf16[272,768]{1,0:T(8,128)(2,1)}, bf16[272,768]{1,0:T(8,128)(2,1)S(1)}, u32[]{:S(2)}, u32[]{:S(2)}) collective-permute-start(bf16[272,768]{1,0:T(8,128)(2,1)} %get-tuple-element.185), channel_id=1, source_target_pairs={{0,2},{1,3},{2,0},{3,1},{4,6},{5,7},{6,4},{7,5},{8,10},{9,11},{10,... | collective-permute-start | bytes 1253384 | tf_op jit(solution)/shard_map/ppermute | solution.py:25
  182.7 15.8 %collective-permute-start.30 = (f32[200,768]{1,0:T(8,128)S(1)}, f32[200,768]{1,0:T(8,128)S(1)}, u32[]{:S(2)}, u32[]{:S(2)}) collective-permute-start(f32[200,768]{1,0:T(8,128)S(1)} %get-tuple-element.194), channel_id=1, source_target_pairs={{0,32},{4,12},{8,40},{12,20},{16,48},{20,28},{24,56},{28,4},{32,64... | collective-permute-start | bytes 1843208 | tf_op jit(solution)/shard_map/ppermute | solution.py:413
  184.3 14.5 %collective-permute-start.31 = (f32[200,768]{1,0:T(8,128)S(1)}, f32[200,768]{1,0:T(8,128)S(1)}, u32[]{:S(2)}, u32[]{:S(2)}) collective-permute-start(f32[200,768]{1,0:T(8,128)S(1)} %get-tuple-element.195), channel_id=1, source_target_pairs={{0,96},{4,28},{8,104},{12,4},{16,112},{20,12},{24,120},{28,20},{32... | collective-permute-start | bytes 1843208 | tf_op jit(solution)/shard_map/ppermute | solution.py:413
  201.6 15.4 %collective-permute-start.36 = (f32[192,768]{1,0:T(8,128)S(1)}, f32[192,768]{1,0:T(8,128)S(1)}, u32[]{:S(2)}, u32[]{:S(2)}) collective-permute-start(f32[192,768]{1,0:T(8,128)S(1)} %slice.61), channel_id=1, source_target_pairs={{0,8},{4,36},{8,16},{12,44},{16,24},{20,52},{24,0},{28,60},{32,40}... | collective-permute-start | bytes 1769480 | tf_op jit(solution)/shard_map/ppermute | solution.py:413
  218.8 15.3 %collective-permute-start.39 = (f32[192,768]{1,0:T(8,128)S(1)}, f32[192,768]{1,0:T(8,128)S(1)}, u32[]{:S(2)}, u32[]{:S(2)}) collective-permute-start(f32[192,768]{1,0:T(8,128)S(1)} %add_add_fusion.1.refs_0_), channel_id=1, source_target_pairs={{0,32},{4,12},{8,40},{12,20},{16,48},{20,28},{24,56},{28,4},{32,64... | collective-permute-start | bytes 1769480 | tf_op jit(solution)/shard_map/ppermute | solution.py:413
  220.5 14.0 %collective-permute-start.40 = (f32[192,768]{1,0:T(8,128)S(1)}, f32[192,768]{1,0:T(8,128)}, u32[]{:S(2)}, u32[]{:S(2)}) collective-permute-start(f32[192,768]{1,0:T(8,128)S(1)} %add_add_fusion.1.refs_0_), channel_id=1, source_target_pairs={{0,96},{4,28},{8,104},{12,4},{16,112},{20,12},{24,120},{28,20},{32... | collective-permute-start | bytes 1769480 | tf_op jit(solution)/shard_map/ppermute | solution.py:413
  (53 other events, 484.0 us)

commit v4 on v3

--- a/solution.py
+++ b/solution.py
@@ -325,12 +325,14 @@
         + jnp.where(t == 1, loss_near, 0.0)
     ) / pairs
     row_loss, piece = tied(row_loss, piece)
-    p2, p1, p3, first = tied(*(turned(piece, 0, k) for k in STEPS), shifted(piece, "c", 1))
+    places = [c * half + (lead - k) % 4 * small for k in (0, 1, 3, 2)]
+    others = [(1 - c) * half + (back - k) % 4 * small for k in (0, 1, 3, 2)]
+    first = [piece, shifted(piece, "c", 1)]
+    weight_grad = placed_rows(places[:1] + others[:1], first, None)
+    p2, p1, p3, weight_grad = tied(*(turned(piece, 0, k) for k in STEPS), weight_grad)
     pieces = [piece, p1, p3, p2]
     swapped = [shifted(v, "c", 1) for v in pieces[1:]]
-    places = [c * half + (lead - k) % 4 * small for k in (0, 1, 3, 2)]
-    others = [(1 - c) * half + (back - k) % 4 * small for k in (0, 1, 3, 2)]
-    weight_grad = placed_rows(places + others[:1], pieces + [first], None)
+    weight_grad = placed_rows(places[1:], pieces[1:], weight_grad)
     *swapped, weight_grad = tied(*swapped, weight_grad)
     weight_grad = placed_rows(others[1:], swapped, weight_grad)
     return (row_loss[None], weight_grad[None])
@@ -460,7 +462,7 @@
 def placed_rows(places, pieces, target):
     size, width = pieces[0].shape
     count = len(pieces)
-    operands = in_hbm(pieces)
+    operands = list(pieces)
     specs = [pl.BlockSpec(memory_space=pltpu.VMEM)] * count
     if target is not None:
         operands += in_hbm([target])

time: 250 us -> 249 us (level)
    unnamed x64 -> x56, local copies, waits for them, and re-layouts: 6.28 us -> 7.42 us
    pallas_call x2 -> x3, Pallas kernels: 6.23 us -> 5.12 us  [placed_rows(): pl.pallas_call(functools.partial(place_kernel, count), in_specs=[pl.Block...]
where the time goes in v4:
time: 249 us; the launch traced here: 244 us
  waiting for transfers between devices  113 us (45%)
  starting transfers between devices  56.7 us (23%)
  Pallas kernels  48.2 us (19%)
  local copies, waits for them, and re-layouts  9.76 us (4%)
  other arithmetic  5.07 us (2%)
  blocking collectives  4.76 us (2%)
  matrix products  3.93 us (2%)
  between operations  2.5 us (1%)
    ppermute x28, waiting for transfers between devices, shifted(): lax.ppermute(value, axis, [(i, (i + step) % count) for i in range(count)])  48 us
    ppermute x8, waiting for transfers between devices, crossed(): return lax.ppermute(value, ('m', 't'), [(i, i ^ flip) for i in range(4)])  35 us
    pallas_call x4, Pallas kernels, tile_terms(): pl.pallas_call(body, in_specs=[smem, smem] + [vmem] * len(operands), out_...  34.7 us
    ppermute x28, starting transfers between devices, shifted(): lax.ppermute(value, axis, [(i, (i + step) % count) for i in range(count)])  33.4 us
    ppermute x9, waiting for transfers between devices, turned(): return lax.ppermute(value, ('x', 'y', 'c'), route)  29.8 us
    ppermute x9, starting transfers between devices, turned(): return lax.ppermute(value, ('x', 'y', 'c'), route)  12.7 us
    ppermute x8, starting transfers between devices, crossed(): return lax.ppermute(value, ('m', 't'), [(i, i ^ flip) for i in range(4)])  10.7 us
    unnamed x56, local copies, waits for them, and re-layouts  7.42 us
  transfers between devices with their start and end apart: 45, of which 25 were waited for; matrix products, arithmetic and copies ran while one was open for 2% of the time, Pallas kernels for 18%

profile of v4, /device:TPU:1, one launch (start us, length us, event | category | flops | bytes accessed | tf_op | source)
XLA Modules:
  0.0 243.7 jit_solution(9224664023204629746)
XLA Ops:
  2.3 3.9 %multiply_reduce_fusion = (f32[512]{0:T(512)S(1)}, f32[512,768]{1,0:T(8,128)}) fusion(bf16[1,1536,768]{2,1,0:T(8,128)(2,1)S(1)} %copy-done, bf16[1,512,1536]{2,1,0:T(8,128)(2,1)} %param.4), kind=kOutput, calls=%fused_computation.7 | convolution fusion | flops 1208745472 | bytes 5507072 | tf_op jit(solution)/shard_map/dot_general | solution.py:191
  6.2 4.8 %psum.7 = f32[512]{0:T(512)S(1)} all-reduce(f32[512]{0:T(512)S(1)} %get-tuple-element.223), channel_id=1, replica_groups=mesh['x'=4,'y'=4,'c'=2,'m'=2,'t'=2] {'m'}, use_global_device_ids=true, to_apply=%region_1.0 | all-reduce | flops 512 | bytes 4096 | tf_op jit(solution)/shard_map/psum | solution.py:192
  12.7 3.5 %collective-permute-start.1 = (bf16[256,768]{1,0:T(8,128)(2,1)S(1)}, bf16[256,768]{1,0:T(8,128)(2,1)S(1)}, u32[]{:S(2)}, u32[]{:S(2)}) collective-permute-start(bf16[256,768]{1,0:T(8,128)(2,1)S(1)} %get-tuple-element.217), channel_id=1, source_target_pairs={{0,1},{1,0},{2,3},{3,2},{4,5},{5,4},{6,7},{7,6},{8,9},{9,8},{10,11... | collective-permute-start | bytes 1179656 | tf_op jit(solution)/shard_map/ppermute | solution.py:25
  17.0 6.9 %collective-permute-done.1 = bf16[256,768]{1,0:T(8,128)(2,1)S(1)} collective-permute-done((bf16[256,768]{1,0:T(8,128)(2,1)S(1)}, bf16[256,768]{1,0:T(8,128)(2,1)S(1)}, u32[]{:S(2)}, u32[]{:S(2)}) %collective-permute-start.1) | collective-permute-done | bytes 393248 | tf_op jit(solution)/shard_map/ppermute | solution.py:25
  23.9 8.9 %collective-permute-done.2 = bf16[256,768]{1,0:T(8,128)(2,1)S(1)} collective-permute-done((bf16[256,768]{1,0:T(8,128)(2,1)S(1)}, bf16[256,768]{1,0:T(8,128)(2,1)S(1)}, u32[]{:S(2)}, u32[]{:S(2)}) %collective-permute-start.2) | collective-permute-done | bytes 393248 | tf_op jit(solution)/shard_map/ppermute | solution.py:25
  42.2 11.3 %collective-permute-done.4.refs_3_ = bf16[256,1536]{1,0:T(8,128)(2,1)S(1)} collective-permute-done((bf16[256,1536]{1,0:T(8,128)(2,1)S(1)}, bf16[256,1536]{1,0:T(8,128)(2,1)S(1)}, u32[]{:S(2)}, u32[]{:S(2)}) %collective-permute-start.4) | collective-permute-done | bytes 786464 | tf_op jit(solution)/shard_map/ppermute | solution.py:20
  55.8 2.7 %collective-permute-start.10 = (bf16[256,1536]{1,0:T(8,128)(2,1)S(1)}, bf16[256,1536]{1,0:T(8,128)(2,1)}, u32[]{:S(2)}, u32[]{:S(2)}) collective-permute-start(bf16[256,1536]{1,0:T(8,128)(2,1)S(1)} %collective-permute-done.7.refs_9_.refs_5_), channel_id=1, source_target_pairs={{0,4},{4,0},{1,5},{5,1},{2,6},{6,2},{3,7},{7,3},{8,12},{12,8},{9,1... | collective-permute-start | bytes 2359304 | tf_op jit(solution)/shard_map/ppermute | solution.py:20
  60.7 2.5 %collective-permute-start.11 = (bf16[256,1536]{1,0:T(8,128)(2,1)S(1)}, bf16[256,1536]{1,0:T(8,128)(2,1)S(1)}, u32[]{:S(2)}, u32[]{:S(2)}) collective-permute-start(bf16[256,1536]{1,0:T(8,128)(2,1)S(1)} %get-tuple-element.111.refs_5_.refs_3_.embed_ref), channel_id=1, source_target_pairs={{0,64},{32,96},{64,0},{96,32},{1,65},{33,97},{65,1},{97,33},{2,66}... | collective-permute-start | bytes 2359304 | tf_op jit(solution)/shard_map/ppermute | solution.py:20
  65.0 15.2 %shard_map.59 = (f32[256,1536]{1,0:T(8,128)S(1)}, f32[256,1536]{1,0:T(8,128)S(1)}, f32[256,1536]{1,0:T(8,128)S(1)}, f32[256,1536]{1,0:T(8,128)S(1)}, f32[256,153...) custom-call(s32[1]{0:T(128)} %bitcast.3.refs_0_, ...), custom_call_target="tpu_custom_call" | custom-call | flops 10871635968 | bytes 14155776 | tf_op jit(solution)/shard_map/pallas_call | solution.py:148
  85.0 6.2 %shard_map.60 = (f32[256,1536]{1,0:T(8,128)S(1)}, bf16[256,1536]{1,0:T(8,128)(2,1)}, bf16[256,1536]{1,0:T(8,128)(2,1)}, bf16[256,1536]{1,0:T(8,128)(2,1)}, bf16[...) custom-call(s32[1]{0:T(128)} %bitcast.3.refs_0_, f32[2]{0:T(128)S(1)} %maximum_multiply_fusion.refs_1_, ...), custom_call_target="tpu_custom_call" | custom-call | flops 2415919104 | bytes 7864320 | tf_op jit(solution)/shard_map/pallas_call | solution.py:148
  91.7 5.8 %shard_map.61 = (bf16[256,1536]{1,0:T(8,128)(2,1)}, bf16[256,1536]{1,0:T(8,128)(2,1)}, bf16[256,1536]{1,0:T(8,128)(2,1)}, f32[256,1536]{1,0:T(8,128)S(1)}, f32[2...) custom-call(s32[1]{0:T(128)} %bitcast.3.refs_0_, f32[2]{0:T(128)S(1)} %maximum_multiply_fusion.refs_1_, ...), custom_call_target="tpu_custom_call" | custom-call | flops 2415919104 | bytes 7864320 | tf_op jit(solution)/shard_map/pallas_call | solution.py:148
  103.2 7.5 %shard_map.62 = (bf16[256,1536]{1,0:T(8,128)(2,1)}, bf16[256,1536]{1,0:T(8,128)(2,1)}, bf16[256,1536]{1,0:T(8,128)(2,1)}, bf16[256,1536]{1,0:T(8,128)(2,1)}, bf1...) custom-call(s32[1]{0:T(128)} %bitcast.3.refs_0_, f32[2]{0:T(128)S(1)} %maximum_multiply_fusion.refs_1_, ...), custom_call_target="tpu_custom_call" | custom-call | flops 3623878656 | bytes 7864320 | tf_op jit(solution)/shard_map/pallas_call | solution.py:148
  110.7 7.4 %collective-permute-done.17.refs_2_ = bf16[256,1536]{1,0:T(8,128)(2,1)S(1)} collective-permute-done((bf16[256,1536]{1,0:T(8,128)(2,1)S(1)}, bf16[256,1536]{1,0:T(8,128)(2,1)S(1)}, u32[]{:S(2)}, u32[]{:S(2)}) %collective-permute-start.17) | collective-permute-done | bytes 786464 | tf_op jit(solution)/shard_map/ppermute | solution.py:20
  129.3 14.6 %collective-permute-done.23.refs_1_ = bf16[256,1536]{1,0:T(8,128)(2,1)S(1)} collective-permute-done((bf16[256,1536]{1,0:T(8,128)(2,1)}, bf16[256,1536]{1,0:T(8,128)(2,1)S(1)}, u32[]{:S(2)}, u32[]{:S(2)}) %collective-permute-start.23) | collective-permute-done | bytes 786464 | tf_op jit(solution)/shard_map/ppermute | solution.py:20
  149.3 3.0 %collective-permute-start.25 = (bf16[272,768]{1,0:T(8,128)(2,1)}, bf16[272,768]{1,0:T(8,128)(2,1)S(1)}, u32[]{:S(2)}, u32[]{:S(2)}) collective-permute-start(bf16[272,768]{1,0:T(8,128)(2,1)} %get-tuple-element.184), channel_id=1, source_target_pairs={{0,1},{1,0},{2,3},{3,2},{4,5},{5,4},{6,7},{7,6},{8,9},{9,8},{10,11... | collective-permute-start | bytes 1253384 | tf_op jit(solution)/shard_map/ppermute | solution.py:25
  154.7 2.6 %collective-permute-start.16 = (f32[2,4,256]{2,1,0:T(4,128)S(1)}, f32[2,4,256]{2,1,0:T(4,128)S(1)}, u32[]{:S(2)}, u32[]{:S(2)}) collective-permute-start(f32[2,4,256]{2,1,0:T(4,128)S(1)} %fusion.3), channel_id=1, source_target_pairs={{0,4},{4,0},{1,5},{5,1},{2,6},{6,2},{3,7},{7,3},{8,12},{12,8},{9,1... | collective-permute-start | bytes 24584 | tf_op jit(solution)/shard_map/ppermute | solution.py:20
  160.4 11.2 %collective-permute-done.27.p11 = bf16[272,768]{1,0:T(8,128)(2,1)S(1)} collective-permute-done((bf16[272,768]{1,0:T(8,128)(2,1)}, bf16[272,768]{1,0:T(8,128)(2,1)S(1)}, u32[]{:S(2)}, u32[]{:S(2)}) %collective-permute-start.27) | collective-permute-done | bytes 417824 | tf_op jit(solution)/shard_map/ppermute | solution.py:25
  172.5 2.5 %shard_map.65.own_grad = bf16[512,768]{1,0:T(8,128)(2,1)S(1)} custom-call(s32[2]{0:T(128)S(1)} %pad_add_fusion.flags_ref, f32[1]{0:T(128)S(6)} %div.9.scale_ref, bf16[272,768]{1,0:T(8,128)(2,1)} %get-tuple-element.178.p00, bf16[272,768]{1,0:T(8,128)(2,1)} %copy-done.20, bf16[272,768]{1,0:T(8,128)(2,1)} %copy-done.22, bf16[272,768]{1,0:T(8,128)(2,1)} %copy-done.21, ...), custom_call_target="tpu_custom_call" | custom-call | flops 2359296 | bytes 4718592 | tf_op jit(solution)/shard_map/pallas_call | solution.py:170
  178.2 2.7 %shard_map.66 = (f32[200,768]{1,0:T(8,128)S(1)}, f32[200,768]{1,0:T(8,128)S(1)}, f32[200,768]{1,0:T(8,128)S(1)}, f32[200,768]{1,0:T(8,128)S(1)}) custom-call(s32[1]{0:T(128)} %bitcast.lead_ref, bf16[512,768]{1,0:T(8,128)(2,1)S(1)} %copy-done.9, bf16[512,768]{1,0:T(8,128)(2,1)} %collective-permute-done.others, bf16[512,768]{1,0:T(8,128)(2,1)S(1)} %shard_map.65.own_grad, ...), custom_call_target="tpu_custom_call" | custom-call | flops 1207959552 | bytes 3145728 | tf_op jit(solution)/shard_map/pallas_call | solution.py:437
  185.4 6.6 %collective-permute-done.29 = f32[200,768]{1,0:T(8,128)S(1)} collective-permute-done((f32[200,768]{1,0:T(8,128)S(1)}, f32[200,768]{1,0:T(8,128)S(1)}, u32[]{:S(2)}, u32[]{:S(2)}) %collective-permute-start.29) | collective-permute-done | bytes 614432 | tf_op jit(solution)/shard_map/ppermute | solution.py:415
  192.0 6.5 %collective-permute-done.30 = f32[200,768]{1,0:T(8,128)S(1)} collective-permute-done((f32[200,768]{1,0:T(8,128)S(1)}, f32[200,768]{1,0:T(8,128)S(1)}, u32[]{:S(2)}, u32[]{:S(2)}) %collective-permute-start.30) | collective-permute-done | bytes 614432 | tf_op jit(solution)/shard_map/ppermute | solution.py:415
  211.9 5.2 %collective-permute-done.36 = f32[192,768]{1,0:T(8,128)S(1)} collective-permute-done((f32[192,768]{1,0:T(8,128)S(1)}, f32[192,768]{1,0:T(8,128)S(1)}, u32[]{:S(2)}, u32[]{:S(2)}) %collective-permute-start.36) | collective-permute-done | bytes 589856 | tf_op jit(solution)/shard_map/ppermute | solution.py:415
  224.1 4.9 %collective-permute-done.38.refs_2_ = f32[192,768]{1,0:T(8,128)S(1)} collective-permute-done((f32[192,768]{1,0:T(8,128)S(1)}, f32[192,768]{1,0:T(8,128)S(1)}, u32[]{:S(2)}, u32[]{:S(2)}) %collective-permute-start.38) | collective-permute-done | bytes 589856 | tf_op jit(solution)/shard_map/ppermute | solution.py:415
  229.0 6.3 %collective-permute-done.39.refs_0_ = f32[192,768]{1,0:T(8,128)S(1)} collective-permute-done((f32[192,768]{1,0:T(8,128)S(1)}, f32[192,768]{1,0:T(8,128)S(1)}, u32[]{:S(2)}, u32[]{:S(2)}) %collective-permute-start.39) | collective-permute-done | bytes 589856 | tf_op jit(solution)/shard_map/ppermute | solution.py:415
  (168 shorter events, 88.4 us)
Async XLA Ops:
  16.2 16.6 %collective-permute-start.2 = (bf16[256,768]{1,0:T(8,128)(2,1)S(1)}, bf16[256,768]{1,0:T(8,128)(2,1)S(1)}, u32[]{:S(2)}, u32[]{:S(2)}) collective-permute-start(bf16[256,768]{1,0:T(8,128)(2,1)S(1)} %get-tuple-element.216), channel_id=1, source_target_pairs={{0,2},{1,3},{2,0},{3,1},{4,6},{5,7},{6,4},{7,5},{8,10},{9,11},{10,... | collective-permute-start | bytes 1179656 | tf_op jit(solution)/shard_map/ppermute | solution.py:25
  17.0 17.3 %collective-permute-start.3 = (bf16[256,768]{1,0:T(8,128)(2,1)S(1)}, bf16[256,768]{1,0:T(8,128)(2,1)S(1)}, u32[]{:S(2)}, u32[]{:S(2)}) collective-permute-start(bf16[256,768]{1,0:T(8,128)(2,1)S(1)} %get-tuple-element.215), channel_id=1, source_target_pairs={{0,3},{1,2},{2,1},{3,0},{4,7},{5,6},{6,5},{7,4},{8,11},{9,10},{10,... | collective-permute-start | bytes 1179656 | tf_op jit(solution)/shard_map/ppermute | solution.py:25
  34.4 19.2 %collective-permute-start.4 = (bf16[256,1536]{1,0:T(8,128)(2,1)S(1)}, bf16[256,1536]{1,0:T(8,128)(2,1)S(1)}, u32[]{:S(2)}, u32[]{:S(2)}) collective-permute-start(bf16[256,1536]{1,0:T(8,128)(2,1)S(1)} %get-tuple-element.110.refs_2_.embed_ref), channel_id=1, source_target_pairs={{0,8},{8,16},{16,24},{24,0},{1,9},{9,17},{17,25},{25,1},{2,10},{10... | collective-permute-start | bytes 2359304 | tf_op jit(solution)/shard_map/ppermute | solution.py:20
  35.7 17.8 %collective-permute-start.5 = (bf16[256,1536]{1,0:T(8,128)(2,1)S(1)}, bf16[256,1536]{1,0:T(8,128)(2,1)S(1)}, u32[]{:S(2)}, u32[]{:S(2)}) collective-permute-start(bf16[256,1536]{1,0:T(8,128)(2,1)S(1)} %get-tuple-element.110.refs_2_.embed_ref), channel_id=1, source_target_pairs={{0,24},{8,0},{16,8},{24,16},{1,25},{9,1},{17,9},{25,17},{2,26},{10... | collective-permute-start | bytes 2359304 | tf_op jit(solution)/shard_map/ppermute | solution.py:20
  37.2 18.5 %collective-permute-start.6 = (bf16[256,1536]{1,0:T(8,128)(2,1)S(1)}, bf16[256,1536]{1,0:T(8,128)(2,1)S(1)}, u32[]{:S(2)}, u32[]{:S(2)}) collective-permute-start(bf16[256,1536]{1,0:T(8,128)(2,1)S(1)} %get-tuple-element.111.refs_5_.refs_3_.embed_ref), channel_id=1, source_target_pairs={{0,32},{32,64},{64,96},{96,0},{1,33},{33,65},{65,97},{97,1},{2,34}... | collective-permute-start | bytes 2359304 | tf_op jit(solution)/shard_map/ppermute | solution.py:20
  38.4 17.3 %collective-permute-start.7 = (bf16[256,1536]{1,0:T(8,128)(2,1)S(1)}, bf16[256,1536]{1,0:T(8,128)(2,1)S(1)}, u32[]{:S(2)}, u32[]{:S(2)}) collective-permute-start(bf16[256,1536]{1,0:T(8,128)(2,1)S(1)} %get-tuple-element.111.refs_5_.refs_3_.embed_ref), channel_id=1, source_target_pairs={{0,96},{32,0},{64,32},{96,64},{1,97},{33,1},{65,33},{97,65},{2,98}... | collective-permute-start | bytes 2359304 | tf_op jit(solution)/shard_map/ppermute | solution.py:20
  39.9 15.9 %collective-permute-start.8 = (bf16[256,1536]{1,0:T(8,128)(2,1)S(1)}, bf16[256,1536]{1,0:T(8,128)(2,1)S(1)}, u32[]{:S(2)}, u32[]{:S(2)}) collective-permute-start(bf16[256,1536]{1,0:T(8,128)(2,1)S(1)} %get-tuple-element.111.refs_5_.refs_3_.embed_ref), channel_id=1, source_target_pairs={{0,4},{4,0},{1,5},{5,1},{2,6},{6,2},{3,7},{7,3},{8,12},{12,8},{9,1... | collective-permute-start | bytes 2359304 | tf_op jit(solution)/shard_map/ppermute | solution.py:20
  60.7 20.7 %collective-permute-start.11 = (bf16[256,1536]{1,0:T(8,128)(2,1)S(1)}, bf16[256,1536]{1,0:T(8,128)(2,1)S(1)}, u32[]{:S(2)}, u32[]{:S(2)}) collective-permute-start(bf16[256,1536]{1,0:T(8,128)(2,1)S(1)} %get-tuple-element.111.refs_5_.refs_3_.embed_ref), channel_id=1, source_target_pairs={{0,64},{32,96},{64,0},{96,32},{1,65},{33,97},{65,1},{97,33},{2,66}... | collective-permute-start | bytes 2359304 | tf_op jit(solution)/shard_map/ppermute | solution.py:20
  63.2 20.5 %collective-permute-start.12 = (bf16[256,1536]{1,0:T(8,128)(2,1)S(1)}, bf16[256,1536]{1,0:T(8,128)(2,1)S(1)}, u32[]{:S(2)}, u32[]{:S(2)}) collective-permute-start(bf16[256,1536]{1,0:T(8,128)(2,1)S(1)} %get-tuple-element.110.refs_2_.embed_ref), channel_id=1, source_target_pairs={{0,16},{8,24},{16,0},{24,8},{1,17},{9,25},{17,1},{25,9},{2,18},{10... | collective-permute-start | bytes 2359304 | tf_op jit(solution)/shard_map/ppermute | solution.py:20
  98.9 19.2 %collective-permute-start.17 = (bf16[256,1536]{1,0:T(8,128)(2,1)S(1)}, bf16[256,1536]{1,0:T(8,128)(2,1)S(1)}, u32[]{:S(2)}, u32[]{:S(2)}) collective-permute-start(bf16[256,1536]{1,0:T(8,128)(2,1)S(1)} %add_convert_fusion.2), channel_id=1, source_target_pairs={{0,96},{32,0},{64,32},{96,64},{1,97},{33,1},{65,33},{97,65},{2,98}... | collective-permute-start | bytes 2359304 | tf_op jit(solution)/shard_map/ppermute | solution.py:20
  100.1 20.0 %collective-permute-start.18 = (bf16[256,1536]{1,0:T(8,128)(2,1)S(1)}, bf16[256,1536]{1,0:T(8,128)(2,1)S(1)}, u32[]{:S(2)}, u32[]{:S(2)}) collective-permute-start(bf16[256,1536]{1,0:T(8,128)(2,1)S(1)} %add_convert_fusion.1), channel_id=1, source_target_pairs={{0,32},{32,64},{64,96},{96,0},{1,33},{33,65},{65,97},{97,1},{2,34}... | collective-permute-start | bytes 2359304 | tf_op jit(solution)/shard_map/ppermute | solution.py:20
  100.4 20.0 %collective-permute-start.19 = (bf16[256,1536]{1,0:T(8,128)(2,1)S(1)}, bf16[256,1536]{1,0:T(8,128)(2,1)S(1)}, u32[]{:S(2)}, u32[]{:S(2)}) collective-permute-start(bf16[256,1536]{1,0:T(8,128)(2,1)S(1)} %copy-done.27), channel_id=1, source_target_pairs={{0,16},{8,24},{16,0},{24,8},{1,17},{9,25},{17,1},{25,9},{2,18},{10... | collective-permute-start | bytes 2359304 | tf_op jit(solution)/shard_map/ppermute | solution.py:20
  102.0 19.3 %collective-permute-start.20 = (bf16[256,1536]{1,0:T(8,128)(2,1)S(1)}, bf16[256,1536]{1,0:T(8,128)(2,1)S(1)}, u32[]{:S(2)}, u32[]{:S(2)}) collective-permute-start(bf16[256,1536]{1,0:T(8,128)(2,1)S(1)} %copy-done.26), channel_id=1, source_target_pairs={{0,4},{4,0},{1,5},{5,1},{2,6},{6,2},{3,7},{7,3},{8,12},{12,8},{9,1... | collective-permute-start | bytes 2359304 | tf_op jit(solution)/shard_map/ppermute | solution.py:20
  125.0 51.4 %collective-permute-start = (bf16[512,768]{1,0:T(8,128)(2,1)}, bf16[512,768]{1,0:T(8,128)(2,1)}, u32[]{:S(2)}, u32[]{:S(2)}) collective-permute-start(bf16[512,768]{1,0:T(8,128)(2,1)} %get-tuple-element.212), channel_id=1, source_target_pairs={{0,4},{4,0},{1,5},{5,1},{2,6},{6,2},{3,7},{7,3},{8,12},{12,8},{9,1... | collective-permute-start | bytes 2359304 | tf_op jit(solution)/shard_map/ppermute | solution.py:20
  125.0 19.0 %collective-permute-start.23 = (bf16[256,1536]{1,0:T(8,128)(2,1)}, bf16[256,1536]{1,0:T(8,128)(2,1)S(1)}, u32[]{:S(2)}, u32[]{:S(2)}) collective-permute-start(bf16[256,1536]{1,0:T(8,128)(2,1)} %get-tuple-element.173), channel_id=1, source_target_pairs={{0,24},{8,0},{16,8},{24,16},{1,25},{9,1},{17,9},{25,17},{2,26},{10... | collective-permute-start | bytes 2359304 | tf_op jit(solution)/shard_map/ppermute | solution.py:20
  126.4 19.8 %collective-permute-start.24 = (bf16[256,1536]{1,0:T(8,128)(2,1)}, bf16[256,1536]{1,0:T(8,128)(2,1)S(1)}, u32[]{:S(2)}, u32[]{:S(2)}) collective-permute-start(bf16[256,1536]{1,0:T(8,128)(2,1)} %get-tuple-element.174), channel_id=1, source_target_pairs={{0,8},{8,16},{16,24},{24,0},{1,9},{9,17},{17,25},{25,1},{2,10},{10... | collective-permute-start | bytes 2359304 | tf_op jit(solution)/shard_map/ppermute | solution.py:20
  128.1 19.6 %collective-permute-start.22 = (bf16[256,1536]{1,0:T(8,128)(2,1)S(1)}, bf16[256,1536]{1,0:T(8,128)(2,1)S(1)}, u32[]{:S(2)}, u32[]{:S(2)}) collective-permute-start(bf16[256,1536]{1,0:T(8,128)(2,1)S(1)} %add_convert_fusion), channel_id=1, source_target_pairs={{0,64},{32,96},{64,0},{96,32},{1,65},{33,97},{65,1},{97,33},{2,66}... | collective-permute-start | bytes 2359304 | tf_op jit(solution)/shard_map/ppermute | solution.py:20
  152.4 19.3 %collective-permute-start.27 = (bf16[272,768]{1,0:T(8,128)(2,1)}, bf16[272,768]{1,0:T(8,128)(2,1)S(1)}, u32[]{:S(2)}, u32[]{:S(2)}) collective-permute-start(bf16[272,768]{1,0:T(8,128)(2,1)} %get-tuple-element.186), channel_id=1, source_target_pairs={{0,3},{1,2},{2,1},{3,0},{4,7},{5,6},{6,5},{7,4},{8,11},{9,10},{10,... | collective-permute-start | bytes 1253384 | tf_op jit(solution)/shard_map/ppermute | solution.py:25
  154.3 17.4 %collective-permute-start.26 = (bf16[272,768]{1,0:T(8,128)(2,1)}, bf16[272,768]{1,0:T(8,128)(2,1)S(1)}, u32[]{:S(2)}, u32[]{:S(2)}) collective-permute-start(bf16[272,768]{1,0:T(8,128)(2,1)} %get-tuple-element.185), channel_id=1, source_target_pairs={{0,2},{1,3},{2,0},{3,1},{4,6},{5,7},{6,4},{7,5},{8,10},{9,11},{10,... | collective-permute-start | bytes 1253384 | tf_op jit(solution)/shard_map/ppermute | solution.py:25
  182.7 15.8 %collective-permute-start.30 = (f32[200,768]{1,0:T(8,128)S(1)}, f32[200,768]{1,0:T(8,128)S(1)}, u32[]{:S(2)}, u32[]{:S(2)}) collective-permute-start(f32[200,768]{1,0:T(8,128)S(1)} %get-tuple-element.194), channel_id=1, source_target_pairs={{0,32},{4,12},{8,40},{12,20},{16,48},{20,28},{24,56},{28,4},{32,64... | collective-permute-start | bytes 1843208 | tf_op jit(solution)/shard_map/ppermute | solution.py:415
  184.3 14.5 %collective-permute-start.31 = (f32[200,768]{1,0:T(8,128)S(1)}, f32[200,768]{1,0:T(8,128)S(1)}, u32[]{:S(2)}, u32[]{:S(2)}) collective-permute-start(f32[200,768]{1,0:T(8,128)S(1)} %get-tuple-element.195), channel_id=1, source_target_pairs={{0,96},{4,28},{8,104},{12,4},{16,112},{20,12},{24,120},{28,20},{32... | collective-permute-start | bytes 1843208 | tf_op jit(solution)/shard_map/ppermute | solution.py:415
  201.7 15.4 %collective-permute-start.36 = (f32[192,768]{1,0:T(8,128)S(1)}, f32[192,768]{1,0:T(8,128)S(1)}, u32[]{:S(2)}, u32[]{:S(2)}) collective-permute-start(f32[192,768]{1,0:T(8,128)S(1)} %slice.61), channel_id=1, source_target_pairs={{0,8},{4,36},{8,16},{12,44},{16,24},{20,52},{24,0},{28,60},{32,40}... | collective-permute-start | bytes 1769480 | tf_op jit(solution)/shard_map/ppermute | solution.py:415
  203.2 13.9 %collective-permute-start.37 = (f32[192,768]{1,0:T(8,128)S(1)}, f32[192,768]{1,0:T(8,128)S(1)}, u32[]{:S(2)}, u32[]{:S(2)}) collective-permute-start(f32[192,768]{1,0:T(8,128)S(1)} %slice.61), channel_id=1, source_target_pairs={{0,24},{4,100},{8,0},{12,108},{16,8},{20,116},{24,16},{28,124},{32... | collective-permute-start | bytes 1769480 | tf_op jit(solution)/shard_map/ppermute | solution.py:415
  219.8 15.5 %collective-permute-start.39 = (f32[192,768]{1,0:T(8,128)S(1)}, f32[192,768]{1,0:T(8,128)S(1)}, u32[]{:S(2)}, u32[]{:S(2)}) collective-permute-start(f32[192,768]{1,0:T(8,128)S(1)} %add_add_fusion.1.refs_0_), channel_id=1, source_target_pairs={{0,32},{4,12},{8,40},{12,20},{16,48},{20,28},{24,56},{28,4},{32,64... | collective-permute-start | bytes 1769480 | tf_op jit(solution)/shard_map/ppermute | solution.py:415
  (49 other events, 435.9 us)

commit v5 on v4

--- a/solution.py
+++ b/solution.py
@@ -206,13 +206,13 @@
     other = jnp.concatenate([far, cross], axis=1)
     own, other = tied(own, other)
 
-    r1, r3, c1, c3, d0 = tied(
+    r1, r3, c1, c3 = tied(
         shifted(own, "y", 1),
         shifted(own, "y", 3),
         shifted(other, "x", 1),
         shifted(other, "x", 3),
-        shifted(other, "c", 1),
-    )
+    )
+    d0 = shifted(other, "c", 1)
     c2, r2 = shifted(other, "x", 2), shifted(own, "y", 2)
     d1, d3 = shifted(c1, "c", 1), shifted(c3, "c", 1)
     diag = jnp.where(m == t, 0, 2 * part).astype(jnp.int32).reshape(1)

time: 249 us -> 248 us (level)
    unnamed x56 -> x54, local copies, waits for them, and re-layouts: 7.42 us -> 7.42 us
where the time goes in v5:
time: 248 us; the launch traced here: 243 us
  waiting for transfers between devices  112 us (45%)
  starting transfers between devices  56.4 us (23%)
  Pallas kernels  48.2 us (19%)
  local copies, waits for them, and re-layouts  9.73 us (4%)
  other arithmetic  5.07 us (2%)
  blocking collectives  4.76 us (2%)
  matrix products  3.93 us (2%)
  between operations  2.5 us (1%)
    ppermute x28, waiting for transfers between devices, shifted(): lax.ppermute(value, axis, [(i, (i + step) % count) for i in range(count)])  47.5 us
    ppermute x8, waiting for transfers between devices, crossed(): return lax.ppermute(value, ('m', 't'), [(i, i ^ flip) for i in range(4)])  35 us
    pallas_call x4, Pallas kernels, tile_terms(): pl.pallas_call(body, in_specs=[smem, smem] + [vmem] * len(operands), out_...  34.7 us
    ppermute x28, starting transfers between devices, shifted(): lax.ppermute(value, axis, [(i, (i + step) % count) for i in range(count)])  33 us
    ppermute x9, waiting for transfers between devices, turned(): return lax.ppermute(value, ('x', 'y', 'c'), route)  29.8 us
    ppermute x9, starting transfers between devices, turned(): return lax.ppermute(value, ('x', 'y', 'c'), route)  12.7 us
    ppermute x8, starting transfers between devices, crossed(): return lax.ppermute(value, ('m', 't'), [(i, i ^ flip) for i in range(4)])  10.7 us
    unnamed x54, local copies, waits for them, and re-layouts  7.42 us
  transfers between devices with their start and end apart: 45, of which 25 were waited for; matrix products, arithmetic and copies ran while one was open for 2% of the time, Pallas kernels for 18%

profile of v5, /device:TPU:1, one launch (start us, length us, event | category | flops | bytes accessed | tf_op | source)
XLA Modules:
  0.0 242.8 jit_solution(16962519260746376909)
XLA Ops:
  2.3 3.9 %multiply_reduce_fusion = (f32[512]{0:T(512)S(1)}, f32[512,768]{1,0:T(8,128)}) fusion(bf16[1,1536,768]{2,1,0:T(8,128)(2,1)S(1)} %copy-done, bf16[1,512,1536]{2,1,0:T(8,128)(2,1)} %param.4), kind=kOutput, calls=%fused_computation.7 | convolution fusion | flops 1208745472 | bytes 5507072 | tf_op jit(solution)/shard_map/dot_general | solution.py:191
  6.2 4.8 %psum.7 = f32[512]{0:T(512)S(1)} all-reduce(f32[512]{0:T(512)S(1)} %get-tuple-element.221), channel_id=1, replica_groups=mesh['x'=4,'y'=4,'c'=2,'m'=2,'t'=2] {'m'}, use_global_device_ids=true, to_apply=%region_1.0 | all-reduce | flops 512 | bytes 4096 | tf_op jit(solution)/shard_map/psum | solution.py:192
  12.7 3.5 %collective-permute-start.1 = (bf16[256,768]{1,0:T(8,128)(2,1)S(1)}, bf16[256,768]{1,0:T(8,128)(2,1)S(1)}, u32[]{:S(2)}, u32[]{:S(2)}) collective-permute-start(bf16[256,768]{1,0:T(8,128)(2,1)S(1)} %get-tuple-element.215), channel_id=1, source_target_pairs={{0,1},{1,0},{2,3},{3,2},{4,5},{5,4},{6,7},{7,6},{8,9},{9,8},{10,11... | collective-permute-start | bytes 1179656 | tf_op jit(solution)/shard_map/ppermute | solution.py:25
  17.0 6.9 %collective-permute-done.1 = bf16[256,768]{1,0:T(8,128)(2,1)S(1)} collective-permute-done((bf16[256,768]{1,0:T(8,128)(2,1)S(1)}, bf16[256,768]{1,0:T(8,128)(2,1)S(1)}, u32[]{:S(2)}, u32[]{:S(2)}) %collective-permute-start.1) | collective-permute-done | bytes 393248 | tf_op jit(solution)/shard_map/ppermute | solution.py:25
  23.9 8.9 %collective-permute-done.2 = bf16[256,768]{1,0:T(8,128)(2,1)S(1)} collective-permute-done((bf16[256,768]{1,0:T(8,128)(2,1)S(1)}, bf16[256,768]{1,0:T(8,128)(2,1)S(1)}, u32[]{:S(2)}, u32[]{:S(2)}) %collective-permute-start.2) | collective-permute-done | bytes 393248 | tf_op jit(solution)/shard_map/ppermute | solution.py:25
  42.2 11.3 %collective-permute-done.4.refs_3_ = bf16[256,1536]{1,0:T(8,128)(2,1)S(1)} collective-permute-done((bf16[256,1536]{1,0:T(8,128)(2,1)S(1)}, bf16[256,1536]{1,0:T(8,128)(2,1)S(1)}, u32[]{:S(2)}, u32[]{:S(2)}) %collective-permute-start.4) | collective-permute-done | bytes 786464 | tf_op jit(solution)/shard_map/ppermute | solution.py:20
  55.8 2.7 %collective-permute-start.10 = (bf16[256,1536]{1,0:T(8,128)(2,1)S(1)}, bf16[256,1536]{1,0:T(8,128)(2,1)}, u32[]{:S(2)}, u32[]{:S(2)}) collective-permute-start(bf16[256,1536]{1,0:T(8,128)(2,1)S(1)} %collective-permute-done.7.refs_9_.refs_5_), channel_id=1, source_target_pairs={{0,4},{4,0},{1,5},{5,1},{2,6},{6,2},{3,7},{7,3},{8,12},{12,8},{9,1... | collective-permute-start | bytes 2359304 | tf_op jit(solution)/shard_map/ppermute | solution.py:20
  60.0 2.4 collective-permute-start.11
  64.1 15.2 %shard_map.59 = (f32[256,1536]{1,0:T(8,128)S(1)}, f32[256,1536]{1,0:T(8,128)S(1)}, f32[256,1536]{1,0:T(8,128)S(1)}, f32[256,1536]{1,0:T(8,128)S(1)}, f32[256,153...) custom-call(s32[1]{0:T(128)} %bitcast.3.refs_0_, ...), custom_call_target="tpu_custom_call" | custom-call | flops 10871635968 | bytes 14155776 | tf_op jit(solution)/shard_map/pallas_call | solution.py:148
  84.2 6.2 %shard_map.60 = (f32[256,1536]{1,0:T(8,128)S(1)}, bf16[256,1536]{1,0:T(8,128)(2,1)}, bf16[256,1536]{1,0:T(8,128)(2,1)}, bf16[256,1536]{1,0:T(8,128)(2,1)}, bf16[...) custom-call(s32[1]{0:T(128)} %bitcast.3.refs_0_, f32[2]{0:T(128)S(1)} %maximum_multiply_fusion.refs_1_, ...), custom_call_target="tpu_custom_call" | custom-call | flops 2415919104 | bytes 7864320 | tf_op jit(solution)/shard_map/pallas_call | solution.py:148
  90.9 5.8 %shard_map.61 = (bf16[256,1536]{1,0:T(8,128)(2,1)}, bf16[256,1536]{1,0:T(8,128)(2,1)}, bf16[256,1536]{1,0:T(8,128)(2,1)}, f32[256,1536]{1,0:T(8,128)S(1)}, f32[2...) custom-call(s32[1]{0:T(128)} %bitcast.3.refs_0_, f32[2]{0:T(128)S(1)} %maximum_multiply_fusion.refs_1_, ...), custom_call_target="tpu_custom_call" | custom-call | flops 2415919104 | bytes 7864320 | tf_op jit(solution)/shard_map/pallas_call | solution.py:148
  102.4 7.5 %shard_map.62 = (bf16[256,1536]{1,0:T(8,128)(2,1)}, bf16[256,1536]{1,0:T(8,128)(2,1)}, bf16[256,1536]{1,0:T(8,128)(2,1)}, bf16[256,1536]{1,0:T(8,128)(2,1)}, bf1...) custom-call(s32[1]{0:T(128)} %bitcast.3.refs_0_, f32[2]{0:T(128)S(1)} %maximum_multiply_fusion.refs_1_, ...), custom_call_target="tpu_custom_call" | custom-call | flops 3623878656 | bytes 7864320 | tf_op jit(solution)/shard_map/pallas_call | solution.py:148
  109.9 7.4 %collective-permute-done.17.refs_2_ = bf16[256,1536]{1,0:T(8,128)(2,1)S(1)} collective-permute-done((bf16[256,1536]{1,0:T(8,128)(2,1)S(1)}, bf16[256,1536]{1,0:T(8,128)(2,1)S(1)}, u32[]{:S(2)}, u32[]{:S(2)}) %collective-permute-start.17) | collective-permute-done | bytes 786464 | tf_op jit(solution)/shard_map/ppermute | solution.py:20
  128.5 14.6 %collective-permute-done.23.refs_1_ = bf16[256,1536]{1,0:T(8,128)(2,1)S(1)} collective-permute-done((bf16[256,1536]{1,0:T(8,128)(2,1)}, bf16[256,1536]{1,0:T(8,128)(2,1)S(1)}, u32[]{:S(2)}, u32[]{:S(2)}) %collective-permute-start.23) | collective-permute-done | bytes 786464 | tf_op jit(solution)/shard_map/ppermute | solution.py:20
  148.5 3.0 %collective-permute-start.25 = (bf16[272,768]{1,0:T(8,128)(2,1)}, bf16[272,768]{1,0:T(8,128)(2,1)S(1)}, u32[]{:S(2)}, u32[]{:S(2)}) collective-permute-start(bf16[272,768]{1,0:T(8,128)(2,1)} %get-tuple-element.182), channel_id=1, source_target_pairs={{0,1},{1,0},{2,3},{3,2},{4,5},{5,4},{6,7},{7,6},{8,9},{9,8},{10,11... | collective-permute-start | bytes 1253384 | tf_op jit(solution)/shard_map/ppermute | solution.py:25
  153.8 2.6 %collective-permute-start.16 = (f32[2,4,256]{2,1,0:T(4,128)S(1)}, f32[2,4,256]{2,1,0:T(4,128)S(1)}, u32[]{:S(2)}, u32[]{:S(2)}) collective-permute-start(f32[2,4,256]{2,1,0:T(4,128)S(1)} %fusion.3), channel_id=1, source_target_pairs={{0,4},{4,0},{1,5},{5,1},{2,6},{6,2},{3,7},{7,3},{8,12},{12,8},{9,1... | collective-permute-start | bytes 24584 | tf_op jit(solution)/shard_map/ppermute | solution.py:20
  159.6 11.2 %collective-permute-done.27.p11 = bf16[272,768]{1,0:T(8,128)(2,1)S(1)} collective-permute-done((bf16[272,768]{1,0:T(8,128)(2,1)}, bf16[272,768]{1,0:T(8,128)(2,1)S(1)}, u32[]{:S(2)}, u32[]{:S(2)}) %collective-permute-start.27) | collective-permute-done | bytes 417824 | tf_op jit(solution)/shard_map/ppermute | solution.py:25
  171.7 2.5 %shard_map.65.own_grad = bf16[512,768]{1,0:T(8,128)(2,1)S(1)} custom-call(s32[2]{0:T(128)S(1)} %pad_add_fusion.flags_ref, f32[1]{0:T(128)S(6)} %div.9.scale_ref, bf16[272,768]{1,0:T(8,128)(2,1)} %get-tuple-element.176.p00, bf16[272,768]{1,0:T(8,128)(2,1)} %copy-done.20, bf16[272,768]{1,0:T(8,128)(2,1)} %copy-done.22, bf16[272,768]{1,0:T(8,128)(2,1)} %copy-done.21, ...), custom_call_target="tpu_custom_call" | custom-call | flops 2359296 | bytes 4718592 | tf_op jit(solution)/shard_map/pallas_call | solution.py:170
  177.3 2.7 %shard_map.66 = (f32[200,768]{1,0:T(8,128)S(1)}, f32[200,768]{1,0:T(8,128)S(1)}, f32[200,768]{1,0:T(8,128)S(1)}, f32[200,768]{1,0:T(8,128)S(1)}) custom-call(s32[1]{0:T(128)} %bitcast.lead_ref, bf16[512,768]{1,0:T(8,128)(2,1)S(1)} %copy-done.9, bf16[512,768]{1,0:T(8,128)(2,1)} %collective-permute-done.others, bf16[512,768]{1,0:T(8,128)(2,1)S(1)} %shard_map.65.own_grad, ...), custom_call_target="tpu_custom_call" | custom-call | flops 1207959552 | bytes 3145728 | tf_op jit(solution)/shard_map/pallas_call | solution.py:437
  184.5 6.6 %collective-permute-done.29 = f32[200,768]{1,0:T(8,128)S(1)} collective-permute-done((f32[200,768]{1,0:T(8,128)S(1)}, f32[200,768]{1,0:T(8,128)S(1)}, u32[]{:S(2)}, u32[]{:S(2)}) %collective-permute-start.29) | collective-permute-done | bytes 614432 | tf_op jit(solution)/shard_map/ppermute | solution.py:415
  191.1 6.5 %collective-permute-done.30 = f32[200,768]{1,0:T(8,128)S(1)} collective-permute-done((f32[200,768]{1,0:T(8,128)S(1)}, f32[200,768]{1,0:T(8,128)S(1)}, u32[]{:S(2)}, u32[]{:S(2)}) %collective-permute-start.30) | collective-permute-done | bytes 614432 | tf_op jit(solution)/shard_map/ppermute | solution.py:415
  211.0 5.2 %collective-permute-done.36 = f32[192,768]{1,0:T(8,128)S(1)} collective-permute-done((f32[192,768]{1,0:T(8,128)S(1)}, f32[192,768]{1,0:T(8,128)S(1)}, u32[]{:S(2)}, u32[]{:S(2)}) %collective-permute-start.36) | collective-permute-done | bytes 589856 | tf_op jit(solution)/shard_map/ppermute | solution.py:415
  223.3 4.9 %collective-permute-done.38.refs_2_ = f32[192,768]{1,0:T(8,128)S(1)} collective-permute-done((f32[192,768]{1,0:T(8,128)S(1)}, f32[192,768]{1,0:T(8,128)S(1)}, u32[]{:S(2)}, u32[]{:S(2)}) %collective-permute-start.38) | collective-permute-done | bytes 589856 | tf_op jit(solution)/shard_map/ppermute | solution.py:415
  228.2 6.3 %collective-permute-done.39.refs_0_ = f32[192,768]{1,0:T(8,128)S(1)} collective-permute-done((f32[192,768]{1,0:T(8,128)S(1)}, f32[192,768]{1,0:T(8,128)S(1)}, u32[]{:S(2)}, u32[]{:S(2)}) %collective-permute-start.39) | collective-permute-done | bytes 589856 | tf_op jit(solution)/shard_map/ppermute | solution.py:415
  (166 shorter events, 87.7 us)
Async XLA Ops:
  16.2 16.6 %collective-permute-start.2 = (bf16[256,768]{1,0:T(8,128)(2,1)S(1)}, bf16[256,768]{1,0:T(8,128)(2,1)S(1)}, u32[]{:S(2)}, u32[]{:S(2)}) collective-permute-start(bf16[256,768]{1,0:T(8,128)(2,1)S(1)} %get-tuple-element.214), channel_id=1, source_target_pairs={{0,2},{1,3},{2,0},{3,1},{4,6},{5,7},{6,4},{7,5},{8,10},{9,11},{10,... | collective-permute-start | bytes 1179656 | tf_op jit(solution)/shard_map/ppermute | solution.py:25
  17.0 17.3 %collective-permute-start.3 = (bf16[256,768]{1,0:T(8,128)(2,1)S(1)}, bf16[256,768]{1,0:T(8,128)(2,1)S(1)}, u32[]{:S(2)}, u32[]{:S(2)}) collective-permute-start(bf16[256,768]{1,0:T(8,128)(2,1)S(1)} %get-tuple-element.213), channel_id=1, source_target_pairs={{0,3},{1,2},{2,1},{3,0},{4,7},{5,6},{6,5},{7,4},{8,11},{9,10},{10,... | collective-permute-start | bytes 1179656 | tf_op jit(solution)/shard_map/ppermute | solution.py:25
  34.4 19.2 %collective-permute-start.4 = (bf16[256,1536]{1,0:T(8,128)(2,1)S(1)}, bf16[256,1536]{1,0:T(8,128)(2,1)S(1)}, u32[]{:S(2)}, u32[]{:S(2)}) collective-permute-start(bf16[256,1536]{1,0:T(8,128)(2,1)S(1)} %get-tuple-element.109.refs_2_.embed_ref), channel_id=1, source_target_pairs={{0,8},{8,16},{16,24},{24,0},{1,9},{9,17},{17,25},{25,1},{2,10},{10... | collective-permute-start | bytes 2359304 | tf_op jit(solution)/shard_map/ppermute | solution.py:20
  35.7 17.8 %collective-permute-start.5 = (bf16[256,1536]{1,0:T(8,128)(2,1)S(1)}, bf16[256,1536]{1,0:T(8,128)(2,1)S(1)}, u32[]{:S(2)}, u32[]{:S(2)}) collective-permute-start(bf16[256,1536]{1,0:T(8,128)(2,1)S(1)} %get-tuple-element.109.refs_2_.embed_ref), channel_id=1, source_target_pairs={{0,24},{8,0},{16,8},{24,16},{1,25},{9,1},{17,9},{25,17},{2,26},{10... | collective-permute-start | bytes 2359304 | tf_op jit(solution)/shard_map/ppermute | solution.py:20
  37.2 18.5 %collective-permute-start.6 = (bf16[256,1536]{1,0:T(8,128)(2,1)S(1)}, bf16[256,1536]{1,0:T(8,128)(2,1)S(1)}, u32[]{:S(2)}, u32[]{:S(2)}) collective-permute-start(bf16[256,1536]{1,0:T(8,128)(2,1)S(1)} %get-tuple-element.110.refs_5_.refs_3_.embed_ref), channel_id=1, source_target_pairs={{0,32},{32,64},{64,96},{96,0},{1,33},{33,65},{65,97},{97,1},{2,34}... | collective-permute-start | bytes 2359304 | tf_op jit(solution)/shard_map/ppermute | solution.py:20
  38.4 17.3 %collective-permute-start.7 = (bf16[256,1536]{1,0:T(8,128)(2,1)S(1)}, bf16[256,1536]{1,0:T(8,128)(2,1)S(1)}, u32[]{:S(2)}, u32[]{:S(2)}) collective-permute-start(bf16[256,1536]{1,0:T(8,128)(2,1)S(1)} %get-tuple-element.110.refs_5_.refs_3_.embed_ref), channel_id=1, source_target_pairs={{0,96},{32,0},{64,32},{96,64},{1,97},{33,1},{65,33},{97,65},{2,98}... | collective-permute-start | bytes 2359304 | tf_op jit(solution)/shard_map/ppermute | solution.py:20
  39.9 24.2 %collective-permute-start.8 = (bf16[256,1536]{1,0:T(8,128)(2,1)S(1)}, bf16[256,1536]{1,0:T(8,128)(2,1)}, u32[]{:S(2)}, u32[]{:S(2)}) collective-permute-start(bf16[256,1536]{1,0:T(8,128)(2,1)S(1)} %get-tuple-element.110.refs_5_.refs_3_.embed_ref), channel_id=1, source_target_pairs={{0,4},{4,0},{1,5},{5,1},{2,6},{6,2},{3,7},{7,3},{8,12},{12,8},{9,1... | collective-permute-start | bytes 2359304 | tf_op jit(solution)/shard_map/ppermute | solution.py:20
  60.0 20.2 %collective-permute-start.11 = (bf16[256,1536]{1,0:T(8,128)(2,1)S(1)}, bf16[256,1536]{1,0:T(8,128)(2,1)S(1)}, u32[]{:S(2)}, u32[]{:S(2)}) collective-permute-start(bf16[256,1536]{1,0:T(8,128)(2,1)S(1)} %get-tuple-element.110.refs_5_.refs_3_.embed_ref), channel_id=1, source_target_pairs={{0,64},{32,96},{64,0},{96,32},{1,65},{33,97},{65,1},{97,33},{2,66}... | collective-permute-start | bytes 2359304 | tf_op jit(solution)/shard_map/ppermute | solution.py:20
  62.4 20.0 %collective-permute-start.12 = (bf16[256,1536]{1,0:T(8,128)(2,1)S(1)}, bf16[256,1536]{1,0:T(8,128)(2,1)S(1)}, u32[]{:S(2)}, u32[]{:S(2)}) collective-permute-start(bf16[256,1536]{1,0:T(8,128)(2,1)S(1)} %get-tuple-element.109.refs_2_.embed_ref), channel_id=1, source_target_pairs={{0,16},{8,24},{16,0},{24,8},{1,17},{9,25},{17,1},{25,9},{2,18},{10... | collective-permute-start | bytes 2359304 | tf_op jit(solution)/shard_map/ppermute | solution.py:20
  98.0 19.2 %collective-permute-start.17 = (bf16[256,1536]{1,0:T(8,128)(2,1)S(1)}, bf16[256,1536]{1,0:T(8,128)(2,1)S(1)}, u32[]{:S(2)}, u32[]{:S(2)}) collective-permute-start(bf16[256,1536]{1,0:T(8,128)(2,1)S(1)} %add_convert_fusion.2), channel_id=1, source_target_pairs={{0,96},{32,0},{64,32},{96,64},{1,97},{33,1},{65,33},{97,65},{2,98}... | collective-permute-start | bytes 2359304 | tf_op jit(solution)/shard_map/ppermute | solution.py:20
  99.3 20.0 %collective-permute-start.18 = (bf16[256,1536]{1,0:T(8,128)(2,1)S(1)}, bf16[256,1536]{1,0:T(8,128)(2,1)S(1)}, u32[]{:S(2)}, u32[]{:S(2)}) collective-permute-start(bf16[256,1536]{1,0:T(8,128)(2,1)S(1)} %add_convert_fusion.1), channel_id=1, source_target_pairs={{0,32},{32,64},{64,96},{96,0},{1,33},{33,65},{65,97},{97,1},{2,34}... | collective-permute-start | bytes 2359304 | tf_op jit(solution)/shard_map/ppermute | solution.py:20
  99.6 20.0 %collective-permute-start.19 = (bf16[256,1536]{1,0:T(8,128)(2,1)S(1)}, bf16[256,1536]{1,0:T(8,128)(2,1)S(1)}, u32[]{:S(2)}, u32[]{:S(2)}) collective-permute-start(bf16[256,1536]{1,0:T(8,128)(2,1)S(1)} %copy-done.26), channel_id=1, source_target_pairs={{0,16},{8,24},{16,0},{24,8},{1,17},{9,25},{17,1},{25,9},{2,18},{10... | collective-permute-start | bytes 2359304 | tf_op jit(solution)/shard_map/ppermute | solution.py:20
  101.1 19.4 %collective-permute-start.20 = (bf16[256,1536]{1,0:T(8,128)(2,1)S(1)}, bf16[256,1536]{1,0:T(8,128)(2,1)S(1)}, u32[]{:S(2)}, u32[]{:S(2)}) collective-permute-start(bf16[256,1536]{1,0:T(8,128)(2,1)S(1)} %copy-done.25), channel_id=1, source_target_pairs={{0,4},{4,0},{1,5},{5,1},{2,6},{6,2},{3,7},{7,3},{8,12},{12,8},{9,1... | collective-permute-start | bytes 2359304 | tf_op jit(solution)/shard_map/ppermute | solution.py:20
  124.1 51.4 %collective-permute-start = (bf16[512,768]{1,0:T(8,128)(2,1)}, bf16[512,768]{1,0:T(8,128)(2,1)}, u32[]{:S(2)}, u32[]{:S(2)}) collective-permute-start(bf16[512,768]{1,0:T(8,128)(2,1)} %get-tuple-element.210), channel_id=1, source_target_pairs={{0,4},{4,0},{1,5},{5,1},{2,6},{6,2},{3,7},{7,3},{8,12},{12,8},{9,1... | collective-permute-start | bytes 2359304 | tf_op jit(solution)/shard_map/ppermute | solution.py:20
  124.1 19.0 %collective-permute-start.23 = (bf16[256,1536]{1,0:T(8,128)(2,1)}, bf16[256,1536]{1,0:T(8,128)(2,1)S(1)}, u32[]{:S(2)}, u32[]{:S(2)}) collective-permute-start(bf16[256,1536]{1,0:T(8,128)(2,1)} %get-tuple-element.171), channel_id=1, source_target_pairs={{0,24},{8,0},{16,8},{24,16},{1,25},{9,1},{17,9},{25,17},{2,26},{10... | collective-permute-start | bytes 2359304 | tf_op jit(solution)/shard_map/ppermute | solution.py:20
  125.6 19.8 %collective-permute-start.24 = (bf16[256,1536]{1,0:T(8,128)(2,1)}, bf16[256,1536]{1,0:T(8,128)(2,1)S(1)}, u32[]{:S(2)}, u32[]{:S(2)}) collective-permute-start(bf16[256,1536]{1,0:T(8,128)(2,1)} %get-tuple-element.172), channel_id=1, source_target_pairs={{0,8},{8,16},{16,24},{24,0},{1,9},{9,17},{17,25},{25,1},{2,10},{10... | collective-permute-start | bytes 2359304 | tf_op jit(solution)/shard_map/ppermute | solution.py:20
  127.2 19.6 %collective-permute-start.22 = (bf16[256,1536]{1,0:T(8,128)(2,1)S(1)}, bf16[256,1536]{1,0:T(8,128)(2,1)S(1)}, u32[]{:S(2)}, u32[]{:S(2)}) collective-permute-start(bf16[256,1536]{1,0:T(8,128)(2,1)S(1)} %add_convert_fusion), channel_id=1, source_target_pairs={{0,64},{32,96},{64,0},{96,32},{1,65},{33,97},{65,1},{97,33},{2,66}... | collective-permute-start | bytes 2359304 | tf_op jit(solution)/shard_map/ppermute | solution.py:20
  151.5 19.3 %collective-permute-start.27 = (bf16[272,768]{1,0:T(8,128)(2,1)}, bf16[272,768]{1,0:T(8,128)(2,1)S(1)}, u32[]{:S(2)}, u32[]{:S(2)}) collective-permute-start(bf16[272,768]{1,0:T(8,128)(2,1)} %get-tuple-element.184), channel_id=1, source_target_pairs={{0,3},{1,2},{2,1},{3,0},{4,7},{5,6},{6,5},{7,4},{8,11},{9,10},{10,... | collective-permute-start | bytes 1253384 | tf_op jit(solution)/shard_map/ppermute | solution.py:25
  153.4 17.4 %collective-permute-start.26 = (bf16[272,768]{1,0:T(8,128)(2,1)}, bf16[272,768]{1,0:T(8,128)(2,1)S(1)}, u32[]{:S(2)}, u32[]{:S(2)}) collective-permute-start(bf16[272,768]{1,0:T(8,128)(2,1)} %get-tuple-element.183), channel_id=1, source_target_pairs={{0,2},{1,3},{2,0},{3,1},{4,6},{5,7},{6,4},{7,5},{8,10},{9,11},{10,... | collective-permute-start | bytes 1253384 | tf_op jit(solution)/shard_map/ppermute | solution.py:25
  181.9 15.8 %collective-permute-start.30 = (f32[200,768]{1,0:T(8,128)S(1)}, f32[200,768]{1,0:T(8,128)S(1)}, u32[]{:S(2)}, u32[]{:S(2)}) collective-permute-start(f32[200,768]{1,0:T(8,128)S(1)} %get-tuple-element.192), channel_id=1, source_target_pairs={{0,32},{4,12},{8,40},{12,20},{16,48},{20,28},{24,56},{28,4},{32,64... | collective-permute-start | bytes 1843208 | tf_op jit(solution)/shard_map/ppermute | solution.py:415
  183.5 14.5 %collective-permute-start.31 = (f32[200,768]{1,0:T(8,128)S(1)}, f32[200,768]{1,0:T(8,128)S(1)}, u32[]{:S(2)}, u32[]{:S(2)}) collective-permute-start(f32[200,768]{1,0:T(8,128)S(1)} %get-tuple-element.193), channel_id=1, source_target_pairs={{0,96},{4,28},{8,104},{12,4},{16,112},{20,12},{24,120},{28,20},{32... | collective-permute-start | bytes 1843208 | tf_op jit(solution)/shard_map/ppermute | solution.py:415
  200.8 15.4 %collective-permute-start.36 = (f32[192,768]{1,0:T(8,128)S(1)}, f32[192,768]{1,0:T(8,128)S(1)}, u32[]{:S(2)}, u32[]{:S(2)}) collective-permute-start(f32[192,768]{1,0:T(8,128)S(1)} %slice.61), channel_id=1, source_target_pairs={{0,8},{4,36},{8,16},{12,44},{16,24},{20,52},{24,0},{28,60},{32,40}... | collective-permute-start | bytes 1769480 | tf_op jit(solution)/shard_map/ppermute | solution.py:415
  218.9 15.5 %collective-permute-start.39 = (f32[192,768]{1,0:T(8,128)S(1)}, f32[192,768]{1,0:T(8,128)S(1)}, u32[]{:S(2)}, u32[]{:S(2)}) collective-permute-start(f32[192,768]{1,0:T(8,128)S(1)} %add_add_fusion.1.refs_0_), channel_id=1, source_target_pairs={{0,32},{4,12},{8,40},{12,20},{16,48},{20,28},{24,56},{28,4},{32,64... | collective-permute-start | bytes 1769480 | tf_op jit(solution)/shard_map/ppermute | solution.py:415
  220.5 13.9 %collective-permute-start.40 = (f32[192,768]{1,0:T(8,128)S(1)}, f32[192,768]{1,0:T(8,128)S(1)}, u32[]{:S(2)}, u32[]{:S(2)}) collective-permute-start(f32[192,768]{1,0:T(8,128)S(1)} %add_add_fusion.1.refs_0_), channel_id=1, source_target_pairs={{0,96},{4,28},{8,104},{12,4},{16,112},{20,12},{24,120},{28,20},{32... | collective-permute-start | bytes 1769480 | tf_op jit(solution)/shard_map/ppermute | solution.py:415
  (48 other events, 428.6 us)
